TPU v7x, 512 devices: a whole 4x8x8 slice. The times are simulated.
512 devices in a mesh: dp: 64 (over z_lo, y, core), mp: 8 (over z_hi, x).
Axes of the slice: x: 4, y: 8, z: 8 (z_hi: 2, z_lo: 4; z = z_hi * 4 + z_lo), core: 2. Of those that a mesh axis runs over, the one named last changes fastest.
Arguments:
- tokens: bfloat16 [24576, 1024], P('dp', 'mp'), may hold values from -400 to 400
- cotangent: bfloat16 [24576, 8192], P('dp', 'mp'), may hold values from -1.5625 to 1.5625
Outputs:
- update: bfloat16 [1024, 8192], P('dp', 'mp')
All inputs are finite; a program needn't handle non-finite values.
Results may differ from a plain program's by a relative error of at most 0.012.
The roundings to bfloat16 on the way count: a program that leaves them out, or rounds other values in their place, can miss the bound.
Values may be sent and summed in bfloat16 or wider, within the bound.
No kernel may reach another device: no remote copies, remote signals or barrier semaphores. Data moves between devices by JAX's collectives and lax.ppermute only.
A program may use at most 64 MiB of HBM per device.

v0:
```python
import jax
import jax.numpy as jnp
from jax import lax
from jax.sharding import PartitionSpec as P

BLK = 512
ITERS = 4


def from_root(value, axis, root):
    mine = lax.axis_index(axis) == root
    return lax.psum(jnp.where(mine, value, jnp.zeros_like(value)), axis)


def root_of(gram):
    size = gram.shape[0]
    identity = jnp.eye(size, dtype=jnp.float32)
    damp = 0.1 * jnp.trace(gram) / size + 1e-06
    matrix = gram + damp * identity
    frobenius = jnp.sqrt(jnp.sum(matrix * matrix))
    current = matrix / frobenius
    estimate = frobenius ** (-0.25) * identity
    for _ in range(ITERS):
        factor = ((5.0 * identity - current) * 0.25).astype(jnp.bfloat16)
        square = jnp.dot(factor, factor, preferred_element_type=jnp.float32).astype(jnp.bfloat16)
        fourth = jnp.dot(square, square, preferred_element_type=jnp.float32).astype(jnp.bfloat16)
        current = jnp.dot(fourth, current.astype(jnp.bfloat16), preferred_element_type=jnp.float32)
        estimate = jnp.dot(
            estimate.astype(jnp.bfloat16), factor, preferred_element_type=jnp.float32
        )
    return estimate.astype(jnp.bfloat16)


def contract_tokens(left_part, right_part):
    return lax.dot_general(
        left_part, right_part, (((0,), (0,)), ((), ())), preferred_element_type=jnp.float32
    )


def body(tokens, cotangent):
    features = lax.all_gather(tokens, "mp", axis=1, tiled=True)
    dp_count = lax.axis_size("dp")
    dp_index = lax.axis_index("dp")
    row_count = features.shape[1] // dp_count
    own_rows = lax.psum_scatter(
        contract_tokens(features, cotangent), "dp", scatter_dimension=0, tiled=True
    )
    gradient = lax.all_gather(own_rows.astype(jnp.bfloat16), "dp", axis=0, tiled=True)
    stat_index = dp_index % 8
    side = stat_index // 4
    row_block = stat_index // 2 % 2
    col_block = stat_index % 2
    block = lax.dynamic_slice(gradient, (row_block * BLK, col_block * BLK), (BLK, BLK))
    operand = jnp.where(side == 0, block, block.T)
    own_root = root_of(jnp.dot(operand, operand.T, preferred_element_type=jnp.float32))
    collected = []
    for owner in range(8):
        collected.append(from_root(own_root, "dp", owner))
    roots = jnp.stack(collected, 0)
    first_row = dp_index * row_count
    my_block = first_row // BLK
    offset = first_row - my_block * BLK
    outputs = []
    for column in range(2):
        lroot = lax.dynamic_index_in_dim(roots, my_block * 2 + column, 0, keepdims=False)
        rroot = lax.dynamic_index_in_dim(roots, 4 + my_block * 2 + column, 0, keepdims=False)
        lroot_rows = lax.dynamic_slice_in_dim(lroot, offset, row_count, 0)
        grad_block = lax.dynamic_slice(gradient, (my_block * BLK, column * BLK), (BLK, BLK))
        half = jnp.dot(lroot_rows, grad_block, preferred_element_type=jnp.float32).astype(
            jnp.bfloat16
        )
        outputs.append(
            jnp.dot(half, rroot, preferred_element_type=jnp.float32).astype(jnp.bfloat16)
        )
    return jnp.concatenate(outputs, 1)


def solution(mesh):
    return jax.shard_map(
        body,
        mesh=mesh,
        in_specs=(P("dp", "mp"), P("dp", "mp")),
        out_specs=P("dp", "mp"),
        check_vma=False,
    )
```

profile of v0, /device:TPU:1, one launch (start us, length us, event | category | flops | bytes accessed | tf_op | source)
XLA Modules:
  0.0 1049.8 jit_solution(3800995700705472492)
XLA Ops:
  6.5 0.0 copy-start
  6.5 0.0 reduce-scatter.2.cloned.1.call-start
  6.5 46.1 %all_gather.6 = bf16[384,1024]{1,0:T(8,128)(2,1)S(1)} all-gather(bf16[384,128]{1,0:T(8,128)(2,1)} %param.2), channel_id=1, replica_groups=mesh['dp'=64,'mp'=8] {'mp'}, dimensions={1}, use_global_device_ids=true | all-gather | bytes 884736 | tf_op jit(solution)/shard_map/all_gather | solution.py:41
  52.7 0.0 copy-done
  52.7 3.2 fusion.75
  55.9 0.0 reduce-scatter.2.cloned.1.call-update
  56.0 0.0 all-gather.2.cloned.1.call-start
  56.0 288.3 %reduce-scatter.2.cloned.1.call-done = f32[16,1024]{1,0:T(8,128)} async-done(((f32[1024,1024]{1,0:T(8,128)}), f32[16,1024]{1,0:T(8,128)}) %reduce-scatter.2.cloned.1.call-update) | async-done | bytes 65552 | tf_op jit(solution)/shard_map/reduce_scatter | solution.py:45
  344.3 1.5 convert_element_type.70
  345.8 0.0 all-gather.2.cloned.1.call-update
  345.8 0.0 all-reduce.3.cloned.1.call-start
  346.0 118.1 %all-gather.2.cloned.1.call-done = bf16[1024,1024]{1,0:T(8,128)(2,1)} async-done(((bf16[16,1024]{1,0:T(8,128)(2,1)}), bf16[1024,1024]{1,0:T(8,128)(2,1)}) %all-gather.2.cloned.1.call-update) | async-done | bytes 2097168 | tf_op jit(solution)/shard_map/all_gather | solution.py:48
  464.1 1.1 dynamic_slice.28
  465.1 0.2 copy.3
  465.4 1.1 select_reduce_fusion
  467.1 0.9 multiply_reduce_fusion
  468.7 0.2 fusion.3
  468.8 0.0 copy-start.6
  468.8 0.8 copy-done.6
  469.6 1.1 convolution_convert_fusion.7
  470.7 0.5 fusion.21
  471.2 1.1 convolution_convert_fusion.4
  472.3 2.5 convolution_convert_fusion.6
  474.9 0.4 fusion.19
  475.3 0.0 copy-start.7
  475.3 1.1 convolution_convert_fusion.1
  476.4 0.4 fusion.1
  476.9 0.0 copy-done.7
  476.9 3.0 select_bitcast_fusion
  479.9 0.0 all-reduce.3.cloned.1.call-update
  480.0 548.9 %all-reduce.3.cloned.1.call-done = (bf16[1,512,512]{2,1,0:T(8,128)(2,1)}, bf16[1,512,512]{2,1,0:T(8,128)(2,1)}, bf16[1,512,512]{2,1,0:T(8,128)(2,1)}, bf16[1,512...) async-done(((bf16[1,512,512]{2,1,0:T(8,128)(2,1)}, ...) | async-done | bytes 4194320 | tf_op jit(solution)/shard_map/psum | solution.py:12
  1028.9 0.0 copy-start.5
  1028.9 0.0 copy-start.4
  1028.9 0.0 copy-start.3
  1028.9 0.0 copy-start.2
  1028.9 0.0 copy-start.1
  1028.9 2.0 constant_dynamic-update-slice_fusion.7
  1030.9 1.9 constant_dynamic-update-slice_fusion.6
  1032.8 1.9 constant_dynamic-update-slice_fusion.5
  1034.6 1.9 constant_dynamic-update-slice_fusion.4
  1036.5 0.0 copy-done.5
  1036.5 0.8 constant_dynamic-update-slice_fusion.3
  1037.4 0.0 copy-done.4
  1037.4 0.8 constant_dynamic-update-slice_fusion.2
  1038.2 0.0 copy-done.3
  1038.2 0.8 constant_dynamic-update-slice_fusion.1
  1039.0 0.0 copy-done.2
  1039.0 0.8 constant_dynamic-update-slice_fusion
  1039.8 0.0 copy-done.1
  1039.9 1.4 convolution_convert_fusion.12
  1041.2 1.4 convolution_convert_fusion.10
  1042.6 0.6 pad_maximum_fusion
Async XLA Ops:
  6.5 46.2 %copy-start = (bf16[384,1024]{1,0:T(8,128)(2,1)S(1)}, bf16[384,1024]{1,0:T(8,128)(2,1)}, u32[]{:S(2)}) copy-start(bf16[384,1024]{1,0:T(8,128)(2,1)} %param.3) | copy-start | bytes 2359300
  6.5 337.8 %reduce-scatter.2.cloned.1.call-start = ((), (), s32[]{:S(2)}) async-start(), calls=%async_computation.1 | async-start | bytes 4259840 | tf_op jit(solution)/shard_map/reduce_scatter | solution.py:45
  56.0 408.1 %all-gather.2.cloned.1.call-start = ((), (), s32[]{:S(2)}) async-start(), calls=%async_computation.2 | async-start | bytes 2129920 | tf_op jit(solution)/shard_map/all_gather | solution.py:48
  345.8 683.0 %all-reduce.3.cloned.1.call-start = ((), (), s32[]{:S(2)}) async-start(), calls=%async_computation.3 | async-start | bytes 8388608 | tf_op jit(solution)/shard_map/psum | solution.py:12
  468.8 0.8 copy-start.6
  475.3 1.6 copy-start.7
  1028.9 7.7 copy-start.5
  1028.9 8.5 copy-start.4
  1028.9 9.3 copy-start.3
  1028.9 10.2 copy-start.2
  1028.9 11.0 %copy-start.1 = (bf16[1024,1024]{1,0:T(8,128)(2,1)S(1)}, bf16[1024,1024]{1,0:T(8,128)(2,1)}, u32[]{:S(2)}) copy-start(bf16[1024,1024]{1,0:T(8,128)(2,1)} %all-gather.2.cloned.1.call-done) | copy-start | bytes 6291460
Sparse Core Ops, SparseCore 0:
  56.1 288.2 reduce-scatter.1
  346.7 117.3 all-gather.1
  480.0 548.7 all-reduce.2
where the time goes:
time: 1050 us
  waiting for transfers between devices  955 us (91%)
  blocking collectives  46.1 us (4%)
  matrix products  17.2 us (2%)
  between operations  14.8 us (1%)
  local copies, waits for them, and re-layouts  13.1 us (1%)
    psum x1, waiting for transfers between devices, from_root(): return lax.psum(jnp.where(mine, value, jnp.zeros_like(value)), axis)  549 us
    reduce_scatter x1, waiting for transfers between devices, body(): lax.psum_scatter(contract_tokens(features, cotangent), 'dp', scatter_dime...  288 us
    all_gather x1, waiting for transfers between devices, body(): lax.all_gather(own_rows.astype(jnp.bfloat16), 'dp', axis=0, tiled=True)  118 us
    all_gather x1, blocking collectives, body(): features = lax.all_gather(tokens, 'mp', axis=1, tiled=True)  46.1 us
  transfers between devices with their start and end apart: 3, of which 3 were waited for; matrix products, arithmetic and copies ran while one was open for 0% of the time, Pallas kernels for 0%

commit v1 on v0

v1 whole, which is shorter than its diff:
```python
import functools

import jax
import jax.numpy as jnp
from jax import lax
from jax.experimental import pallas as pl
from jax.experimental.pallas import tpu as pltpu
from jax.sharding import Mesh
from jax.sharding import PartitionSpec as P

BLK = 512
ITERS = 4
ROWS = 32
VMEM_BYTES = 48 * 1024 * 1024


def dot(left, right, dims=((1,), (0,))):
    return lax.dot_general(left, right, (dims, ((), ())), preferred_element_type=jnp.float32)


def contract_kernel(core_ref, tokens_ref, cotangent_ref, partial_ref):
    for half in range(2):
        for place in range(4):
            total = None
            for source in range(2):
                term = dot(
                    tokens_ref[source, place, half], cotangent_ref[source], ((0,), (0,))
                )
                total = term if total is None else total + term
            row = half * BLK + place * 128
            partial_ref[row : row + 128, :] = total.astype(partial_ref.dtype)


def contract(core, tokens, cotangent):
    return pl.pallas_call(
        contract_kernel,
        grid_spec=pltpu.PrefetchScalarGridSpec(
            num_scalar_prefetch=1,
            grid=(1,),
            in_specs=[
                pl.BlockSpec(tokens.shape, lambda i, core: (0, 0, 0, 0, 0)),
                pl.BlockSpec((2, 384, BLK), lambda i, core: (0, 0, core[0])),
            ],
            out_specs=pl.BlockSpec((2 * BLK, BLK), lambda i, core: (0, 0)),
        ),
        out_shape=jax.ShapeDtypeStruct((2 * BLK, BLK), jnp.bfloat16),
        compiler_params=pltpu.CompilerParams(vmem_limit_bytes=VMEM_BYTES),
        name="contract",
    )(core, tokens, cotangent)


def roots_kernel(first_ref, block_ref, out_ref, left_ref, right_ref):
    block = block_ref[...]
    row_ids = lax.broadcasted_iota(jnp.int32, (BLK, BLK), 0)
    col_ids = lax.broadcasted_iota(jnp.int32, (BLK, BLK), 1)
    eye = jnp.where(row_ids == col_ids, 1.0, 0.0).astype(jnp.float32)

    def start(gram):
        damp = 0.1 * jnp.sum(gram * eye) / BLK + 1e-06
        matrix = gram + damp * eye
        fro = jnp.sqrt(jnp.sum(matrix * matrix, keepdims=True))
        return matrix / fro, jnp.sqrt(jnp.sqrt(1.0 / fro))

    left, left_scale = start(dot(block, block, ((1,), (1,))))
    right, right_scale = start(dot(block, block, ((0,), (0,))))
    scales = (left_scale, right_scale)
    first = first_ref[0]
    pick_row = lax.broadcasted_iota(jnp.int32, (ROWS, BLK), 0) + first
    pick_col = lax.broadcasted_iota(jnp.int32, (ROWS, BLK), 1)
    rows = jnp.where(pick_row == pick_col, left_scale, 0.0)
    steps = []
    for it in range(ITERS):
        factors = [((5.0 * eye - m) * 0.25).astype(jnp.bfloat16) for m in (left, right)]
        rows = dot(rows.astype(jnp.bfloat16), factors[0])
        steps.append(factors[1])
        if it < ITERS - 1:
            squares = [dot(f, f).astype(jnp.bfloat16) for f in factors]
            fourths = [dot(s, s).astype(jnp.bfloat16) for s in squares]
            left, right = (
                dot(f, m.astype(jnp.bfloat16)) for f, m in zip(fourths, (left, right))
            )
    half = dot(rows.astype(jnp.bfloat16), block).astype(jnp.bfloat16)
    value = half * right_scale.astype(jnp.bfloat16)
    for it in range(ITERS):
        value = dot(value.astype(jnp.bfloat16), steps[it])
    out_ref[...] = value.astype(out_ref.dtype)


def apply_roots(first, block):
    return pl.pallas_call(
        roots_kernel,
        in_specs=[
            pl.BlockSpec(memory_space=pltpu.SMEM),
            pl.BlockSpec(memory_space=pltpu.VMEM),
        ],
        out_specs=pl.BlockSpec(memory_space=pltpu.VMEM),
        out_shape=jax.ShapeDtypeStruct((ROWS, BLK), jnp.bfloat16),
        scratch_shapes=[pltpu.VMEM((8, 128), jnp.float32)] * 2,
        compiler_params=pltpu.CompilerParams(vmem_limit_bytes=VMEM_BYTES),
        name="apply_roots",
    )(first, block)


def body(tokens, cotangent):
    core = lax.axis_index("core")
    features = lax.all_gather(tokens[None], "zh", axis=0, tiled=True)
    features = lax.all_gather(features[None], "x", axis=0, tiled=True)
    features = lax.all_gather(features[None], "core", axis=0, tiled=True)
    both = lax.all_gather(cotangent[None], "core", axis=0, tiled=True)
    partial = contract(core[None], features, both)
    shares = lax.all_to_all(
        partial.reshape(32, ROWS, BLK), ("zr", "zp", "y"), 0, 0, tiled=True
    )
    own_rows = jnp.sum(shares.astype(jnp.float32), axis=0).astype(jnp.bfloat16)
    block = lax.all_gather(own_rows, "zp", axis=0, tiled=True)
    block = lax.all_gather(block, "y", axis=0, tiled=True)
    first = (lax.axis_index("y") * 2 + lax.axis_index("zp")) * ROWS
    update = apply_roots(first[None], block)
    pieces = lax.all_to_all(update.reshape(2, 16, BLK), "core", 0, 0, tiled=True)
    return jnp.concatenate([pieces[0], pieces[1]], axis=1)


def solution(mesh):
    devices = mesh.devices.reshape(2, 2, 8, 2, 2, 4)
    fine = Mesh(devices, ("zr", "zp", "y", "core", "zh", "x"))
    spec = P(("zr", "zp", "y", "core"), ("zh", "x"))
    return jax.shard_map(
        body, mesh=fine, in_specs=(spec, spec), out_specs=spec, check_vma=False
    )
```

time: 1050 us -> 152 us (0.14)
  waiting for transfers between devices: 955 us -> 51.4 us
  blocking collectives: 46.1 us -> 63.8 us
  matrix products: 17.2 us -> 0 us
    psum x1 -> x0, waiting for transfers between devices: 549 us -> none  [from_root(): return lax.psum(jnp.where(mine, value, jnp.zeros_like(value)), axis)]
    reduce_scatter x1 -> x0, waiting for transfers between devices: 288 us -> none  [body(): lax.psum_scatter(contract_tokens(features, cotangent), 'dp', scatter_dime...]
    all_gather x1 -> x2, waiting for transfers between devices: 118 us -> 24.6 us  [the longest x1 24 us: body(): features = lax.all_gather(features[None], 'core', axis=0, tiled=True)]
    all_to_all x0 -> x1, waiting for transfers between devices: none -> 26.1 us  [body(): lax.all_to_all(partial.reshape(32, ROWS, BLK), ('zr', 'zp', 'y'), 0, 0, t...]
    dot_general x12 -> x0, matrix products: 17.2 us -> none  [the longest x2 5.57 us: root_of(): jnp.dot(estimate.astype(jnp.bfloat16), factor, preferred_element_type=jnp...]
    all_to_all x0 -> x1, blocking collectives: none -> 14.1 us  [body(): lax.all_to_all(update.reshape(2, 16, BLK), 'core', 0, 0, tiled=True)]
    all_gather x1 -> x4, blocking collectives: 46.1 us -> 49.7 us  [the longest x1 19.8 us: body(): block = lax.all_gather(block, 'y', axis=0, tiled=True)]
where the time goes in v1:
time: 152 us; the launch traced here: 151 us
  blocking collectives  63.8 us (42%)
  waiting for transfers between devices  51.4 us (34%)
  between operations  13.4 us (9%)
  Pallas kernels  10.1 us (7%)
  starting transfers between devices  9.14 us (6%)
  local copies, waits for them, and re-layouts  2.82 us (2%)
    all_to_all x1, waiting for transfers between devices, body(): lax.all_to_all(partial.reshape(32, ROWS, BLK), ('zr', 'zp', 'y'), 0, 0, t...  26.1 us
    all_gather x1, waiting for transfers between devices, body(): features = lax.all_gather(features[None], 'core', axis=0, tiled=True)  24 us
    all_gather x1, blocking collectives, body(): block = lax.all_gather(block, 'y', axis=0, tiled=True)  19.8 us
    all_to_all x1, blocking collectives, body(): lax.all_to_all(update.reshape(2, 16, BLK), 'core', 0, 0, tiled=True)  14.1 us
    all_gather x1, blocking collectives, body(): features = lax.all_gather(features[None], 'x', axis=0, tiled=True)  13.8 us
    all_gather x1, blocking collectives, body(): features = lax.all_gather(tokens[None], 'zh', axis=0, tiled=True)  12.6 us
    all_to_all x1, starting transfers between devices, body(): lax.all_to_all(partial.reshape(32, ROWS, BLK), ('zr', 'zp', 'y'), 0, 0, t...  9.1 us
    pallas_call x1, Pallas kernels, apply_roots(): pl.pallas_call(roots_kernel, in_specs=[pl.BlockSpec(memory_space=pltpu.SM...  7.81 us
  transfers between devices with their start and end apart: 3, of which 3 were waited for; matrix products, arithmetic and copies ran while one was open for 0% of the time, Pallas kernels for 0%

profile of v1, /device:TPU:1, one launch (start us, length us, event | category | flops | bytes accessed | tf_op | source)
XLA Modules:
  0.0 151.5 jit_solution(17990550744346652359)
XLA Ops:
  6.5 0.0 all-gather.9.cloned.1.call-start
  6.5 0.7 all-gather.9.cloned.1.call-update
  7.3 0.0 all-gather.7.cloned.1.call-start
  7.3 12.6 %all-gather = bf16[768,128]{1,0:T(8,128)(2,1)S(1)} all-gather(bf16[384,128]{1,0:T(8,128)(2,1)} %param.2), channel_id=2, replica_groups=mesh['zr'=2,'zp'=2,'y'=8,'core'=2,'zh'=2,'x'=4] {'zh'}, dimensions={0}, use_global_device_ids=true | all-gather | bytes 294912 | tf_op jit(solution)/shard_map/all_gather | solution.py:106
  19.9 13.8 %all-gather.1 = bf16[8,384,128]{2,1,0:T(8,128)(2,1)} all-gather(bf16[2,384,128]{2,1,0:T(8,128)(2,1)S(1)} %bitcast.16), channel_id=3, replica_groups=mesh['zr'=2,'zp'=2,'y'=8,'core'=2,'zh'=2,'x'=4] {'x'}, dimensions={0}, use_global_device_ids=true | all-gather | bytes 983040 | tf_op jit(solution)/shard_map/all_gather | solution.py:107
  33.7 0.0 all-gather.7.cloned.1.call-update
  33.7 0.6 all-gather.9.cloned.1.call-done
  34.4 24.0 %all-gather.7.cloned.1.call-done = bf16[8,2,384,128]{3,2,1,0:T(8,128)(2,1)} async-done(((bf16[4,2,384,128]{3,2,1,0:T(8,128)(2,1)}), bf16[8,2,384,128]{3,2,1,0:T(8,128)(2,1)}) %all-gather.7.cloned.1.call-update) | async-done | bytes 1572880 | tf_op jit(solution)/shard_map/all_gather | solution.py:108
  58.3 0.0 copy-start
  58.3 1.4 copy-done
  59.8 0.0 copy-start.1
  59.8 1.4 copy-done.1
  61.2 2.3 %contract.1 = bf16[1024,512]{1,0:T(8,128)(2,1)} custom-call(s32[1]{0:T(128)} %bitcast.1.core_ref, bf16[2,4,2,384,128]{4,3,2,1,0:T(8,128)(2,1)S(1)} %bitcast.13, bf16[2,384,1024]{2,1,0:T(8,128)(2,1)S(1)} %bitcast.12), custom_call_target="tpu_custom_call" | custom-call | tf_op jit(solution)/shard_map/contract/pallas_call | solution.py:35
  63.4 9.1 %all-to-all-start = ((bf16[32,32,512]{2,1,0:T(8,128)(2,1)}), bf16[32,32,512]{2,1,0:T(8,128)(2,1)S(1)}, u32[]{:S(2)}, u32[]{:S(2)}) async-start(bf16[32,32,512]{2,1,0:T(8,128)(2,1)} %bitcast.6), calls=%async_computation | async-start | bytes 2097152 | tf_op jit(solution)/shard_map/all_to_all | solution.py:111
  72.5 26.1 %all-to-all-done = bf16[32,32,512]{2,1,0:T(8,128)(2,1)S(1)} async-done(((bf16[32,32,512]{2,1,0:T(8,128)(2,1)}), bf16[32,32,512]{2,1,0:T(8,128)(2,1)S(1)}, u32[]{:S(2)}, u32[]{:S(2)}) %all-to-all-start) | async-done | bytes 1048608 | tf_op jit(solution)/shard_map/all_to_all | solution.py:111
  98.6 0.2 reduce_sum.12
  98.8 3.5 %all_gather.22 = bf16[64,512]{1,0:T(8,128)(2,1)S(1)} all-gather(bf16[32,512]{1,0:T(8,128)(2,1)S(1)} %reduce_sum.12), channel_id=1, replica_groups=mesh['zr'=2,'zp'=2,'y'=8,'core'=2,'zh'=2,'x'=4] {'zp'}, dimensions={0}, use_global_device_ids=true | all-gather | bytes 98304 | tf_op jit(solution)/shard_map/all_gather | solution.py:115
  102.3 19.8 %all_gather.23.block_ref = bf16[512,512]{1,0:T(8,128)(2,1)S(1)} all-gather(bf16[64,512]{1,0:T(8,128)(2,1)S(1)} %all_gather.22), channel_id=1, replica_groups=mesh['zr'=2,'zp'=2,'y'=8,'core'=2,'zh'=2,'x'=4] {'y'}, dimensions={0}, use_global_device_ids=true | all-gather | bytes 589824 | tf_op jit(solution)/shard_map/all_gather | solution.py:116
  122.1 7.8 %apply_roots.1 = bf16[32,512]{1,0:T(8,128)(2,1)S(1)} custom-call(s32[1]{0:T(128)} %bitcast.first_ref, bf16[512,512]{1,0:T(8,128)(2,1)S(1)} %all_gather.23.block_ref), custom_call_target="tpu_custom_call" | custom-call | tf_op jit(solution)/shard_map/apply_roots/pallas_call | solution.py:90
  129.9 14.1 %all_to_all.10 = bf16[2,16,512]{2,1,0:T(8,128)(2,1)S(1)} all-to-all(bf16[2,16,512]{2,1,0:T(8,128)(2,1)S(1)} %bitcast.14), channel_id=1, replica_groups=mesh['zr'=2,'zp'=2,'y'=8,'core'=2,'zh'=2,'x'=4] {'core'}, dimensions={0} | all-to-all | bytes 65536 | tf_op jit(solution)/shard_map/all_to_all | solution.py:119
  144.0 0.6 pad_maximum_fusion
  (1 shorter events, 0.0 us)
Async XLA Ops:
  6.5 27.8 %all-gather.9.cloned.1.call-start = ((), (), s32[]{:S(2)}) async-start(), calls=%async_computation.3 | async-start | bytes 2359296 | tf_op jit(solution)/shard_map/all_gather | solution.py:109
  7.3 51.1 %all-gather.7.cloned.1.call-start = ((), (), s32[]{:S(2)}) async-start(), calls=%async_computation.2 | async-start | bytes 2359296 | tf_op jit(solution)/shard_map/all_gather | solution.py:108
  58.3 1.4 copy-start
  59.8 1.4 copy-start.1
  63.4 35.2 %all-to-all-start = ((bf16[32,32,512]{2,1,0:T(8,128)(2,1)}), bf16[32,32,512]{2,1,0:T(8,128)(2,1)S(1)}, u32[]{:S(2)}, u32[]{:S(2)}) async-start(bf16[32,32,512]{2,1,0:T(8,128)(2,1)} %bitcast.6), calls=%async_computation | async-start | bytes 2097152 | tf_op jit(solution)/shard_map/all_to_all | solution.py:111
Sparse Core Ops, SparseCore 0:
  9.4 24.8 all-gather.8
  36.4 21.8 all-gather.6

commit v2 on v1

v2 whole, which is shorter than its diff:
```python
import jax
import jax.numpy as jnp
from jax import lax
from jax.experimental import pallas as pl
from jax.experimental.pallas import tpu as pltpu
from jax.sharding import Mesh
from jax.sharding import PartitionSpec as P

BLK = 512
ITERS = 4
ROWS = 32
VMEM_BYTES = 48 * 1024 * 1024
VMEM_SPEC = pl.BlockSpec(memory_space=pltpu.VMEM)


def dot(left, right, dims=((1,), (0,))):
    return lax.dot_general(left, right, (dims, ((), ())), preferred_element_type=jnp.float32)


def own_kernel(tokens_ref, cotangent_ref, partial_ref):
    for place in range(8):
        partial_ref[place * 128 : place * 128 + 128, :] = dot(
            tokens_ref[place], cotangent_ref[...], ((0,), (0,))
        )


def pair_kernel(parity_ref, tokens_ref, cotangent_ref, own_ref, keep_ref, low_ref, high_ref, total_ref):
    parity = parity_ref[0]
    for place in range(8):
        total_ref[...] = own_ref[place * 128 : place * 128 + 128, :] + dot(
            tokens_ref[place], cotangent_ref[...], ((0,), (0,))
        )
        for group in range(2):
            row = place * 64 + group * ROWS
            kept = pl.multiple_of(group * 64 + parity * ROWS, ROWS)
            sent = pl.multiple_of(group * 64 + (1 - parity) * ROWS, ROWS)
            keep_ref[row : row + ROWS, :] = total_ref[pl.ds(kept, ROWS), :]
            other = total_ref[pl.ds(sent, ROWS), :].astype(jnp.bfloat16)
            low_ref[row : row + ROWS, :] = other[:, :256]
            high_ref[row : row + ROWS, :] = other[:, 256:]


def contract_own(tokens, cotangent):
    return pl.pallas_call(
        own_kernel,
        in_specs=[VMEM_SPEC] * 2,
        out_specs=VMEM_SPEC,
        out_shape=jax.ShapeDtypeStruct((2 * BLK, BLK), jnp.float32),
        compiler_params=pltpu.CompilerParams(vmem_limit_bytes=VMEM_BYTES),
        cost_estimate=pl.CostEstimate(flops=2 * 384 * 1024 * 512, bytes_accessed=3 << 20, transcendentals=0),
        name="contract_own",
    )(tokens, cotangent)


def contract_pair(parity, tokens, cotangent, own):
    half = jax.ShapeDtypeStruct((BLK, 256), jnp.bfloat16)
    return pl.pallas_call(
        pair_kernel,
        in_specs=[pl.BlockSpec(memory_space=pltpu.SMEM)] + [VMEM_SPEC] * 3,
        out_specs=[VMEM_SPEC] * 3,
        out_shape=[jax.ShapeDtypeStruct((BLK, BLK), jnp.float32), half, half],
        scratch_shapes=[pltpu.VMEM((128, BLK), jnp.float32)],
        compiler_params=pltpu.CompilerParams(vmem_limit_bytes=VMEM_BYTES),
        cost_estimate=pl.CostEstimate(flops=2 * 384 * 1024 * 512, bytes_accessed=5 << 20, transcendentals=0),
        name="contract_pair",
    )(parity, tokens, cotangent, own)


def add_kernel(keep_ref, low_ref, high_ref, sum_ref):
    for share in range(16):
        rows = slice(share * ROWS, share * ROWS + ROWS)
        sum_ref[share, :, :256] = (keep_ref[rows, :256] + low_ref[rows, :].astype(jnp.float32)).astype(jnp.bfloat16)
        sum_ref[share, :, 256:] = (keep_ref[rows, 256:] + high_ref[rows, :].astype(jnp.float32)).astype(jnp.bfloat16)


def add_pair(keep, low, high):
    return pl.pallas_call(
        add_kernel,
        in_specs=[VMEM_SPEC] * 3,
        out_specs=VMEM_SPEC,
        out_shape=jax.ShapeDtypeStruct((16, ROWS, BLK), jnp.bfloat16),
        compiler_params=pltpu.CompilerParams(vmem_limit_bytes=VMEM_BYTES),
        name="add_pair",
    )(keep, low, high)


def total_kernel(shares_ref, copies_ref):
    total = shares_ref[0].astype(jnp.float32)
    for share in range(1, 16):
        total += shares_ref[share].astype(jnp.float32)
    total = total.astype(jnp.bfloat16)
    for copy in range(16):
        copies_ref[copy] = total


def total_copies(shares):
    return pl.pallas_call(
        total_kernel,
        in_specs=[VMEM_SPEC],
        out_specs=VMEM_SPEC,
        out_shape=jax.ShapeDtypeStruct((16, ROWS, BLK), jnp.bfloat16),
        compiler_params=pltpu.CompilerParams(vmem_limit_bytes=VMEM_BYTES),
        name="total_copies",
    )(shares)


def roots_kernel(first_ref, block_ref, out_ref):
    block = block_ref[...]
    row_ids = lax.broadcasted_iota(jnp.int32, (BLK, BLK), 0)
    col_ids = lax.broadcasted_iota(jnp.int32, (BLK, BLK), 1)
    eye = jnp.where(row_ids == col_ids, 1.0, 0.0).astype(jnp.float32)

    def start(gram):
        damp = 0.1 * jnp.sum(gram * eye) / BLK + 1e-06
        matrix = gram + damp * eye
        fro = jnp.sqrt(jnp.sum(matrix * matrix, keepdims=True))
        return matrix / fro, jnp.sqrt(jnp.sqrt(1.0 / fro))

    left, left_scale = start(dot(block, block, ((1,), (1,))))
    right, right_scale = start(dot(block, block, ((0,), (0,))))
    first = first_ref[0]
    pick_row = lax.broadcasted_iota(jnp.int32, (ROWS, BLK), 0) + first
    pick_col = lax.broadcasted_iota(jnp.int32, (ROWS, BLK), 1)
    rows = jnp.where(pick_row == pick_col, left_scale, 0.0)
    steps = []
    for it in range(ITERS):
        factors = [((5.0 * eye - m) * 0.25).astype(jnp.bfloat16) for m in (left, right)]
        rows = dot(rows.astype(jnp.bfloat16), factors[0])
        steps.append(factors[1])
        if it < ITERS - 1:
            squares = [dot(f, f).astype(jnp.bfloat16) for f in factors]
            fourths = [dot(s, s).astype(jnp.bfloat16) for s in squares]
            left, right = (
                dot(f, m.astype(jnp.bfloat16)) for f, m in zip(fourths, (left, right))
            )
    half = dot(rows.astype(jnp.bfloat16), block).astype(jnp.bfloat16)
    value = half * right_scale.astype(jnp.bfloat16)
    for it in range(ITERS):
        value = dot(value.astype(jnp.bfloat16), steps[it])
    out_ref[...] = value.astype(out_ref.dtype)


def apply_roots(first, block):
    return pl.pallas_call(
        roots_kernel,
        in_specs=[pl.BlockSpec(memory_space=pltpu.SMEM), VMEM_SPEC],
        out_specs=VMEM_SPEC,
        out_shape=jax.ShapeDtypeStruct((ROWS, BLK), jnp.bfloat16),
        compiler_params=pltpu.CompilerParams(vmem_limit_bytes=VMEM_BYTES),
        name="apply_roots",
    )(first, block)


def swap(value, axis):
    return lax.ppermute(value, axis, [(0, 1), (1, 0)])


def neighbours(value, up):
    pairs = [(i, (i + 1 if (i % 2 == 0) == up else i - 1) % 8) for i in range(8)]
    return lax.ppermute(value, ("q", "p"), pairs)


def body(tokens, cotangent):
    core = lax.axis_index("core")
    parity = lax.axis_index("p")
    first = lax.axis_index("zp") * 256 + lax.axis_index("q") * 64 + parity * ROWS
    sent = lax.dynamic_slice_in_dim(cotangent, (1 - core) * BLK, BLK, 1)
    other_cotangent = swap(sent, "core")
    own_cotangent = lax.dynamic_slice_in_dim(cotangent, core * BLK, BLK, 1)
    copies = jnp.broadcast_to(tokens[None], (8, *tokens.shape))
    features = lax.all_to_all(copies, ("zh", "x"), 0, 0, tiled=True)
    other_features = swap(features, "core")
    own = contract_own(features, own_cotangent)
    keep, low, high = contract_pair(parity[None], other_features, other_cotangent, own)
    shares = add_pair(keep, neighbours(low, True), neighbours(high, False))
    shares = lax.all_to_all(shares, ("zr", "zp", "q"), 0, 0, tiled=True)
    rows = lax.all_to_all(total_copies(shares), ("zp", "q", "p"), 0, 0, tiled=True)
    update = apply_roots(first[None], rows.reshape(BLK, BLK))
    return lax.all_to_all(update, "core", split_axis=0, concat_axis=1, tiled=True)


def solution(mesh):
    devices = mesh.devices.reshape(2, 2, 4, 2, 2, 2, 4)
    fine = Mesh(devices, ("zr", "zp", "q", "p", "core", "zh", "x"))
    spec = P(("zr", "zp", "q", "p", "core"), ("zh", "x"))
    return jax.shard_map(
        body, mesh=fine, in_specs=(spec, spec), out_specs=spec, check_vma=False
    )
```

time: 152 us -> 120 us (0.79)
  waiting for transfers between devices: 51.4 us -> 20.3 us
  starting transfers between devices: 9.14 us -> 24.2 us
  between operations: 13.4 us -> 0.11 us
    all_gather x4 -> x0, blocking collectives: 49.7 us -> none  [the longest x1 19.8 us: body(): block = lax.all_gather(block, 'y', axis=0, tiled=True)]
    all_to_all x1 -> x3, blocking collectives: 14.1 us -> 63 us  [the longest x1 28.4 us: body(): features = lax.all_to_all(copies, ('zh', 'x'), 0, 0, tiled=True)]
    all_gather x2 -> x0, waiting for transfers between devices: 24.6 us -> none  [the longest x1 24 us: body(): features = lax.all_gather(features[None], 'core', axis=0, tiled=True)]
    ppermute x0 -> x4, starting transfers between devices: none -> 20.6 us  [the longest x2 12.5 us: swap(): return lax.ppermute(value, axis, [(0, 1), (1, 0)])]
    all_to_all x1, waiting for transfers between devices: 26.1 us -> 13.1 us  [body(): lax.all_to_all(total_copies(shares), ('zp', 'q', 'p'), 0, 0, tiled=True)]
    ppermute x0 -> x4, waiting for transfers between devices: none -> 7.24 us  [the longest x2 6.28 us: neighbours(): return lax.ppermute(value, ('q', 'p'), pairs)]
    all_to_all x1, starting transfers between devices: 9.1 us -> 3.57 us  [body(): lax.all_to_all(total_copies(shares), ('zp', 'q', 'p'), 0, 0, tiled=True)]
    unnamed x4 -> x2, local copies, waits for them, and re-layouts: 2.81 us -> 0.01 us
  transfers between devices with their start and end apart: 3 -> 5, of which waited for: 3 -> 4; matrix products, arithmetic and copies ran while one was open for 0% -> 0% of each run, Pallas kernels for 0% -> 1%
where the time goes in v2:
time: 120 us
  blocking collectives  63 us (52%)
  starting transfers between devices  24.2 us (20%)
  waiting for transfers between devices  20.3 us (17%)
  Pallas kernels  10.3 us (9%)
  local copies, waits for them, and re-layouts  1.76 us (1%)
    all_to_all x1, blocking collectives, body(): features = lax.all_to_all(copies, ('zh', 'x'), 0, 0, tiled=True)  28.4 us
    all_to_all x1, blocking collectives, body(): shares = lax.all_to_all(shares, ('zr', 'zp', 'q'), 0, 0, tiled=True)  27.6 us
    all_to_all x1, waiting for transfers between devices, body(): lax.all_to_all(total_copies(shares), ('zp', 'q', 'p'), 0, 0, tiled=True)  13.1 us
    ppermute x2, starting transfers between devices, swap(): return lax.ppermute(value, axis, [(0, 1), (1, 0)])  12.5 us
    ppermute x2, starting transfers between devices, neighbours(): return lax.ppermute(value, ('q', 'p'), pairs)  8.07 us
    pallas_call x1, Pallas kernels, apply_roots(): pl.pallas_call(roots_kernel, in_specs=[pl.BlockSpec(memory_space=pltpu.SM...  7.83 us
    all_to_all x1, blocking collectives, body(): lax.all_to_all(update, 'core', split_axis=0, concat_axis=1, tiled=True)  6.96 us
    ppermute x2, waiting for transfers between devices, neighbours(): return lax.ppermute(value, ('q', 'p'), pairs)  6.28 us
  transfers between devices with their start and end apart: 5, of which 4 were waited for; matrix products, arithmetic and copies ran while one was open for 0% of the time, Pallas kernels for 1%

profile of v2, /device:TPU:1, one launch (start us, length us, event | category | flops | bytes accessed | tf_op | source)
XLA Modules:
  0.0 119.7 jit_solution(3642261091329504088)
XLA Ops:
  0.0 0.0 copy-start
  0.0 1.1 broadcast_in_dim.14
  1.1 28.4 %all_to_all.34.tokens_ref = bf16[8,384,128]{2,1,0:T(8,128)(2,1)S(1)} all-to-all(bf16[8,384,128]{2,1,0:T(8,128)(2,1)S(1)} %broadcast_in_dim.14), channel_id=1, replica_groups=mesh['zr'=2,'zp'=2,'q'=4,'p'=2,'core'=2,'zh'=2,'x'=4] {'zh','x'}, dimensions={0} | all-to-all | bytes 1572864 | tf_op jit(solution)/shard_map/all_to_all | solution.py:171
  29.5 10.6 %collective-permute-start = (bf16[8,384,128]{2,1,0:T(8,128)(2,1)S(1)}, bf16[8,384,128]{2,1,0:T(8,128)(2,1)S(1)}, u32[]{:S(2)}, u32[]{:S(2)}) collective-permute-start(bf16[8,384,128]{2,1,0:T(8,128)(2,1)S(1)} %all_to_all.34.tokens_ref), channel_id=1, source_target_pairs={{0,8},{8,0},{1,9},{9,1},{2,10},{10,2},{3,11},{11,3},{4,12},{12,4},... | collective-permute-start | bytes 2359304 | tf_op jit(solution)/shard_map/ppermute | solution.py:155
  40.1 0.0 copy-done
  40.2 0.1 constant_dynamic-slice_fusion
  40.2 1.9 %collective-permute-start.1 = (bf16[384,512]{1,0:T(8,128)(2,1)S(1)}, bf16[384,512]{1,0:T(8,128)(2,1)S(1)}, u32[]{:S(2)}, u32[]{:S(2)}) collective-permute-start(bf16[384,512]{1,0:T(8,128)(2,1)S(1)} %get-tuple-element.12), channel_id=1, source_target_pairs={{0,8},{8,0},{1,9},{9,1},{2,10},{10,2},{3,11},{11,3},{4,12},{12,4},... | collective-permute-start | bytes 1179656 | tf_op jit(solution)/shard_map/ppermute | solution.py:155
  42.2 0.7 contract_own.1.own_ref
  42.9 0.9 collective-permute-done.1.cotangent_ref
  43.9 0.0 collective-permute-done.tokens_ref
  43.9 0.8 contract_pair.1
  44.7 3.2 %collective-permute-start.2 = (bf16[512,256]{1,0:T(8,128)(2,1)S(1)}, bf16[512,256]{1,0:T(8,128)(2,1)S(1)}, u32[]{:S(2)}, u32[]{:S(2)}) collective-permute-start(bf16[512,256]{1,0:T(8,128)(2,1)S(1)} %get-tuple-element.9), channel_id=1, source_target_pairs={{0,16},{16,0},{32,48},{48,32},{64,80},{80,64},{96,112},{112,96},{1... | collective-permute-start | bytes 786440 | tf_op jit(solution)/shard_map/ppermute | solution.py:160
  47.9 4.9 %collective-permute-start.3 = (bf16[512,256]{1,0:T(8,128)(2,1)S(1)}, bf16[512,256]{1,0:T(8,128)(2,1)S(1)}, u32[]{:S(2)}, u32[]{:S(2)}) collective-permute-start(bf16[512,256]{1,0:T(8,128)(2,1)S(1)} %get-tuple-element.10), channel_id=1, source_target_pairs={{0,112},{16,32},{32,16},{48,64},{64,48},{80,96},{96,80},{112,0},{1... | collective-permute-start | bytes 786440 | tf_op jit(solution)/shard_map/ppermute | solution.py:160
  52.8 1.6 %collective-permute-done.2.low_ref = bf16[512,256]{1,0:T(8,128)(2,1)S(1)} collective-permute-done((bf16[512,256]{1,0:T(8,128)(2,1)S(1)}, bf16[512,256]{1,0:T(8,128)(2,1)S(1)}, u32[]{:S(2)}, u32[]{:S(2)}) %collective-permute-start.2) | collective-permute-done | bytes 262176 | tf_op jit(solution)/shard_map/ppermute | solution.py:160
  54.3 4.7 %collective-permute-done.3.high_ref = bf16[512,256]{1,0:T(8,128)(2,1)S(1)} collective-permute-done((bf16[512,256]{1,0:T(8,128)(2,1)S(1)}, bf16[512,256]{1,0:T(8,128)(2,1)S(1)}, u32[]{:S(2)}, u32[]{:S(2)}) %collective-permute-start.3) | collective-permute-done | bytes 262176 | tf_op jit(solution)/shard_map/ppermute | solution.py:160
  59.0 0.1 add_pair.1
  59.1 27.6 %all_to_all.35.shares_ref = bf16[16,32,512]{2,1,0:T(8,128)(2,1)S(1)} all-to-all(bf16[16,32,512]{2,1,0:T(8,128)(2,1)S(1)} %add_pair.1), channel_id=1, replica_groups=mesh['zr'=2,'zp'=2,'q'=4,'p'=2,'core'=2,'zh'=2,'x'=4] {'zr','zp','q'}, dimensions={0} | all-to-all | bytes 1048576 | tf_op jit(solution)/shard_map/all_to_all | solution.py:176
  86.7 0.9 total_copies.1
  87.6 3.6 %all-to-all-start.2 = ((bf16[16,32,512]{2,1,0:T(8,128)(2,1)}), bf16[16,32,512]{2,1,0:T(8,128)(2,1)S(1)}, u32[]{:S(2)}, u32[]{:S(2)}) async-start(bf16[16,32,512]{2,1,0:T(8,128)(2,1)} %total_copies.1), calls=%async_computation.2 | async-start | bytes 1048576 | tf_op jit(solution)/shard_map/all_to_all | solution.py:177
  91.2 13.1 %all-to-all-done.2 = bf16[16,32,512]{2,1,0:T(8,128)(2,1)S(1)} async-done(((bf16[16,32,512]{2,1,0:T(8,128)(2,1)}), bf16[16,32,512]{2,1,0:T(8,128)(2,1)S(1)}, u32[]{:S(2)}, u32[]{:S(2)}) %all-to-all-start.2) | async-done | bytes 524320 | tf_op jit(solution)/shard_map/all_to_all | solution.py:177
  104.3 7.8 %apply_roots.1 = bf16[32,512]{1,0:T(8,128)(2,1)S(1)} custom-call(s32[1]{0:T(128)} %bitcast.first_ref, bf16[512,512]{1,0:T(8,128)(2,1)S(1)} %bitcast.7), custom_call_target="tpu_custom_call" | custom-call | tf_op jit(solution)/shard_map/apply_roots/pallas_call | solution.py:144
  112.1 7.0 %all_to_all.36 = bf16[2,16,512]{2,1,0:T(8,128)(2,1)S(1)} all-to-all(bf16[2,16,512]{2,1,0:T(8,128)(2,1)S(1)} %bitcast.8), channel_id=1, replica_groups=mesh['zr'=2,'zp'=2,'q'=4,'p'=2,'core'=2,'zh'=2,'x'=4] {'core'}, dimensions={0} | all-to-all | bytes 65536 | tf_op jit(solution)/shard_map/all_to_all | solution.py:179
  119.1 0.6 copy.4
Async XLA Ops:
  0.0 40.1 %copy-start = (bf16[384,1024]{1,0:T(8,128)(2,1)S(1)}, bf16[384,1024]{1,0:T(8,128)(2,1)}, u32[]{:S(2)}) copy-start(bf16[384,1024]{1,0:T(8,128)(2,1)} %param.3) | copy-start | bytes 2359300
  29.5 14.3 %collective-permute-start = (bf16[8,384,128]{2,1,0:T(8,128)(2,1)S(1)}, bf16[8,384,128]{2,1,0:T(8,128)(2,1)S(1)}, u32[]{:S(2)}, u32[]{:S(2)}) collective-permute-start(bf16[8,384,128]{2,1,0:T(8,128)(2,1)S(1)} %all_to_all.34.tokens_ref), channel_id=1, source_target_pairs={{0,8},{8,0},{1,9},{9,1},{2,10},{10,2},{3,11},{11,3},{4,12},{12,4},... | collective-permute-start | bytes 2359304 | tf_op jit(solution)/shard_map/ppermute | solution.py:155
  40.2 3.6 %collective-permute-start.1 = (bf16[384,512]{1,0:T(8,128)(2,1)S(1)}, bf16[384,512]{1,0:T(8,128)(2,1)S(1)}, u32[]{:S(2)}, u32[]{:S(2)}) collective-permute-start(bf16[384,512]{1,0:T(8,128)(2,1)S(1)} %get-tuple-element.12), channel_id=1, source_target_pairs={{0,8},{8,0},{1,9},{9,1},{2,10},{10,2},{3,11},{11,3},{4,12},{12,4},... | collective-permute-start | bytes 1179656 | tf_op jit(solution)/shard_map/ppermute | solution.py:155
  44.7 9.7 %collective-permute-start.2 = (bf16[512,256]{1,0:T(8,128)(2,1)S(1)}, bf16[512,256]{1,0:T(8,128)(2,1)S(1)}, u32[]{:S(2)}, u32[]{:S(2)}) collective-permute-start(bf16[512,256]{1,0:T(8,128)(2,1)S(1)} %get-tuple-element.9), channel_id=1, source_target_pairs={{0,16},{16,0},{32,48},{48,32},{64,80},{80,64},{96,112},{112,96},{1... | collective-permute-start | bytes 786440 | tf_op jit(solution)/shard_map/ppermute | solution.py:160
  47.9 11.2 %collective-permute-start.3 = (bf16[512,256]{1,0:T(8,128)(2,1)S(1)}, bf16[512,256]{1,0:T(8,128)(2,1)S(1)}, u32[]{:S(2)}, u32[]{:S(2)}) collective-permute-start(bf16[512,256]{1,0:T(8,128)(2,1)S(1)} %get-tuple-element.10), channel_id=1, source_target_pairs={{0,112},{16,32},{32,16},{48,64},{64,48},{80,96},{96,80},{112,0},{1... | collective-permute-start | bytes 786440 | tf_op jit(solution)/shard_map/ppermute | solution.py:160
  87.6 16.7 %all-to-all-start.2 = ((bf16[16,32,512]{2,1,0:T(8,128)(2,1)}), bf16[16,32,512]{2,1,0:T(8,128)(2,1)S(1)}, u32[]{:S(2)}, u32[]{:S(2)}) async-start(bf16[16,32,512]{2,1,0:T(8,128)(2,1)} %total_copies.1), calls=%async_computation.2 | async-start | bytes 1048576 | tf_op jit(solution)/shard_map/all_to_all | solution.py:177

commit v3 on v1

v3 whole, which is shorter than its diff:
```python
import jax
import jax.numpy as jnp
from jax import lax
from jax.experimental import pallas as pl
from jax.experimental.pallas import tpu as pltpu
from jax.sharding import Mesh
from jax.sharding import PartitionSpec as P

BLK = 512
ITERS = 4
ROWS = 32
PARAMS = pltpu.CompilerParams(vmem_limit_bytes=48 * 1024 * 1024)
VMEM = pl.BlockSpec(memory_space=pltpu.VMEM)
SMEM = pl.BlockSpec(memory_space=pltpu.SMEM)


def dot(left, right):
    return jnp.dot(left, right, preferred_element_type=jnp.float32)


def spread_kernel(tokens_ref, copies_ref):
    features = tokens_ref[...].T
    for parity in range(2):
        for place in range(8):
            copies_ref[parity * 8 + place] = features[parity * 64 : parity * 64 + 64]


def spread(tokens):
    return pl.pallas_call(
        spread_kernel,
        in_specs=[VMEM],
        out_specs=VMEM,
        out_shape=jax.ShapeDtypeStruct((16, 64, 384), jnp.bfloat16),
        compiler_params=PARAMS,
        name="spread",
    )(tokens)


def contract_kernel(place_ref, features_ref, own_ref, other_ref, out_ref):
    parity = place_ref[0]
    columns = pl.ds(pl.multiple_of(place_ref[1] * BLK, BLK), BLK)
    out_ref[...] = (
        dot(features_ref[parity], own_ref[:, columns])
        + dot(features_ref[1 - parity], other_ref[:, columns])
    ).astype(out_ref.dtype)


def contract(parity, half, features, own, other, dtype):
    return pl.pallas_call(
        contract_kernel,
        in_specs=[SMEM] + [VMEM] * 3,
        out_specs=VMEM,
        out_shape=jax.ShapeDtypeStruct((BLK, BLK), dtype),
        compiler_params=PARAMS,
        name="contract",
    )(jnp.stack([parity, half]), features, own, other)


def add_kernel(keep_ref, arrived_ref, sum_ref):
    total = keep_ref[...] + arrived_ref[...].astype(jnp.float32)
    sum_ref[...] = total.astype(sum_ref.dtype)


def add(keep, arrived):
    return pl.pallas_call(
        add_kernel,
        in_specs=[VMEM] * 2,
        out_specs=VMEM,
        out_shape=jax.ShapeDtypeStruct((BLK, BLK), jnp.bfloat16),
        compiler_params=PARAMS,
        name="add",
    )(keep, arrived)


def total_kernel(shares_ref, copies_ref):
    total = shares_ref[0].astype(jnp.float32)
    for share in range(1, 16):
        total += shares_ref[share].astype(jnp.float32)
    total = total.astype(jnp.bfloat16)
    for copy in range(16):
        copies_ref[copy] = total


def total_copies(shares):
    return pl.pallas_call(
        total_kernel,
        in_specs=[VMEM],
        out_specs=VMEM,
        out_shape=jax.ShapeDtypeStruct((16, ROWS, BLK), jnp.bfloat16),
        compiler_params=PARAMS,
        name="total_copies",
    )(shares)


def roots_kernel(place_ref, block_ref, keep_ref, send_ref):
    block = block_ref[...]
    flipped = block.T
    wide = block.astype(jnp.float32)
    trace = jnp.sum(wide * wide, keepdims=True)
    row_ids = lax.broadcasted_iota(jnp.int32, (BLK, BLK), 0)
    col_ids = lax.broadcasted_iota(jnp.int32, (BLK, BLK), 1)
    diagonal = row_ids == col_ids
    damp = jnp.where(diagonal, 0.1 * trace / BLK + 1e-06, 0.0)
    base = jnp.where(diagonal, 1.25, 0.0)

    def start(gram):
        matrix = gram + damp
        inverse = lax.rsqrt(jnp.sum(matrix * matrix, keepdims=True))
        return matrix * inverse, jnp.sqrt(jnp.sqrt(inverse))

    left, left_scale = start(dot(block, flipped))
    right, right_scale = start(dot(flipped, block))
    order = lax.rem(lax.broadcasted_iota(jnp.int32, (ROWS, BLK), 0) + place_ref[1] * 16, ROWS)
    own = lax.broadcasted_iota(jnp.int32, (ROWS, BLK), 1) == order + place_ref[0]
    rows = jnp.where(own, left_scale, 0.0)
    steps = []
    for it in range(ITERS):
        factors = [(base - m * 0.25).astype(jnp.bfloat16) for m in (left, right)]
        rows = dot(rows.astype(jnp.bfloat16), factors[0])
        steps.append(factors[1])
        if it < ITERS - 1:
            squares = [dot(f, f).astype(jnp.bfloat16) for f in factors]
            fourths = [dot(s, s).astype(jnp.bfloat16) for s in squares]
            left, right = (
                dot(f, m.astype(jnp.bfloat16)) for f, m in zip(fourths, (left, right))
            )
    half = dot(rows.astype(jnp.bfloat16), block).astype(jnp.bfloat16)
    value = half * right_scale.astype(jnp.bfloat16)
    for step in steps:
        value = dot(value, step).astype(jnp.bfloat16)
    keep_ref[...] = value[:16]
    send_ref[...] = value[16:]


def apply_roots(first, core, block):
    piece = jax.ShapeDtypeStruct((16, BLK), jnp.bfloat16)
    return pl.pallas_call(
        roots_kernel,
        in_specs=[SMEM, VMEM],
        out_specs=[VMEM] * 2,
        out_shape=[piece] * 2,
        compiler_params=PARAMS,
        name="apply_roots",
    )(jnp.stack([first, core]), block)


def join_kernel(core_ref, keep_ref, arrived_ref, out_ref):
    core = core_ref[0]
    out_ref[:, pl.ds(pl.multiple_of(core * BLK, BLK), BLK)] = keep_ref[...]
    out_ref[:, pl.ds(pl.multiple_of((1 - core) * BLK, BLK), BLK)] = arrived_ref[...]


def join(core, keep, arrived):
    return pl.pallas_call(
        join_kernel,
        in_specs=[SMEM] + [VMEM] * 2,
        out_specs=VMEM,
        out_shape=jax.ShapeDtypeStruct((16, 2 * BLK), jnp.bfloat16),
        compiler_params=PARAMS,
        name="join",
    )(core[None], keep, arrived)


def swap(value, axis):
    return lax.ppermute(value, axis, [(0, 1), (1, 0)])


def exchange(value, axes):
    return lax.all_to_all(value, axes, 0, 0, tiled=True)


def body(tokens, cotangent):
    core, p, q, zp = (lax.axis_index(name) for name in ("core", "p", "q", "zp"))
    other = swap(cotangent, "p")
    features = exchange(spread(tokens), ("p", "zh", "x")).reshape(2, BLK, 384)
    sent = contract(p, 1 - core, features, cotangent, other, jnp.bfloat16)
    arrived = swap(sent, "core")
    keep = contract(p, core, features, cotangent, other, jnp.float32)
    shares = exchange(add(keep, arrived).reshape(16, ROWS, BLK), ("zr", "q", "zp"))
    block = exchange(total_copies(shares), ("p", "q", "zp")).reshape(BLK, BLK)
    first = ((q % 2) * 8 + (zp * 2 + q // 2) * 2 + p) * ROWS
    keep, sent = apply_roots(first, core, block)
    return join(core, keep, swap(sent, "core"))


def solution(mesh):
    devices = mesh.devices.reshape(2, 2, 4, 2, 2, 2, 4)
    fine = Mesh(devices, ("zr", "zp", "q", "p", "core", "zh", "x"))
    spec = P(("zr", "zp", "q", "p", "core"), ("zh", "x"))
    return jax.shard_map(
        body, mesh=fine, in_specs=(spec, spec), out_specs=spec, check_vma=False
    )
```

time: 152 us -> 112 us (0.74)
  blocking collectives: 63.8 us -> 26.7 us
  starting transfers between devices: 9.14 us -> 31 us
  between operations: 13.4 us -> 0.1 us
  waiting for transfers between devices: 51.4 us -> 39.5 us
  Pallas kernels: 10.1 us -> 12.9 us
  local copies, waits for them, and re-layouts: 2.82 us -> 0.9 us
    all_gather x4 -> x0, blocking collectives: 49.7 us -> none  [the longest x1 19.8 us: body(): block = lax.all_gather(block, 'y', axis=0, tiled=True)]
    all_gather x2 -> x0, waiting for transfers between devices: 24.6 us -> none  [the longest x1 24 us: body(): features = lax.all_gather(features[None], 'core', axis=0, tiled=True)]
    ppermute x0 -> x3, waiting for transfers between devices: none -> 24.3 us  [swap(): return lax.ppermute(value, axis, [(0, 1), (1, 0)])]
    all_to_all x1, blocking collectives: 14.1 us -> 26.7 us  [exchange(): return lax.all_to_all(value, axes, 0, 0, tiled=True)]
    ppermute x0 -> x3, starting transfers between devices: none -> 12.3 us  [swap(): return lax.ppermute(value, axis, [(0, 1), (1, 0)])]
    all_to_all x1 -> x2, waiting for transfers between devices: 26.1 us -> 15.1 us  [exchange(): return lax.all_to_all(value, axes, 0, 0, tiled=True)]
    all_to_all x1 -> x2, starting transfers between devices: 9.1 us -> 18.7 us  [exchange(): return lax.all_to_all(value, axes, 0, 0, tiled=True)]
    pallas_call x2 -> x7, Pallas kernels: 10.1 us -> 12.9 us  [the longest x1 7.81 us: apply_roots(): pl.pallas_call(roots_kernel, in_specs=[SMEM, VMEM], out_specs=[VMEM] * 2,...]
  transfers between devices with their start and end apart: 3 -> 5, of which waited for: 3 -> 4; matrix products, arithmetic and copies ran while one was open for 0% -> 0% of each run, Pallas kernels for 0% -> 1%
where the time goes in v3:
time: 112 us; the launch traced here: 111 us
  waiting for transfers between devices  39.5 us (35%)
  starting transfers between devices  31 us (28%)
  blocking collectives  26.7 us (24%)
  Pallas kernels  12.9 us (12%)
    all_to_all x1, blocking collectives, exchange(): return lax.all_to_all(value, axes, 0, 0, tiled=True)  26.7 us
    ppermute x3, waiting for transfers between devices, swap(): return lax.ppermute(value, axis, [(0, 1), (1, 0)])  24.3 us
    all_to_all x2, starting transfers between devices, exchange(): return lax.all_to_all(value, axes, 0, 0, tiled=True)  18.7 us
    all_to_all x2, waiting for transfers between devices, exchange(): return lax.all_to_all(value, axes, 0, 0, tiled=True)  15.1 us
    ppermute x3, starting transfers between devices, swap(): return lax.ppermute(value, axis, [(0, 1), (1, 0)])  12.3 us
    pallas_call x1, Pallas kernels, apply_roots(): pl.pallas_call(roots_kernel, in_specs=[SMEM, VMEM], out_specs=[VMEM] * 2,...  7.81 us
    pallas_call x2, Pallas kernels, contract(): pl.pallas_call(contract_kernel, in_specs=[SMEM] + [VMEM] * 3, out_specs=V...  2.49 us
  transfers between devices with their start and end apart: 5, of which 4 were waited for; matrix products, arithmetic and copies ran while one was open for 0% of the time, Pallas kernels for 1%

profile of v3, /device:TPU:1, one launch (start us, length us, event | category | flops | bytes accessed | tf_op | source)
XLA Modules:
  0.0 111.2 jit_solution(396416280924903116)
XLA Ops:
  0.0 0.0 copy-start.1
  0.0 0.9 copy-done.1
  0.9 1.0 spread.1
  1.9 0.0 copy-start
  1.9 14.5 %all-to-all-start = ((bf16[16,64,384]{2,1,0:T(8,128)(2,1)}), bf16[16,64,384]{2,1,0:T(8,128)(2,1)S(1)}, u32[]{:S(2)}, u32[]{:S(2)}) async-start(bf16[16,64,384]{2,1,0:T(8,128)(2,1)} %spread.1), calls=%async_computation | async-start | bytes 1572864 | tf_op jit(solution)/shard_map/all_to_all | solution.py:169
  16.4 0.0 copy-done
  16.5 3.3 %collective-permute-start = (bf16[384,1024]{1,0:T(8,128)(2,1)S(1)}, bf16[384,1024]{1,0:T(8,128)(2,1)S(1)}, u32[]{:S(2)}, u32[]{:S(2)}) collective-permute-start(bf16[384,1024]{1,0:T(8,128)(2,1)S(1)} %copy-done), channel_id=1, source_target_pairs={{0,16},{16,0},{1,17},{17,1},{2,18},{18,2},{3,19},{19,3},{4,20},{20... | collective-permute-start | bytes 2359304 | tf_op jit(solution)/shard_map/ppermute | solution.py:165
  19.7 0.1 pad_add_fusion.1.place_ref
  19.8 23.3 %collective-permute-done.other_ref = bf16[384,1024]{1,0:T(8,128)(2,1)S(1)} collective-permute-done((bf16[384,1024]{1,0:T(8,128)(2,1)S(1)}, bf16[384,1024]{1,0:T(8,128)(2,1)S(1)}, u32[]{:S(2)}, u32[]{:S(2)}) %collective-permute-start) | collective-permute-done | bytes 786464 | tf_op jit(solution)/shard_map/ppermute | solution.py:165
  43.2 0.0 all-to-all-done
  43.2 1.2 %contract.3 = bf16[512,512]{1,0:T(8,128)(2,1)S(1)} custom-call(s32[2]{0:T(128)S(1)} %pad_add_fusion.1.place_ref, bf16[2,512,384]{2,1,0:T(8,128)(2,1)S(1)} %bitcast.7, bf16[384,1024]{1,0:T(8,128)(2,1)S(1)} %copy-done, bf16[384,1024]{1,0:T(8,128)(2,1)S(1)} %collective-permute-done.other_ref), custom_call_target="tpu_custom_call" | custom-call | tf_op jit(solution)/shard_map/contract/pallas_call | solution.py:49
  44.4 3.8 %collective-permute-start.1 = (bf16[512,512]{1,0:T(8,128)(2,1)S(1)}, bf16[512,512]{1,0:T(8,128)(2,1)S(1)}, u32[]{:S(2)}, u32[]{:S(2)}) collective-permute-start(bf16[512,512]{1,0:T(8,128)(2,1)S(1)} %contract.3), channel_id=1, source_target_pairs={{0,8},{8,0},{1,9},{9,1},{2,10},{10,2},{3,11},{11,3},{4,12},{12,4},... | collective-permute-start | bytes 1572872 | tf_op jit(solution)/shard_map/ppermute | solution.py:165
  48.2 0.1 pad_add_fusion.2.place_ref
  48.3 1.2 %contract.2.keep_ref = f32[512,512]{1,0:T(8,128)S(1)} custom-call(s32[2]{0:T(128)S(1)} %pad_add_fusion.2.place_ref, bf16[2,512,384]{2,1,0:T(8,128)(2,1)S(1)} %bitcast.8, bf16[384,1024]{1,0:T(8,128)(2,1)S(1)} %copy-done, bf16[384,1024]{1,0:T(8,128)(2,1)S(1)} %collective-permute-done.other_ref), custom_call_target="tpu_custom_call" | custom-call | tf_op jit(solution)/shard_map/contract/pallas_call | solution.py:49
  49.5 0.2 collective-permute-done.1.arrived_ref
  49.7 0.1 add.25
  49.8 26.7 %all_to_all.15.shares_ref = bf16[16,32,512]{2,1,0:T(8,128)(2,1)S(1)} all-to-all(bf16[16,32,512]{2,1,0:T(8,128)(2,1)S(1)} %bitcast.10), channel_id=1, replica_groups=mesh['zr'=2,'zp'=2,'q'=4,'p'=2,'core'=2,'zh'=2,'x'=4] {'zr','q','zp'}, dimensions={0} | all-to-all | bytes 1048576 | tf_op jit(solution)/shard_map/all_to_all | solution.py:169
  76.5 0.9 total_copies.1
  77.4 4.1 %all-to-all-start.2 = ((bf16[16,32,512]{2,1,0:T(8,128)(2,1)}), bf16[16,32,512]{2,1,0:T(8,128)(2,1)S(1)}, u32[]{:S(2)}, u32[]{:S(2)}) async-start(bf16[16,32,512]{2,1,0:T(8,128)(2,1)} %total_copies.1), calls=%async_computation.2 | async-start | bytes 1048576 | tf_op jit(solution)/shard_map/all_to_all | solution.py:169
  81.6 0.1 pad_add_fusion.place_ref
  81.6 15.1 %all-to-all-done.2 = bf16[16,32,512]{2,1,0:T(8,128)(2,1)S(1)} async-done(((bf16[16,32,512]{2,1,0:T(8,128)(2,1)}), bf16[16,32,512]{2,1,0:T(8,128)(2,1)S(1)}, u32[]{:S(2)}, u32[]{:S(2)}) %all-to-all-start.2) | async-done | bytes 524320 | tf_op jit(solution)/shard_map/all_to_all | solution.py:169
  96.8 7.8 %apply_roots.1 = (bf16[16,512]{1,0:T(8,128)(2,1)S(1)}, bf16[16,512]{1,0:T(8,128)(2,1)S(1)}) custom-call(s32[2]{0:T(128)S(1)} %pad_add_fusion.place_ref, bf16[512,512]{1,0:T(8,128)(2,1)S(1)} %bitcast.9), custom_call_target="tpu_custom_call" | custom-call | tf_op jit(solution)/shard_map/apply_roots/pallas_call | solution.py:137
  104.6 5.2 %collective-permute-start.2 = (bf16[16,512]{1,0:T(8,128)(2,1)S(1)}, bf16[16,512]{1,0:T(8,128)(2,1)S(1)}, u32[]{:S(2)}, u32[]{:S(2)}) collective-permute-start(bf16[16,512]{1,0:T(8,128)(2,1)S(1)} %get-tuple-element.8), channel_id=1, source_target_pairs={{0,8},{8,0},{1,9},{9,1},{2,10},{10,2},{3,11},{11,3},{4,12},{12,4},... | collective-permute-start | bytes 49160 | tf_op jit(solution)/shard_map/ppermute | solution.py:165
  109.8 0.8 collective-permute-done.2.arrived_ref
  110.6 0.6 join.1
Async XLA Ops:
  0.0 0.9 copy-start.1
  1.9 14.6 %copy-start = (bf16[384,1024]{1,0:T(8,128)(2,1)S(1)}, bf16[384,1024]{1,0:T(8,128)(2,1)}, u32[]{:S(2)}) copy-start(bf16[384,1024]{1,0:T(8,128)(2,1)} %own_ref.3) | copy-start | bytes 2359300
  1.9 41.3 %all-to-all-start = ((bf16[16,64,384]{2,1,0:T(8,128)(2,1)}), bf16[16,64,384]{2,1,0:T(8,128)(2,1)S(1)}, u32[]{:S(2)}, u32[]{:S(2)}) async-start(bf16[16,64,384]{2,1,0:T(8,128)(2,1)} %spread.1), calls=%async_computation | async-start | bytes 1572864 | tf_op jit(solution)/shard_map/all_to_all | solution.py:169
  16.5 26.7 %collective-permute-start = (bf16[384,1024]{1,0:T(8,128)(2,1)S(1)}, bf16[384,1024]{1,0:T(8,128)(2,1)S(1)}, u32[]{:S(2)}, u32[]{:S(2)}) collective-permute-start(bf16[384,1024]{1,0:T(8,128)(2,1)S(1)} %copy-done), channel_id=1, source_target_pairs={{0,16},{16,0},{1,17},{17,1},{2,18},{18,2},{3,19},{19,3},{4,20},{20... | collective-permute-start | bytes 2359304 | tf_op jit(solution)/shard_map/ppermute | solution.py:165
  44.4 5.3 %collective-permute-start.1 = (bf16[512,512]{1,0:T(8,128)(2,1)S(1)}, bf16[512,512]{1,0:T(8,128)(2,1)S(1)}, u32[]{:S(2)}, u32[]{:S(2)}) collective-permute-start(bf16[512,512]{1,0:T(8,128)(2,1)S(1)} %contract.3), channel_id=1, source_target_pairs={{0,8},{8,0},{1,9},{9,1},{2,10},{10,2},{3,11},{11,3},{4,12},{12,4},... | collective-permute-start | bytes 1572872 | tf_op jit(solution)/shard_map/ppermute | solution.py:165
  77.4 19.4 %all-to-all-start.2 = ((bf16[16,32,512]{2,1,0:T(8,128)(2,1)}), bf16[16,32,512]{2,1,0:T(8,128)(2,1)S(1)}, u32[]{:S(2)}, u32[]{:S(2)}) async-start(bf16[16,32,512]{2,1,0:T(8,128)(2,1)} %total_copies.1), calls=%async_computation.2 | async-start | bytes 1048576 | tf_op jit(solution)/shard_map/all_to_all | solution.py:169
  104.6 6.1 %collective-permute-start.2 = (bf16[16,512]{1,0:T(8,128)(2,1)S(1)}, bf16[16,512]{1,0:T(8,128)(2,1)S(1)}, u32[]{:S(2)}, u32[]{:S(2)}) collective-permute-start(bf16[16,512]{1,0:T(8,128)(2,1)S(1)} %get-tuple-element.8), channel_id=1, source_target_pairs={{0,8},{8,0},{1,9},{9,1},{2,10},{10,2},{3,11},{11,3},{4,12},{12,4},... | collective-permute-start | bytes 49160 | tf_op jit(solution)/shard_map/ppermute | solution.py:165

commit v4 on v3

--- a/solution.py
+++ b/solution.py
@@ -39,10 +39,9 @@
 def contract_kernel(place_ref, features_ref, own_ref, other_ref, out_ref):
     parity = place_ref[0]
     columns = pl.ds(pl.multiple_of(place_ref[1] * BLK, BLK), BLK)
-    out_ref[...] = (
-        dot(features_ref[parity], own_ref[:, columns])
-        + dot(features_ref[1 - parity], other_ref[:, columns])
-    ).astype(out_ref.dtype)
+    features = jnp.concatenate([features_ref[parity], features_ref[1 - parity]], axis=1)
+    cotangent = jnp.concatenate([own_ref[:, columns], other_ref[:, columns]], axis=0)
+    out_ref[...] = dot(features, cotangent).astype(out_ref.dtype)
 
 
 def contract(parity, half, features, own, other, dtype):
@@ -169,10 +168,33 @@
     return lax.all_to_all(value, axes, 0, 0, tiled=True)
 
 
+def partner(y, core):
+    return (y + 1 if (y + core) % 2 == 0 else y - 1) % 8
+
+
+def pair_groups():
+    groups = []
+    for core in range(2):
+        for even in range(0, 8, 2):
+            pair = (even, partner(even, core))
+            groups.append(
+                [(y * 2 + core) * 8 + feature for y in pair for feature in range(8)]
+            )
+    return groups
+
+
 def body(tokens, cotangent):
     core, p, q, zp = (lax.axis_index(name) for name in ("core", "p", "q", "zp"))
-    other = swap(cotangent, "p")
-    features = exchange(spread(tokens), ("p", "zh", "x")).reshape(2, BLK, 384)
+    pairs = [(y * 2 + k, partner(y, k) * 2 + k) for y in range(8) for k in range(2)]
+    other = lax.ppermute(cotangent, ("q", "p", "core"), pairs)
+    features = lax.all_to_all(
+        spread(tokens),
+        ("q", "p", "core", "zh", "x"),
+        0,
+        0,
+        axis_index_groups=pair_groups(),
+        tiled=True,
+    ).reshape(2, BLK, 384)
     sent = contract(p, 1 - core, features, cotangent, other, jnp.bfloat16)
     arrived = swap(sent, "core")
     keep = contract(p, core, features, cotangent, other, jnp.float32)

time: 112 us -> 108 us (0.964)
  waiting for transfers between devices: 39.5 us -> 37.3 us
  blocking collectives: 26.7 us -> 24.5 us
    ppermute x3 -> x2, waiting for transfers between devices: 24.3 us -> 1.49 us  [swap(): return lax.ppermute(value, axis, [(0, 1), (1, 0)])]
    all_to_all x0 -> x1, starting transfers between devices: none -> 16.4 us  [body(): lax.all_to_all(spread(tokens), ('q', 'p', 'core', 'zh', 'x'), 0, 0, axis_...]
    all_to_all x2 -> x1, starting transfers between devices: 18.7 us -> 3.89 us  [exchange(): return lax.all_to_all(value, axes, 0, 0, tiled=True)]
    ppermute x0 -> x1, waiting for transfers between devices: none -> 12.1 us  [body(): other = lax.ppermute(cotangent, ('q', 'p', 'core'), pairs)]
    all_to_all x0 -> x1, waiting for transfers between devices: none -> 8.73 us  [body(): lax.all_to_all(spread(tokens), ('q', 'p', 'core', 'zh', 'x'), 0, 0, axis_...]
    ppermute x3 -> x2, starting transfers between devices: 12.3 us -> 7.23 us  [swap(): return lax.ppermute(value, axis, [(0, 1), (1, 0)])]
    ppermute x0 -> x1, starting transfers between devices: none -> 4.48 us  [body(): other = lax.ppermute(cotangent, ('q', 'p', 'core'), pairs)]
    all_to_all x1, blocking collectives: 26.7 us -> 24.5 us  [exchange(): return lax.all_to_all(value, axes, 0, 0, tiled=True)]
  transfers between devices with their start and end apart: 5 -> 5, of which waited for: 4 -> 5; matrix products, arithmetic and copies ran while one was open for 0% -> 0% of each run, Pallas kernels for 1% -> 1%
where the time goes in v4:
time: 108 us
  waiting for transfers between devices  37.3 us (35%)
  starting transfers between devices  32 us (30%)
  blocking collectives  24.5 us (23%)
  Pallas kernels  12.7 us (12%)
    all_to_all x1, blocking collectives, exchange(): return lax.all_to_all(value, axes, 0, 0, tiled=True)  24.5 us
    all_to_all x1, starting transfers between devices, body(): lax.all_to_all(spread(tokens), ('q', 'p', 'core', 'zh', 'x'), 0, 0, axis_...  16.4 us
    all_to_all x1, waiting for transfers between devices, exchange(): return lax.all_to_all(value, axes, 0, 0, tiled=True)  15 us
    ppermute x1, waiting for transfers between devices, body(): other = lax.ppermute(cotangent, ('q', 'p', 'core'), pairs)  12.1 us
    all_to_all x1, waiting for transfers between devices, body(): lax.all_to_all(spread(tokens), ('q', 'p', 'core', 'zh', 'x'), 0, 0, axis_...  8.73 us
    pallas_call x1, Pallas kernels, apply_roots(): pl.pallas_call(roots_kernel, in_specs=[SMEM, VMEM], out_specs=[VMEM] * 2,...  7.81 us
    ppermute x2, starting transfers between devices, swap(): return lax.ppermute(value, axis, [(0, 1), (1, 0)])  7.23 us
    ppermute x1, starting transfers between devices, body(): other = lax.ppermute(cotangent, ('q', 'p', 'core'), pairs)  4.48 us
  transfers between devices with their start and end apart: 5, of which 5 were waited for; matrix products, arithmetic and copies ran while one was open for 0% of the time, Pallas kernels for 1%

profile of v4, /device:TPU:1, one launch (start us, length us, event | category | flops | bytes accessed | tf_op | source)
XLA Modules:
  0.0 107.7 jit_solution(2772150101011774962)
XLA Ops:
  0.0 0.0 copy-start.1
  0.0 0.9 copy-done.1
  0.9 1.0 spread.1
  1.9 0.0 copy-start
  1.9 16.4 %all-to-all-start = ((bf16[16,64,384]{2,1,0:T(8,128)(2,1)}), bf16[16,64,384]{2,1,0:T(8,128)(2,1)S(1)}, u32[]{:S(2)}, u32[]{:S(2)}) async-start(bf16[16,64,384]{2,1,0:T(8,128)(2,1)} %spread.1), calls=%async_computation | async-start | bytes 1572864 | tf_op jit(solution)/shard_map/all_to_all | solution.py:190
  18.3 0.0 copy-done
  18.4 4.5 %collective-permute-start = (bf16[384,1024]{1,0:T(8,128)(2,1)S(1)}, bf16[384,1024]{1,0:T(8,128)(2,1)S(1)}, u32[]{:S(2)}, u32[]{:S(2)}) collective-permute-start(bf16[384,1024]{1,0:T(8,128)(2,1)S(1)} %copy-done), channel_id=1, source_target_pairs={{0,16},{8,120},{16,0},{24,40},{32,48},{40,24},{48,32},{56,72},{64,... | collective-permute-start | bytes 2359304 | tf_op jit(solution)/shard_map/ppermute | solution.py:189
  22.9 0.1 pad_add_fusion.1.place_ref
  22.9 12.1 %collective-permute-done.other_ref = bf16[384,1024]{1,0:T(8,128)(2,1)S(1)} collective-permute-done((bf16[384,1024]{1,0:T(8,128)(2,1)S(1)}, bf16[384,1024]{1,0:T(8,128)(2,1)S(1)}, u32[]{:S(2)}, u32[]{:S(2)}) %collective-permute-start) | collective-permute-done | bytes 786464 | tf_op jit(solution)/shard_map/ppermute | solution.py:189
  35.0 8.7 %all-to-all-done = bf16[16,64,384]{2,1,0:T(8,128)(2,1)S(1)} async-done(((bf16[16,64,384]{2,1,0:T(8,128)(2,1)}), bf16[16,64,384]{2,1,0:T(8,128)(2,1)S(1)}, u32[]{:S(2)}, u32[]{:S(2)}) %all-to-all-start) | async-done | bytes 786464 | tf_op jit(solution)/shard_map/all_to_all | solution.py:190
  43.7 1.1 %contract.3 = bf16[512,512]{1,0:T(8,128)(2,1)S(1)} custom-call(s32[2]{0:T(128)S(1)} %pad_add_fusion.1.place_ref, bf16[2,512,384]{2,1,0:T(8,128)(2,1)S(1)} %bitcast.7, bf16[384,1024]{1,0:T(8,128)(2,1)S(1)} %copy-done, bf16[384,1024]{1,0:T(8,128)(2,1)S(1)} %collective-permute-done.other_ref), custom_call_target="tpu_custom_call" | custom-call | tf_op jit(solution)/shard_map/contract/pallas_call | solution.py:48
  44.9 1.9 %collective-permute-start.1 = (bf16[512,512]{1,0:T(8,128)(2,1)S(1)}, bf16[512,512]{1,0:T(8,128)(2,1)S(1)}, u32[]{:S(2)}, u32[]{:S(2)}) collective-permute-start(bf16[512,512]{1,0:T(8,128)(2,1)S(1)} %contract.3), channel_id=1, source_target_pairs={{0,8},{8,0},{1,9},{9,1},{2,10},{10,2},{3,11},{11,3},{4,12},{12,4},... | collective-permute-start | bytes 1572872 | tf_op jit(solution)/shard_map/ppermute | solution.py:164
  46.8 0.1 pad_add_fusion.2.place_ref
  46.9 1.1 %contract.2.keep_ref = f32[512,512]{1,0:T(8,128)S(1)} custom-call(s32[2]{0:T(128)S(1)} %pad_add_fusion.2.place_ref, bf16[2,512,384]{2,1,0:T(8,128)(2,1)S(1)} %bitcast.8, bf16[384,1024]{1,0:T(8,128)(2,1)S(1)} %copy-done, bf16[384,1024]{1,0:T(8,128)(2,1)S(1)} %collective-permute-done.other_ref), custom_call_target="tpu_custom_call" | custom-call | tf_op jit(solution)/shard_map/contract/pallas_call | solution.py:48
  48.0 0.7 collective-permute-done.1.arrived_ref
  48.7 0.1 add.25
  48.8 24.5 %all_to_all.15.shares_ref = bf16[16,32,512]{2,1,0:T(8,128)(2,1)S(1)} all-to-all(bf16[16,32,512]{2,1,0:T(8,128)(2,1)S(1)} %bitcast.10), channel_id=1, replica_groups=mesh['zr'=2,'zp'=2,'q'=4,'p'=2,'core'=2,'zh'=2,'x'=4] {'zr','q','zp'}, dimensions={0} | all-to-all | bytes 1048576 | tf_op jit(solution)/shard_map/all_to_all | solution.py:168
  73.2 0.9 total_copies.1
  74.1 3.9 %all-to-all-start.2 = ((bf16[16,32,512]{2,1,0:T(8,128)(2,1)}), bf16[16,32,512]{2,1,0:T(8,128)(2,1)S(1)}, u32[]{:S(2)}, u32[]{:S(2)}) async-start(bf16[16,32,512]{2,1,0:T(8,128)(2,1)} %total_copies.1), calls=%async_computation.2 | async-start | bytes 1048576 | tf_op jit(solution)/shard_map/all_to_all | solution.py:168
  78.1 0.1 pad_add_fusion.place_ref
  78.1 15.0 %all-to-all-done.2 = bf16[16,32,512]{2,1,0:T(8,128)(2,1)S(1)} async-done(((bf16[16,32,512]{2,1,0:T(8,128)(2,1)}), bf16[16,32,512]{2,1,0:T(8,128)(2,1)S(1)}, u32[]{:S(2)}, u32[]{:S(2)}) %all-to-all-start.2) | async-done | bytes 524320 | tf_op jit(solution)/shard_map/all_to_all | solution.py:168
  93.2 7.8 %apply_roots.1 = (bf16[16,512]{1,0:T(8,128)(2,1)S(1)}, bf16[16,512]{1,0:T(8,128)(2,1)S(1)}) custom-call(s32[2]{0:T(128)S(1)} %pad_add_fusion.place_ref, bf16[512,512]{1,0:T(8,128)(2,1)S(1)} %bitcast.9), custom_call_target="tpu_custom_call" | custom-call | tf_op jit(solution)/shard_map/apply_roots/pallas_call | solution.py:136
  101.0 5.3 %collective-permute-start.2 = (bf16[16,512]{1,0:T(8,128)(2,1)S(1)}, bf16[16,512]{1,0:T(8,128)(2,1)S(1)}, u32[]{:S(2)}, u32[]{:S(2)}) collective-permute-start(bf16[16,512]{1,0:T(8,128)(2,1)S(1)} %get-tuple-element.8), channel_id=1, source_target_pairs={{0,8},{8,0},{1,9},{9,1},{2,10},{10,2},{3,11},{11,3},{4,12},{12,4},... | collective-permute-start | bytes 49160 | tf_op jit(solution)/shard_map/ppermute | solution.py:164
  106.3 0.8 collective-permute-done.2.arrived_ref
  107.1 0.6 join.1
Async XLA Ops:
  0.0 0.9 copy-start.1
  1.9 16.4 %copy-start = (bf16[384,1024]{1,0:T(8,128)(2,1)S(1)}, bf16[384,1024]{1,0:T(8,128)(2,1)}, u32[]{:S(2)}) copy-start(bf16[384,1024]{1,0:T(8,128)(2,1)} %own_ref.3) | copy-start | bytes 2359300
  1.9 41.8 %all-to-all-start = ((bf16[16,64,384]{2,1,0:T(8,128)(2,1)}), bf16[16,64,384]{2,1,0:T(8,128)(2,1)S(1)}, u32[]{:S(2)}, u32[]{:S(2)}) async-start(bf16[16,64,384]{2,1,0:T(8,128)(2,1)} %spread.1), calls=%async_computation | async-start | bytes 1572864 | tf_op jit(solution)/shard_map/all_to_all | solution.py:190
  18.4 16.7 %collective-permute-start = (bf16[384,1024]{1,0:T(8,128)(2,1)S(1)}, bf16[384,1024]{1,0:T(8,128)(2,1)S(1)}, u32[]{:S(2)}, u32[]{:S(2)}) collective-permute-start(bf16[384,1024]{1,0:T(8,128)(2,1)S(1)} %copy-done), channel_id=1, source_target_pairs={{0,16},{8,120},{16,0},{24,40},{32,48},{40,24},{48,32},{56,72},{64,... | collective-permute-start | bytes 2359304 | tf_op jit(solution)/shard_map/ppermute | solution.py:189
  44.9 3.8 %collective-permute-start.1 = (bf16[512,512]{1,0:T(8,128)(2,1)S(1)}, bf16[512,512]{1,0:T(8,128)(2,1)S(1)}, u32[]{:S(2)}, u32[]{:S(2)}) collective-permute-start(bf16[512,512]{1,0:T(8,128)(2,1)S(1)} %contract.3), channel_id=1, source_target_pairs={{0,8},{8,0},{1,9},{9,1},{2,10},{10,2},{3,11},{11,3},{4,12},{12,4},... | collective-permute-start | bytes 1572872 | tf_op jit(solution)/shard_map/ppermute | solution.py:164
  74.1 19.0 %all-to-all-start.2 = ((bf16[16,32,512]{2,1,0:T(8,128)(2,1)}), bf16[16,32,512]{2,1,0:T(8,128)(2,1)S(1)}, u32[]{:S(2)}, u32[]{:S(2)}) async-start(bf16[16,32,512]{2,1,0:T(8,128)(2,1)} %total_copies.1), calls=%async_computation.2 | async-start | bytes 1048576 | tf_op jit(solution)/shard_map/all_to_all | solution.py:168
  101.0 6.1 %collective-permute-start.2 = (bf16[16,512]{1,0:T(8,128)(2,1)S(1)}, bf16[16,512]{1,0:T(8,128)(2,1)S(1)}, u32[]{:S(2)}, u32[]{:S(2)}) collective-permute-start(bf16[16,512]{1,0:T(8,128)(2,1)S(1)} %get-tuple-element.8), channel_id=1, source_target_pairs={{0,8},{8,0},{1,9},{9,1},{2,10},{10,2},{3,11},{11,3},{4,12},{12,4},... | collective-permute-start | bytes 49160 | tf_op jit(solution)/shard_map/ppermute | solution.py:164

commit v5 on v4

--- a/solution.py
+++ b/solution.py
@@ -9,9 +9,10 @@
 BLK = 512
 ITERS = 4
 ROWS = 32
-PARAMS = pltpu.CompilerParams(vmem_limit_bytes=48 * 1024 * 1024)
+PARAMS = pltpu.CompilerParams(vmem_limit_bytes=24 * 1024 * 1024)
 VMEM = pl.BlockSpec(memory_space=pltpu.VMEM)
 SMEM = pl.BlockSpec(memory_space=pltpu.SMEM)
+EARLY = pl.CostEstimate(flops=10**10, bytes_accessed=3 << 20, transcendentals=0)
 
 
 def dot(left, right):
@@ -36,28 +37,58 @@
     )(tokens)
 
 
-def contract_kernel(place_ref, features_ref, own_ref, other_ref, out_ref):
-    parity = place_ref[0]
-    columns = pl.ds(pl.multiple_of(place_ref[1] * BLK, BLK), BLK)
-    features = jnp.concatenate([features_ref[parity], features_ref[1 - parity]], axis=1)
-    cotangent = jnp.concatenate([own_ref[:, columns], other_ref[:, columns]], axis=0)
-    out_ref[...] = dot(features, cotangent).astype(out_ref.dtype)
-
-
-def contract(parity, half, features, own, other, dtype):
+def stack_kernel(parity_ref, own_ref, other_ref, out_ref, sems):
+    parity = parity_ref[0]
+    copies = [
+        pltpu.make_async_copy(
+            source, out_ref.at[pl.ds(pl.multiple_of(place * 384, 384), 384)], sems.at[i]
+        )
+        for i, (source, place) in enumerate(((own_ref, parity), (other_ref, 1 - parity)))
+    ]
+    for copy in copies:
+        copy.start()
+    for copy in copies:
+        copy.wait()
+
+
+def stack(parity, own, other):
+    return pl.pallas_call(
+        stack_kernel,
+        in_specs=[SMEM] + [pl.BlockSpec(memory_space=pl.ANY)] * 2,
+        out_specs=VMEM,
+        out_shape=jax.ShapeDtypeStruct((768, 2 * BLK), jnp.bfloat16),
+        scratch_shapes=[pltpu.SemaphoreType.DMA((2,))],
+        compiler_params=PARAMS,
+        cost_estimate=EARLY,
+        name="stack",
+    )(parity[None], own, other)
+
+
+def contract_kernel(half_ref, features_ref, cotangent_ref, out_ref):
+    rows = pl.ds(pl.multiple_of(half_ref[0] * ROWS, ROWS), ROWS)
+    features = jnp.concatenate(
+        [features_ref[parity, :, rows, :].reshape(256, 384) for parity in range(2)], axis=1
+    )
+    out_ref[...] = dot(features, cotangent_ref[...]).astype(out_ref.dtype)
+
+
+def contract(half, features, cotangent, dtype):
     return pl.pallas_call(
         contract_kernel,
-        in_specs=[SMEM] + [VMEM] * 3,
-        out_specs=VMEM,
-        out_shape=jax.ShapeDtypeStruct((BLK, BLK), dtype),
+        in_specs=[SMEM] + [VMEM] * 2,
+        out_specs=VMEM,
+        out_shape=jax.ShapeDtypeStruct((256, 2 * BLK), dtype),
         compiler_params=PARAMS,
         name="contract",
-    )(jnp.stack([parity, half]), features, own, other)
-
-
-def add_kernel(keep_ref, arrived_ref, sum_ref):
-    total = keep_ref[...] + arrived_ref[...].astype(jnp.float32)
-    sum_ref[...] = total.astype(sum_ref.dtype)
+    )(half[None], features, cotangent)
+
+
+def add_kernel(keep_ref, arrived_ref, shares_ref):
+    for place in range(8):
+        rows = slice(place * ROWS, place * ROWS + ROWS)
+        total = (keep_ref[rows] + arrived_ref[rows].astype(jnp.float32)).astype(jnp.bfloat16)
+        shares_ref[place * 2] = total[:, :BLK]
+        shares_ref[place * 2 + 1] = total[:, BLK:]
 
 
 def add(keep, arrived):
@@ -65,7 +96,7 @@
         add_kernel,
         in_specs=[VMEM] * 2,
         out_specs=VMEM,
-        out_shape=jax.ShapeDtypeStruct((BLK, BLK), jnp.bfloat16),
+        out_shape=jax.ShapeDtypeStruct((16, ROWS, BLK), jnp.bfloat16),
         compiler_params=PARAMS,
         name="add",
     )(keep, arrived)
@@ -76,7 +107,7 @@
     for share in range(1, 16):
         total += shares_ref[share].astype(jnp.float32)
     total = total.astype(jnp.bfloat16)
-    for copy in range(16):
+    for copy in range(8):
         copies_ref[copy] = total
 
 
@@ -85,14 +116,14 @@
         total_kernel,
         in_specs=[VMEM],
         out_specs=VMEM,
-        out_shape=jax.ShapeDtypeStruct((16, ROWS, BLK), jnp.bfloat16),
+        out_shape=jax.ShapeDtypeStruct((8, ROWS, BLK), jnp.bfloat16),
         compiler_params=PARAMS,
         name="total_copies",
     )(shares)
 
 
-def roots_kernel(place_ref, block_ref, keep_ref, send_ref):
-    block = block_ref[...]
+def roots_kernel(place_ref, own_ref, arrived_ref, keep_ref, send_ref):
+    block = jnp.concatenate([own_ref[...], arrived_ref[...]], axis=0)
     flipped = block.T
     wide = block.astype(jnp.float32)
     trace = jnp.sum(wide * wide, keepdims=True)
@@ -109,9 +140,11 @@
 
     left, left_scale = start(dot(block, flipped))
     right, right_scale = start(dot(flipped, block))
-    order = lax.rem(lax.broadcasted_iota(jnp.int32, (ROWS, BLK), 0) + place_ref[1] * 16, ROWS)
-    own = lax.broadcasted_iota(jnp.int32, (ROWS, BLK), 1) == order + place_ref[0]
-    rows = jnp.where(own, left_scale, 0.0)
+    ids = lax.broadcasted_iota(jnp.int32, (ROWS, BLK), 0)
+    picked = jnp.where(ids < 16, ids + place_ref[0], ids - 16 + place_ref[1])
+    rows = jnp.where(
+        lax.broadcasted_iota(jnp.int32, (ROWS, BLK), 1) == picked, left_scale, 0.0
+    )
     steps = []
     for it in range(ITERS):
         factors = [(base - m * 0.25).astype(jnp.bfloat16) for m in (left, right)]
@@ -131,25 +164,25 @@
     send_ref[...] = value[16:]
 
 
-def apply_roots(first, core, block):
+def apply_roots(places, own, arrived):
     piece = jax.ShapeDtypeStruct((16, BLK), jnp.bfloat16)
     return pl.pallas_call(
         roots_kernel,
-        in_specs=[SMEM, VMEM],
+        in_specs=[SMEM] + [VMEM] * 2,
         out_specs=[VMEM] * 2,
         out_shape=[piece] * 2,
         compiler_params=PARAMS,
         name="apply_roots",
-    )(jnp.stack([first, core]), block)
-
-
-def join_kernel(core_ref, keep_ref, arrived_ref, out_ref):
-    core = core_ref[0]
-    out_ref[:, pl.ds(pl.multiple_of(core * BLK, BLK), BLK)] = keep_ref[...]
-    out_ref[:, pl.ds(pl.multiple_of((1 - core) * BLK, BLK), BLK)] = arrived_ref[...]
-
-
-def join(core, keep, arrived):
+    )(places, own, arrived)
+
+
+def join_kernel(column_ref, keep_ref, arrived_ref, out_ref):
+    column = column_ref[0]
+    out_ref[:, pl.ds(pl.multiple_of(column * BLK, BLK), BLK)] = keep_ref[...]
+    out_ref[:, pl.ds(pl.multiple_of((1 - column) * BLK, BLK), BLK)] = arrived_ref[...]
+
+
+def join(column, keep, arrived):
     return pl.pallas_call(
         join_kernel,
         in_specs=[SMEM] + [VMEM] * 2,
@@ -157,7 +190,7 @@
         out_shape=jax.ShapeDtypeStruct((16, 2 * BLK), jnp.bfloat16),
         compiler_params=PARAMS,
         name="join",
-    )(core[None], keep, arrived)
+    )(column[None], keep, arrived)
 
 
 def swap(value, axis):
@@ -194,15 +227,16 @@
         0,
         axis_index_groups=pair_groups(),
         tiled=True,
-    ).reshape(2, BLK, 384)
-    sent = contract(p, 1 - core, features, cotangent, other, jnp.bfloat16)
-    arrived = swap(sent, "core")
-    keep = contract(p, core, features, cotangent, other, jnp.float32)
-    shares = exchange(add(keep, arrived).reshape(16, ROWS, BLK), ("zr", "q", "zp"))
-    block = exchange(total_copies(shares), ("p", "q", "zp")).reshape(BLK, BLK)
-    first = ((q % 2) * 8 + (zp * 2 + q // 2) * 2 + p) * ROWS
-    keep, sent = apply_roots(first, core, block)
-    return join(core, keep, swap(sent, "core"))
+    ).reshape(2, 8, 64, 384)
+    both = stack(p, cotangent, other)
+    arrived = swap(contract(1 - core, features, both, jnp.bfloat16), "core")
+    keep = contract(core, features, both, jnp.float32)
+    shares = exchange(add(keep, arrived), ("zr", "q", "zp"))
+    own = exchange(total_copies(shares), ("p", "q")).reshape(256, BLK)
+    place = jnp.where(p == core, 0, 256) + ((q % 2) * 4 + q // 2) * ROWS + core * 16
+    places = jnp.stack([place + zp * 64, place + (1 - zp) * 64])
+    keep, sent = apply_roots(places, own, swap(own, "core"))
+    return join(zp, keep, swap(sent, "zp"))
 
 
 def solution(mesh):

time: 108 us -> 108 us (level); the launches traced: 108 us -> 106 us
  blocking collectives: 24.5 us -> 37.1 us
  waiting for transfers between devices: 37.3 us -> 27.3 us
  starting transfers between devices: 32 us -> 27.4 us
  local copies, waits for them, and re-layouts: 0.9 us -> 2.93 us
  Pallas kernels: 12.7 us -> 10.9 us
    all_to_all x1 -> x0, waiting for transfers between devices: 15 us -> none  [exchange(): return lax.all_to_all(value, axes, 0, 0, tiled=True)]
    all_to_all x1, waiting for transfers between devices: 8.73 us -> 22.7 us  [body(): lax.all_to_all(spread(tokens), ('q', 'p', 'core', 'zh', 'x'), 0, 0, axis_...]
    all_to_all x1 -> x2, blocking collectives: 24.5 us -> 37.1 us  [exchange(): return lax.all_to_all(value, axes, 0, 0, tiled=True)]
    ppermute x1, waiting for transfers between devices: 12.1 us -> 0.01 us  [body(): other = lax.ppermute(cotangent, ('q', 'p', 'core'), pairs)]
    all_to_all x1 -> x0, starting transfers between devices: 3.89 us -> none  [exchange(): return lax.all_to_all(value, axes, 0, 0, tiled=True)]
    all_to_all x1, starting transfers between devices: 16.4 us -> 12.6 us  [body(): lax.all_to_all(spread(tokens), ('q', 'p', 'core', 'zh', 'x'), 0, 0, axis_...]
    ppermute x2 -> x3, waiting for transfers between devices: 1.49 us -> 4.58 us  [swap(): return lax.ppermute(value, axis, [(0, 1), (1, 0)])]
    unnamed x4 -> x8, local copies, waits for them, and re-layouts: 0.9 us -> 2.93 us
  transfers between devices with their start and end apart: 5 -> 5, of which waited for: 5 -> 4; matrix products, arithmetic and copies ran while one was open for 0% -> 0% of each run, Pallas kernels for 1% -> 2%
where the time goes in v5:
time: 108 us; the launch traced here: 106 us
  blocking collectives  37.1 us (34%)
  starting transfers between devices  27.4 us (25%)
  waiting for transfers between devices  27.3 us (25%)
  Pallas kernels  10.9 us (10%)
  local copies, waits for them, and re-layouts  2.93 us (3%)
    all_to_all x2, blocking collectives, exchange(): return lax.all_to_all(value, axes, 0, 0, tiled=True)  37.1 us
    all_to_all x1, waiting for transfers between devices, body(): lax.all_to_all(spread(tokens), ('q', 'p', 'core', 'zh', 'x'), 0, 0, axis_...  22.7 us
    all_to_all x1, starting transfers between devices, body(): lax.all_to_all(spread(tokens), ('q', 'p', 'core', 'zh', 'x'), 0, 0, axis_...  12.6 us
    ppermute x3, starting transfers between devices, swap(): return lax.ppermute(value, axis, [(0, 1), (1, 0)])  8.88 us
    pallas_call x1, Pallas kernels, apply_roots(): pl.pallas_call(roots_kernel, in_specs=[SMEM] + [VMEM] * 2, out_specs=[VME...  7.81 us
    ppermute x1, starting transfers between devices, body(): other = lax.ppermute(cotangent, ('q', 'p', 'core'), pairs)  5.91 us
    ppermute x3, waiting for transfers between devices, swap(): return lax.ppermute(value, axis, [(0, 1), (1, 0)])  4.58 us
    unnamed x8, local copies, waits for them, and re-layouts  2.93 us
  transfers between devices with their start and end apart: 5, of which 4 were waited for; matrix products, arithmetic and copies ran while one was open for 0% of the time, Pallas kernels for 2%

profile of v5, /device:TPU:1, one launch (start us, length us, event | category | flops | bytes accessed | tf_op | source)
XLA Modules:
  0.0 105.8 jit_solution(2951956215902435613)
XLA Ops:
  0.0 5.9 %collective-permute-start = (bf16[384,1024]{1,0:T(8,128)(2,1)}, bf16[384,1024]{1,0:T(8,128)(2,1)S(1)}, u32[]{:S(2)}, u32[]{:S(2)}) collective-permute-start(bf16[384,1024]{1,0:T(8,128)(2,1)} %own_ref.1), channel_id=1, source_target_pairs={{0,16},{8,120},{16,0},{24,40},{32,48},{40,24},{48,32},{56,72},{64,... | collective-permute-start | bytes 2359304 | tf_op jit(solution)/shard_map/ppermute | solution.py:222
  5.9 0.0 copy-start
  5.9 0.9 copy-done
  6.8 0.0 copy-start.1
  6.8 1.0 spread.1
  7.8 12.6 %all-to-all-start = ((bf16[16,64,384]{2,1,0:T(8,128)(2,1)}), bf16[16,64,384]{2,1,0:T(8,128)(2,1)S(1)}, u32[]{:S(2)}, u32[]{:S(2)}) async-start(bf16[16,64,384]{2,1,0:T(8,128)(2,1)} %spread.1), calls=%async_computation | async-start | bytes 1572864 | tf_op jit(solution)/shard_map/all_to_all | solution.py:223
  20.4 0.0 collective-permute-done.other_ref
  20.4 0.0 copy-start.2
  20.4 0.9 copy-done.2
  21.3 0.0 copy-done.1
  21.3 0.0 copy-start.3
  21.3 1.1 %copy-done.3 = bf16[384,1024]{1,0:T(8,128)(2,1)S(1)} copy-done((bf16[384,1024]{1,0:T(8,128)(2,1)S(1)}, bf16[384,1024]{1,0:T(8,128)(2,1)}, u32[]{:S(2)}) %copy-start.3) | copy-done | bytes 786456
  22.5 0.1 stack.13.cotangent_ref
  22.6 22.7 %all-to-all-done = bf16[16,64,384]{2,1,0:T(8,128)(2,1)S(1)} async-done(((bf16[16,64,384]{2,1,0:T(8,128)(2,1)}), bf16[16,64,384]{2,1,0:T(8,128)(2,1)S(1)}, u32[]{:S(2)}, u32[]{:S(2)}) %all-to-all-start) | async-done | bytes 786464 | tf_op jit(solution)/shard_map/all_to_all | solution.py:223
  45.3 0.6 contract.3
  45.9 1.9 %collective-permute-start.1 = (bf16[256,1024]{1,0:T(8,128)(2,1)S(1)}, bf16[256,1024]{1,0:T(8,128)(2,1)S(1)}, u32[]{:S(2)}, u32[]{:S(2)}) collective-permute-start(bf16[256,1024]{1,0:T(8,128)(2,1)S(1)} %contract.3), channel_id=1, source_target_pairs={{0,8},{8,0},{1,9},{9,1},{2,10},{10,2},{3,11},{11,3},{4,12},{12,4},... | collective-permute-start | bytes 1572872 | tf_op jit(solution)/shard_map/ppermute | solution.py:197
  47.8 0.6 contract.2.keep_ref
  48.4 1.3 %collective-permute-done.1.arrived_ref = bf16[256,1024]{1,0:T(8,128)(2,1)S(1)} collective-permute-done((bf16[256,1024]{1,0:T(8,128)(2,1)S(1)}, bf16[256,1024]{1,0:T(8,128)(2,1)S(1)}, u32[]{:S(2)}, u32[]{:S(2)}) %collective-permute-start.1) | collective-permute-done | bytes 524320 | tf_op jit(solution)/shard_map/ppermute | solution.py:197
  49.7 0.1 add.29
  49.8 26.4 %all_to_all.15.shares_ref = bf16[16,32,512]{2,1,0:T(8,128)(2,1)S(1)} all-to-all(bf16[16,32,512]{2,1,0:T(8,128)(2,1)S(1)} %add.29), channel_id=1, replica_groups=mesh['zr'=2,'zp'=2,'q'=4,'p'=2,'core'=2,'zh'=2,'x'=4] {'zr','q','zp'}, dimensions={0} | all-to-all | bytes 1048576 | tf_op jit(solution)/shard_map/all_to_all | solution.py:201
  76.2 0.1 total_copies.1
  76.2 10.8 %all_to_all.16 = bf16[8,32,512]{2,1,0:T(8,128)(2,1)S(1)} all-to-all(bf16[8,32,512]{2,1,0:T(8,128)(2,1)S(1)} %total_copies.1), channel_id=1, replica_groups=mesh['zr'=2,'zp'=2,'q'=4,'p'=2,'core'=2,'zh'=2,'x'=4] {'p','q'}, dimensions={0} | all-to-all | bytes 524288 | tf_op jit(solution)/shard_map/all_to_all | solution.py:201
  87.0 4.7 %collective-permute-start.2 = (bf16[256,512]{1,0:T(8,128)(2,1)S(1)}, bf16[256,512]{1,0:T(8,128)(2,1)S(1)}, u32[]{:S(2)}, u32[]{:S(2)}) collective-permute-start(bf16[256,512]{1,0:T(8,128)(2,1)S(1)} %bitcast.10), channel_id=1, source_target_pairs={{0,8},{8,0},{1,9},{9,1},{2,10},{10,2},{3,11},{11,3},{4,12},{12,4},... | collective-permute-start | bytes 786440 | tf_op jit(solution)/shard_map/ppermute | solution.py:197
  91.8 0.1 pad_add_fusion.place_ref
  91.9 1.0 collective-permute-done.2.arrived_ref
  92.9 7.8 %apply_roots.1 = (bf16[16,512]{1,0:T(8,128)(2,1)S(1)}, bf16[16,512]{1,0:T(8,128)(2,1)S(1)}) custom-call(s32[2]{0:T(128)S(1)} %pad_add_fusion.place_ref, bf16[256,512]{1,0:T(8,128)(2,1)S(1)} %bitcast.11, bf16[256,512]{1,0:T(8,128)(2,1)S(1)} %collective-permute-done.2.arrived_ref), custom_call_target="tpu_custom_call" | custom-call | tf_op jit(solution)/shard_map/apply_roots/pallas_call | solution.py:169
  100.7 2.2 %collective-permute-start.3 = (bf16[16,512]{1,0:T(8,128)(2,1)S(1)}, bf16[16,512]{1,0:T(8,128)(2,1)S(1)}, u32[]{:S(2)}, u32[]{:S(2)}) collective-permute-start(bf16[16,512]{1,0:T(8,128)(2,1)S(1)} %get-tuple-element.8), channel_id=1, source_target_pairs={{0,128},{128,0},{1,129},{129,1},{2,130},{130,2},{3,131},{131,3},{4... | collective-permute-start | bytes 49160 | tf_op jit(solution)/shard_map/ppermute | solution.py:197
  102.9 2.3 %collective-permute-done.3.arrived_ref = bf16[16,512]{1,0:T(8,128)(2,1)S(1)} collective-permute-done((bf16[16,512]{1,0:T(8,128)(2,1)S(1)}, bf16[16,512]{1,0:T(8,128)(2,1)S(1)}, u32[]{:S(2)}, u32[]{:S(2)}) %collective-permute-start.3) | collective-permute-done | bytes 16416 | tf_op jit(solution)/shard_map/ppermute | solution.py:197
  105.2 0.6 join.1
Async XLA Ops:
  0.0 20.4 %collective-permute-start = (bf16[384,1024]{1,0:T(8,128)(2,1)}, bf16[384,1024]{1,0:T(8,128)(2,1)S(1)}, u32[]{:S(2)}, u32[]{:S(2)}) collective-permute-start(bf16[384,1024]{1,0:T(8,128)(2,1)} %own_ref.1), channel_id=1, source_target_pairs={{0,16},{8,120},{16,0},{24,40},{32,48},{40,24},{48,32},{56,72},{64,... | collective-permute-start | bytes 2359304 | tf_op jit(solution)/shard_map/ppermute | solution.py:222
  5.9 0.9 copy-start
  6.8 14.5 %copy-start.1 = (bf16[384,1024]{1,0:T(8,128)(2,1)S(1)}, bf16[384,1024]{1,0:T(8,128)(2,1)}, u32[]{:S(2)}) copy-start(bf16[384,1024]{1,0:T(8,128)(2,1)} %own_ref.1) | copy-start | bytes 2359300
  7.8 37.5 %all-to-all-start = ((bf16[16,64,384]{2,1,0:T(8,128)(2,1)}), bf16[16,64,384]{2,1,0:T(8,128)(2,1)S(1)}, u32[]{:S(2)}, u32[]{:S(2)}) async-start(bf16[16,64,384]{2,1,0:T(8,128)(2,1)} %spread.1), calls=%async_computation | async-start | bytes 1572864 | tf_op jit(solution)/shard_map/all_to_all | solution.py:223
  20.4 0.9 copy-start.2
  21.3 1.1 %copy-start.3 = (bf16[384,1024]{1,0:T(8,128)(2,1)S(1)}, bf16[384,1024]{1,0:T(8,128)(2,1)}, u32[]{:S(2)}) copy-start(bf16[384,1024]{1,0:T(8,128)(2,1)} %copy-done.2) | copy-start | bytes 2359300
  45.9 3.8 %collective-permute-start.1 = (bf16[256,1024]{1,0:T(8,128)(2,1)S(1)}, bf16[256,1024]{1,0:T(8,128)(2,1)S(1)}, u32[]{:S(2)}, u32[]{:S(2)}) collective-permute-start(bf16[256,1024]{1,0:T(8,128)(2,1)S(1)} %contract.3), channel_id=1, source_target_pairs={{0,8},{8,0},{1,9},{9,1},{2,10},{10,2},{3,11},{11,3},{4,12},{12,4},... | collective-permute-start | bytes 1572872 | tf_op jit(solution)/shard_map/ppermute | solution.py:197
  87.0 5.9 %collective-permute-start.2 = (bf16[256,512]{1,0:T(8,128)(2,1)S(1)}, bf16[256,512]{1,0:T(8,128)(2,1)S(1)}, u32[]{:S(2)}, u32[]{:S(2)}) collective-permute-start(bf16[256,512]{1,0:T(8,128)(2,1)S(1)} %bitcast.10), channel_id=1, source_target_pairs={{0,8},{8,0},{1,9},{9,1},{2,10},{10,2},{3,11},{11,3},{4,12},{12,4},... | collective-permute-start | bytes 786440 | tf_op jit(solution)/shard_map/ppermute | solution.py:197
  100.7 4.5 %collective-permute-start.3 = (bf16[16,512]{1,0:T(8,128)(2,1)S(1)}, bf16[16,512]{1,0:T(8,128)(2,1)S(1)}, u32[]{:S(2)}, u32[]{:S(2)}) collective-permute-start(bf16[16,512]{1,0:T(8,128)(2,1)S(1)} %get-tuple-element.8), channel_id=1, source_target_pairs={{0,128},{128,0},{1,129},{129,1},{2,130},{130,2},{3,131},{131,3},{4... | collective-permute-start | bytes 49160 | tf_op jit(solution)/shard_map/ppermute | solution.py:197

commit v6 on v5

--- a/solution.py
+++ b/solution.py
@@ -7,12 +7,12 @@
 from jax.sharding import PartitionSpec as P
 
 BLK = 512
+HALF = 256
 ITERS = 4
 ROWS = 32
 PARAMS = pltpu.CompilerParams(vmem_limit_bytes=24 * 1024 * 1024)
 VMEM = pl.BlockSpec(memory_space=pltpu.VMEM)
 SMEM = pl.BlockSpec(memory_space=pltpu.SMEM)
-EARLY = pl.CostEstimate(flops=10**10, bytes_accessed=3 << 20, transcendentals=0)
 
 
 def dot(left, right):
@@ -59,7 +59,6 @@
         out_shape=jax.ShapeDtypeStruct((768, 2 * BLK), jnp.bfloat16),
         scratch_shapes=[pltpu.SemaphoreType.DMA((2,))],
         compiler_params=PARAMS,
-        cost_estimate=EARLY,
         name="stack",
     )(parity[None], own, other)
 
@@ -122,55 +121,101 @@
     )(shares)
 
 
-def roots_kernel(place_ref, own_ref, arrived_ref, keep_ref, send_ref):
-    block = jnp.concatenate([own_ref[...], arrived_ref[...]], axis=0)
-    flipped = block.T
-    wide = block.astype(jnp.float32)
+def symmetric_product(left, right, store, rows=None):
+    top = left[:HALF, :] if rows is None else jnp.concatenate([left[:HALF, :], rows], axis=0)
+    top = dot(top, right[...])
+    store(0, 0, top[:HALF, :HALF])
+    store(0, HALF, top[:HALF, HALF:])
+    store(HALF, HALF, dot(left[HALF:, :], right[:, HALF:]))
+    return top[HALF:].astype(jnp.bfloat16)
+
+
+def put(ref, i, j, value):
+    ref[i : i + HALF, j : j + HALF] = value
+    if i != j:
+        ref[j : j + HALF, i : i + HALF] = value.T
+
+
+def rounded(ref):
+    return lambda i, j, value: put(ref, i, j, value.astype(jnp.bfloat16))
+
+
+def roots_kernel(
+    place_ref, own_ref, arrived_ref, keep_ref, send_ref, block_ref, flipped_ref, *scratch
+):
+    lgram, rgram, lstep, rstep, lsquare, rsquare, lfourth, rfourth, lmat, rmat, rroot = scratch
+    block_ref[:HALF, :] = own_ref[...]
+    block_ref[HALF:, :] = arrived_ref[...]
+    flipped_ref[...] = block_ref[...].T
+    wide = block_ref[...].astype(jnp.float32)
     trace = jnp.sum(wide * wide, keepdims=True)
-    row_ids = lax.broadcasted_iota(jnp.int32, (BLK, BLK), 0)
-    col_ids = lax.broadcasted_iota(jnp.int32, (BLK, BLK), 1)
-    diagonal = row_ids == col_ids
-    damp = jnp.where(diagonal, 0.1 * trace / BLK + 1e-06, 0.0)
+    damp = 0.1 * trace / BLK + 1e-06
+    diagonal = lax.broadcasted_iota(jnp.int32, (HALF, HALF), 0) == lax.broadcasted_iota(
+        jnp.int32, (HALF, HALF), 1
+    )
     base = jnp.where(diagonal, 1.25, 0.0)
 
-    def start(gram):
-        matrix = gram + damp
-        inverse = lax.rsqrt(jnp.sum(matrix * matrix, keepdims=True))
-        return matrix * inverse, jnp.sqrt(jnp.sqrt(inverse))
-
-    left, left_scale = start(dot(block, flipped))
-    right, right_scale = start(dot(flipped, block))
+    def set_step(step, i, j, value):
+        put(step, i, j, ((base if i == j else 0.0) - value * 0.25).astype(jnp.bfloat16))
+
+    def start(left, right, gram, mat, step):
+        parts = []
+
+        def store(i, j, value):
+            gram[i : i + HALF, j : j + HALF] = value
+            if i == j:
+                value = value + jnp.where(diagonal, damp, 0.0)
+            parts.append(jnp.sum(value * value, keepdims=True) * (1.0 if i == j else 2.0))
+
+        symmetric_product(left, right, store)
+        inverse = lax.rsqrt(parts[0] + parts[1] + parts[2])
+        for i, j in ((0, 0), (0, HALF), (HALF, HALF)):
+            value = gram[i : i + HALF, j : j + HALF]
+            if i == j:
+                value = value + jnp.where(diagonal, damp, 0.0)
+            value = value * inverse
+            put(mat, i, j, value.astype(jnp.bfloat16))
+            set_step(step, i, j, value)
+        return jnp.sqrt(jnp.sqrt(inverse))
+
+    lscale = start(block_ref, flipped_ref, lgram, lmat, lstep)
+    rscale = start(flipped_ref, block_ref, rgram, rmat, rstep)
     ids = lax.broadcasted_iota(jnp.int32, (ROWS, BLK), 0)
     picked = jnp.where(ids < 16, ids + place_ref[0], ids - 16 + place_ref[1])
-    rows = jnp.where(
-        lax.broadcasted_iota(jnp.int32, (ROWS, BLK), 1) == picked, left_scale, 0.0
-    )
-    steps = []
-    for it in range(ITERS):
-        factors = [(base - m * 0.25).astype(jnp.bfloat16) for m in (left, right)]
-        rows = dot(rows.astype(jnp.bfloat16), factors[0])
-        steps.append(factors[1])
-        if it < ITERS - 1:
-            squares = [dot(f, f).astype(jnp.bfloat16) for f in factors]
-            fourths = [dot(s, s).astype(jnp.bfloat16) for s in squares]
-            left, right = (
-                dot(f, m.astype(jnp.bfloat16)) for f, m in zip(fourths, (left, right))
-            )
-    half = dot(rows.astype(jnp.bfloat16), block).astype(jnp.bfloat16)
-    value = half * right_scale.astype(jnp.bfloat16)
-    for step in steps:
-        value = dot(value, step).astype(jnp.bfloat16)
+    columns = lax.broadcasted_iota(jnp.int32, (ROWS, BLK), 1)
+    rows = jnp.where(columns == picked, lscale, 0.0).astype(jnp.bfloat16)
+    rroot[...] = rstep[...] * rscale.astype(jnp.bfloat16)
+    for it in range(ITERS - 1):
+        rows = symmetric_product(lstep, lstep, rounded(lsquare), rows)
+        symmetric_product(rstep, rstep, rounded(rsquare))
+        if it > 0:
+            rroot[...] = dot(rroot[...], rstep[...]).astype(jnp.bfloat16)
+        symmetric_product(lsquare, lsquare, rounded(lfourth))
+        symmetric_product(rsquare, rsquare, rounded(rfourth))
+        for fourth, mat, step in ((lfourth, lmat, lstep), (rfourth, rmat, rstep)):
+            parts = []
+            symmetric_product(fourth, mat, lambda i, j, value: parts.append((i, j, value)))
+            for i, j, value in parts:
+                if it < ITERS - 2:
+                    put(mat, i, j, value.astype(jnp.bfloat16))
+                set_step(step, i, j, value)
+    rows = dot(rows, lstep[...]).astype(jnp.bfloat16)
+    half = dot(rows, block_ref[...]).astype(jnp.bfloat16)
+    rroot[...] = dot(rroot[...], rstep[...]).astype(jnp.bfloat16)
+    value = dot(half, rroot[...]).astype(jnp.bfloat16)
     keep_ref[...] = value[:16]
     send_ref[...] = value[16:]
 
 
 def apply_roots(places, own, arrived):
     piece = jax.ShapeDtypeStruct((16, BLK), jnp.bfloat16)
+    narrow = pltpu.VMEM((BLK, BLK), jnp.bfloat16)
     return pl.pallas_call(
         roots_kernel,
         in_specs=[SMEM] + [VMEM] * 2,
         out_specs=[VMEM] * 2,
         out_shape=[piece] * 2,
+        scratch_shapes=[narrow] * 2 + [pltpu.VMEM((BLK, BLK), jnp.float32)] * 2 + [narrow] * 9,
         compiler_params=PARAMS,
         name="apply_roots",
     )(places, own, arrived)

time: 108 us -> 104 us (0.963)
  the two profiles are of different devices: /device:TPU:1 before, /device:TPU:12 now
where the time goes in v6:
time: 104 us; the launch traced here: 103 us
  blocking collectives  42.1 us (40%)
  waiting for transfers between devices  25.7 us (25%)
  starting transfers between devices  22.6 us (22%)
  Pallas kernels  9.56 us (9%)
  local copies, waits for them, and re-layouts  2.95 us (3%)
    all_to_all x2, blocking collectives, exchange(): return lax.all_to_all(value, axes, 0, 0, tiled=True)  42.1 us
    all_to_all x1, starting transfers between devices, body(): lax.all_to_all(spread(tokens), ('q', 'p', 'core', 'zh', 'x'), 0, 0, axis_...  14.2 us
    ppermute x1, waiting for transfers between devices, body(): other = lax.ppermute(cotangent, ('q', 'p', 'core'), pairs)  14 us
    pallas_call x1, Pallas kernels, apply_roots(): pl.pallas_call(roots_kernel, in_specs=[SMEM] + [VMEM] * 2, out_specs=[VME...  6.49 us
    ppermute x3, waiting for transfers between devices, swap(): return lax.ppermute(value, axis, [(0, 1), (1, 0)])  6.13 us
    ppermute x3, starting transfers between devices, swap(): return lax.ppermute(value, axis, [(0, 1), (1, 0)])  6.01 us
    all_to_all x1, waiting for transfers between devices, body(): lax.all_to_all(spread(tokens), ('q', 'p', 'core', 'zh', 'x'), 0, 0, axis_...  5.63 us
    unnamed x8, local copies, waits for them, and re-layouts  2.95 us
  transfers between devices with their start and end apart: 5, of which 5 were waited for; matrix products, arithmetic and copies ran while one was open for 0% of the time, Pallas kernels for 1%

profile of v6, /device:TPU:12, one launch (start us, length us, event | category | flops | bytes accessed | tf_op | source)
XLA Modules:
  0.0 103.2 jit_solution(12289542915500967140)
XLA Ops:
  0.0 0.0 copy-start.3
  0.0 0.9 copy-done.3
  0.9 0.0 copy-start
  0.9 1.0 spread.1
  1.9 14.2 %all-to-all-start = ((bf16[16,64,384]{2,1,0:T(8,128)(2,1)}), bf16[16,64,384]{2,1,0:T(8,128)(2,1)S(1)}, u32[]{:S(2)}, u32[]{:S(2)}) async-start(bf16[16,64,384]{2,1,0:T(8,128)(2,1)} %spread.1), calls=%async_computation | async-start | bytes 1572864 | tf_op jit(solution)/shard_map/all_to_all | solution.py:268
  16.1 0.0 copy-done
  16.1 2.5 %collective-permute-start = (bf16[384,1024]{1,0:T(8,128)(2,1)S(1)}, bf16[384,1024]{1,0:T(8,128)(2,1)S(1)}, u32[]{:S(2)}, u32[]{:S(2)}) collective-permute-start(bf16[384,1024]{1,0:T(8,128)(2,1)S(1)} %copy-done), channel_id=1, source_target_pairs={{0,16},{8,120},{16,0},{24,40},{32,48},{40,24},{48,32},{56,72},{64,... | collective-permute-start | bytes 2359304 | tf_op jit(solution)/shard_map/ppermute | solution.py:267
  18.5 14.0 %collective-permute-done.other_ref = bf16[384,1024]{1,0:T(8,128)(2,1)S(1)} collective-permute-done((bf16[384,1024]{1,0:T(8,128)(2,1)S(1)}, bf16[384,1024]{1,0:T(8,128)(2,1)S(1)}, u32[]{:S(2)}, u32[]{:S(2)}) %collective-permute-start) | collective-permute-done | bytes 786464 | tf_op jit(solution)/shard_map/ppermute | solution.py:267
  32.5 0.0 copy-start.1
  32.5 0.9 copy-done.1
  33.4 0.0 copy-start.2
  33.4 1.1 %copy-done.2 = bf16[384,1024]{1,0:T(8,128)(2,1)S(1)} copy-done((bf16[384,1024]{1,0:T(8,128)(2,1)S(1)}, bf16[384,1024]{1,0:T(8,128)(2,1)}, u32[]{:S(2)}) %copy-start.2) | copy-done | bytes 786456
  34.6 0.1 stack.13.cotangent_ref
  34.7 5.6 %all-to-all-done = bf16[16,64,384]{2,1,0:T(8,128)(2,1)S(1)} async-done(((bf16[16,64,384]{2,1,0:T(8,128)(2,1)}), bf16[16,64,384]{2,1,0:T(8,128)(2,1)S(1)}, u32[]{:S(2)}, u32[]{:S(2)}) %all-to-all-start) | async-done | bytes 786464 | tf_op jit(solution)/shard_map/all_to_all | solution.py:268
  40.3 0.6 contract.3
  40.9 1.9 %collective-permute-start.1 = (bf16[256,1024]{1,0:T(8,128)(2,1)S(1)}, bf16[256,1024]{1,0:T(8,128)(2,1)S(1)}, u32[]{:S(2)}, u32[]{:S(2)}) collective-permute-start(bf16[256,1024]{1,0:T(8,128)(2,1)S(1)} %contract.3), channel_id=1, source_target_pairs={{0,8},{8,0},{1,9},{9,1},{2,10},{10,2},{3,11},{11,3},{4,12},{12,4},... | collective-permute-start | bytes 1572872 | tf_op jit(solution)/shard_map/ppermute | solution.py:242
  42.9 0.6 contract.2.keep_ref
  43.4 1.3 %collective-permute-done.1.arrived_ref = bf16[256,1024]{1,0:T(8,128)(2,1)S(1)} collective-permute-done((bf16[256,1024]{1,0:T(8,128)(2,1)S(1)}, bf16[256,1024]{1,0:T(8,128)(2,1)S(1)}, u32[]{:S(2)}, u32[]{:S(2)}) %collective-permute-start.1) | collective-permute-done | bytes 524320 | tf_op jit(solution)/shard_map/ppermute | solution.py:242
  44.7 0.1 add.29
  44.8 27.8 %all_to_all.15.shares_ref = bf16[16,32,512]{2,1,0:T(8,128)(2,1)S(1)} all-to-all(bf16[16,32,512]{2,1,0:T(8,128)(2,1)S(1)} %add.29), channel_id=1, replica_groups=mesh['zr'=2,'zp'=2,'q'=4,'p'=2,'core'=2,'zh'=2,'x'=4] {'zr','q','zp'}, dimensions={0} | all-to-all | bytes 1048576 | tf_op jit(solution)/shard_map/all_to_all | solution.py:246
  72.6 0.1 total_copies.1
  72.7 14.3 %all_to_all.16 = bf16[8,32,512]{2,1,0:T(8,128)(2,1)S(1)} all-to-all(bf16[8,32,512]{2,1,0:T(8,128)(2,1)S(1)} %total_copies.1), channel_id=1, replica_groups=mesh['zr'=2,'zp'=2,'q'=4,'p'=2,'core'=2,'zh'=2,'x'=4] {'p','q'}, dimensions={0} | all-to-all | bytes 524288 | tf_op jit(solution)/shard_map/all_to_all | solution.py:246
  87.0 1.9 %collective-permute-start.2 = (bf16[256,512]{1,0:T(8,128)(2,1)S(1)}, bf16[256,512]{1,0:T(8,128)(2,1)S(1)}, u32[]{:S(2)}, u32[]{:S(2)}) collective-permute-start(bf16[256,512]{1,0:T(8,128)(2,1)S(1)} %bitcast.10), channel_id=1, source_target_pairs={{0,8},{8,0},{1,9},{9,1},{2,10},{10,2},{3,11},{11,3},{4,12},{12,4},... | collective-permute-start | bytes 786440 | tf_op jit(solution)/shard_map/ppermute | solution.py:242
  89.0 0.1 pad_add_fusion.place_ref
  89.0 1.4 %collective-permute-done.2.arrived_ref = bf16[256,512]{1,0:T(8,128)(2,1)S(1)} collective-permute-done((bf16[256,512]{1,0:T(8,128)(2,1)S(1)}, bf16[256,512]{1,0:T(8,128)(2,1)S(1)}, u32[]{:S(2)}, u32[]{:S(2)}) %collective-permute-start.2) | collective-permute-done | bytes 262176 | tf_op jit(solution)/shard_map/ppermute | solution.py:242
  90.4 6.5 %apply_roots.1 = (bf16[16,512]{1,0:T(8,128)(2,1)S(1)}, bf16[16,512]{1,0:T(8,128)(2,1)S(1)}) custom-call(s32[2]{0:T(128)S(1)} %pad_add_fusion.place_ref, bf16[256,512]{1,0:T(8,128)(2,1)S(1)} %bitcast.11, bf16[256,512]{1,0:T(8,128)(2,1)S(1)} %collective-permute-done.2.arrived_ref), custom_call_target="tpu_custom_call" | custom-call | tf_op jit(solution)/shard_map/apply_roots/pallas_call | solution.py:213
  96.9 2.2 %collective-permute-start.3 = (bf16[16,512]{1,0:T(8,128)(2,1)S(1)}, bf16[16,512]{1,0:T(8,128)(2,1)S(1)}, u32[]{:S(2)}, u32[]{:S(2)}) collective-permute-start(bf16[16,512]{1,0:T(8,128)(2,1)S(1)} %get-tuple-element.8), channel_id=1, source_target_pairs={{0,128},{128,0},{1,129},{129,1},{2,130},{130,2},{3,131},{131,3},{4... | collective-permute-start | bytes 49160 | tf_op jit(solution)/shard_map/ppermute | solution.py:242
  99.1 3.4 %collective-permute-done.3.arrived_ref = bf16[16,512]{1,0:T(8,128)(2,1)S(1)} collective-permute-done((bf16[16,512]{1,0:T(8,128)(2,1)S(1)}, bf16[16,512]{1,0:T(8,128)(2,1)S(1)}, u32[]{:S(2)}, u32[]{:S(2)}) %collective-permute-start.3) | collective-permute-done | bytes 16416 | tf_op jit(solution)/shard_map/ppermute | solution.py:242
  102.6 0.6 join.1
Async XLA Ops:
  0.0 0.9 copy-start.3
  0.9 15.2 %copy-start = (bf16[384,1024]{1,0:T(8,128)(2,1)S(1)}, bf16[384,1024]{1,0:T(8,128)(2,1)}, u32[]{:S(2)}) copy-start(bf16[384,1024]{1,0:T(8,128)(2,1)} %own_ref.1) | copy-start | bytes 2359300
  1.9 38.4 %all-to-all-start = ((bf16[16,64,384]{2,1,0:T(8,128)(2,1)}), bf16[16,64,384]{2,1,0:T(8,128)(2,1)S(1)}, u32[]{:S(2)}, u32[]{:S(2)}) async-start(bf16[16,64,384]{2,1,0:T(8,128)(2,1)} %spread.1), calls=%async_computation | async-start | bytes 1572864 | tf_op jit(solution)/shard_map/all_to_all | solution.py:268
  16.1 16.4 %collective-permute-start = (bf16[384,1024]{1,0:T(8,128)(2,1)S(1)}, bf16[384,1024]{1,0:T(8,128)(2,1)S(1)}, u32[]{:S(2)}, u32[]{:S(2)}) collective-permute-start(bf16[384,1024]{1,0:T(8,128)(2,1)S(1)} %copy-done), channel_id=1, source_target_pairs={{0,16},{8,120},{16,0},{24,40},{32,48},{40,24},{48,32},{56,72},{64,... | collective-permute-start | bytes 2359304 | tf_op jit(solution)/shard_map/ppermute | solution.py:267
  32.5 0.9 copy-start.1
  33.4 1.1 %copy-start.2 = (bf16[384,1024]{1,0:T(8,128)(2,1)S(1)}, bf16[384,1024]{1,0:T(8,128)(2,1)}, u32[]{:S(2)}) copy-start(bf16[384,1024]{1,0:T(8,128)(2,1)} %copy-done.1) | copy-start | bytes 2359300
  40.9 3.8 %collective-permute-start.1 = (bf16[256,1024]{1,0:T(8,128)(2,1)S(1)}, bf16[256,1024]{1,0:T(8,128)(2,1)S(1)}, u32[]{:S(2)}, u32[]{:S(2)}) collective-permute-start(bf16[256,1024]{1,0:T(8,128)(2,1)S(1)} %contract.3), channel_id=1, source_target_pairs={{0,8},{8,0},{1,9},{9,1},{2,10},{10,2},{3,11},{11,3},{4,12},{12,4},... | collective-permute-start | bytes 1572872 | tf_op jit(solution)/shard_map/ppermute | solution.py:242
  87.0 3.4 %collective-permute-start.2 = (bf16[256,512]{1,0:T(8,128)(2,1)S(1)}, bf16[256,512]{1,0:T(8,128)(2,1)S(1)}, u32[]{:S(2)}, u32[]{:S(2)}) collective-permute-start(bf16[256,512]{1,0:T(8,128)(2,1)S(1)} %bitcast.10), channel_id=1, source_target_pairs={{0,8},{8,0},{1,9},{9,1},{2,10},{10,2},{3,11},{11,3},{4,12},{12,4},... | collective-permute-start | bytes 786440 | tf_op jit(solution)/shard_map/ppermute | solution.py:242
  96.9 5.6 %collective-permute-start.3 = (bf16[16,512]{1,0:T(8,128)(2,1)S(1)}, bf16[16,512]{1,0:T(8,128)(2,1)S(1)}, u32[]{:S(2)}, u32[]{:S(2)}) collective-permute-start(bf16[16,512]{1,0:T(8,128)(2,1)S(1)} %get-tuple-element.8), channel_id=1, source_target_pairs={{0,128},{128,0},{1,129},{129,1},{2,130},{130,2},{3,131},{131,3},{4... | collective-permute-start | bytes 49160 | tf_op jit(solution)/shard_map/ppermute | solution.py:242

commit v7 on v6

--- a/solution.py
+++ b/solution.py
@@ -13,28 +13,45 @@
 PARAMS = pltpu.CompilerParams(vmem_limit_bytes=24 * 1024 * 1024)
 VMEM = pl.BlockSpec(memory_space=pltpu.VMEM)
 SMEM = pl.BlockSpec(memory_space=pltpu.SMEM)
+EARLY = pl.CostEstimate(flops=7 * 10**9, bytes_accessed=3 << 20, transcendentals=0)
 
 
 def dot(left, right):
     return jnp.dot(left, right, preferred_element_type=jnp.float32)
 
 
-def spread_kernel(tokens_ref, copies_ref):
-    features = tokens_ref[...].T
-    for parity in range(2):
-        for place in range(8):
-            copies_ref[parity * 8 + place] = features[parity * 64 : parity * 64 + 64]
-
-
-def spread(tokens):
+def turn_kernel(tokens_ref, turned_ref):
+    turned_ref[...] = tokens_ref[...].T
+
+
+def turn(tokens):
+    return pl.pallas_call(
+        turn_kernel,
+        in_specs=[VMEM],
+        out_specs=VMEM,
+        out_shape=jax.ShapeDtypeStruct((128, 384), jnp.bfloat16),
+        compiler_params=PARAMS,
+        name="turn",
+    )(tokens)
+
+
+def spread_kernel(zh_ref, turned_ref, far_ref, copies_ref):
+    zh = zh_ref[0]
+    for features, at in ((turned_ref[...], zh), (far_ref[...].T, 1 - zh)):
+        for parity in range(2):
+            for place in range(4):
+                copies_ref[parity * 4 + place, at] = features[parity * 64 : parity * 64 + 64]
+
+
+def spread(zh, turned, far):
     return pl.pallas_call(
         spread_kernel,
-        in_specs=[VMEM],
-        out_specs=VMEM,
-        out_shape=jax.ShapeDtypeStruct((16, 64, 384), jnp.bfloat16),
+        in_specs=[SMEM] + [VMEM] * 2,
+        out_specs=VMEM,
+        out_shape=jax.ShapeDtypeStruct((8, 2, 64, 384), jnp.bfloat16),
         compiler_params=PARAMS,
         name="spread",
-    )(tokens)
+    )(zh[None], turned, far)
 
 
 def stack_kernel(parity_ref, own_ref, other_ref, out_ref, sems):
@@ -59,6 +76,7 @@
         out_shape=jax.ShapeDtypeStruct((768, 2 * BLK), jnp.bfloat16),
         scratch_shapes=[pltpu.SemaphoreType.DMA((2,))],
         compiler_params=PARAMS,
+        cost_estimate=EARLY,
         name="stack",
     )(parity[None], own, other)
 
@@ -66,7 +84,13 @@
 def contract_kernel(half_ref, features_ref, cotangent_ref, out_ref):
     rows = pl.ds(pl.multiple_of(half_ref[0] * ROWS, ROWS), ROWS)
     features = jnp.concatenate(
-        [features_ref[parity, :, rows, :].reshape(256, 384) for parity in range(2)], axis=1
+        [
+            jnp.concatenate(
+                [features_ref[parity, :, zh, rows, :].reshape(128, 384) for zh in range(2)], axis=0
+            )
+            for parity in range(2)
+        ],
+        axis=1,
     )
     out_ref[...] = dot(features, cotangent_ref[...]).astype(out_ref.dtype)
 
@@ -255,9 +279,10 @@
     for core in range(2):
         for even in range(0, 8, 2):
             pair = (even, partner(even, core))
-            groups.append(
-                [(y * 2 + core) * 8 + feature for y in pair for feature in range(8)]
-            )
+            for zh in range(2):
+                groups.append(
+                    [(y * 2 + core) * 8 + zh * 4 + x for y in pair for x in range(4)]
+                )
     return groups
 
 
@@ -266,13 +291,13 @@
     pairs = [(y * 2 + k, partner(y, k) * 2 + k) for y in range(8) for k in range(2)]
     other = lax.ppermute(cotangent, ("q", "p", "core"), pairs)
     features = lax.all_to_all(
-        spread(tokens),
+        spread(lax.axis_index("zh"), turn(tokens), swap(tokens, "zh")),
         ("q", "p", "core", "zh", "x"),
         0,
         0,
         axis_index_groups=pair_groups(),
         tiled=True,
-    ).reshape(2, 8, 64, 384)
+    ).reshape(2, 4, 2, 64, 384)
     both = stack(p, cotangent, other)
     arrived = swap(contract(1 - core, features, both, jnp.bfloat16), "core")
     keep = contract(core, features, both, jnp.float32)

time: 104 us -> 96.3 us (0.926)
  the two profiles are of different devices: /device:TPU:12 before, /device:TPU:1 now
where the time goes in v7:
time: 96.3 us; the launch traced here: 94.8 us
  blocking collectives  37.5 us (39%)
  starting transfers between devices  29.8 us (31%)
  waiting for transfers between devices  14.8 us (15%)
  Pallas kernels  9.62 us (10%)
  local copies, waits for them, and re-layouts  2.93 us (3%)
    all_to_all x2, blocking collectives, exchange(): return lax.all_to_all(value, axes, 0, 0, tiled=True)  37.5 us
    ppermute x4, starting transfers between devices, swap(): return lax.ppermute(value, axis, [(0, 1), (1, 0)])  20.6 us
    all_to_all x1, waiting for transfers between devices, body(): lax.all_to_all(spread(lax.axis_index('zh'), turn(tokens), swap(tokens, 'z...  6.72 us
    pallas_call x1, Pallas kernels, apply_roots(): pl.pallas_call(roots_kernel, in_specs=[SMEM] + [VMEM] * 2, out_specs=[VME...  6.49 us
    ppermute x1, starting transfers between devices, body(): other = lax.ppermute(cotangent, ('q', 'p', 'core'), pairs)  5.1 us
    ppermute x4, waiting for transfers between devices, swap(): return lax.ppermute(value, axis, [(0, 1), (1, 0)])  4.51 us
    all_to_all x1, starting transfers between devices, body(): lax.all_to_all(spread(lax.axis_index('zh'), turn(tokens), swap(tokens, 'z...  4.02 us
    ppermute x1, waiting for transfers between devices, body(): other = lax.ppermute(cotangent, ('q', 'p', 'core'), pairs)  3.55 us
  transfers between devices with their start and end apart: 6, of which 5 were waited for; matrix products, arithmetic and copies ran while one was open for 0% of the time, Pallas kernels for 2%

profile of v7, /device:TPU:1, one launch (start us, length us, event | category | flops | bytes accessed | tf_op | source)
XLA Modules:
  0.0 94.8 jit_solution(15696298943103068560)
XLA Ops:
  0.0 11.5 %collective-permute-start = (bf16[384,128]{1,0:T(8,128)(2,1)}, bf16[384,128]{1,0:T(8,128)(2,1)S(1)}, u32[]{:S(2)}, u32[]{:S(2)}) collective-permute-start(bf16[384,128]{1,0:T(8,128)(2,1)} %tokens_ref.1), channel_id=1, source_target_pairs={{0,4},{4,0},{1,5},{5,1},{2,6},{6,2},{3,7},{7,3},{8,12},{12,8},{9,1... | collective-permute-start | bytes 294920 | tf_op jit(solution)/shard_map/ppermute | solution.py:266
  11.5 5.1 %collective-permute-start.1 = (bf16[384,1024]{1,0:T(8,128)(2,1)}, bf16[384,1024]{1,0:T(8,128)(2,1)S(1)}, u32[]{:S(2)}, u32[]{:S(2)}) collective-permute-start(bf16[384,1024]{1,0:T(8,128)(2,1)} %own_ref.1), channel_id=1, source_target_pairs={{0,16},{8,120},{16,0},{24,40},{32,48},{40,24},{48,32},{56,72},{64,... | collective-permute-start | bytes 2359304 | tf_op jit(solution)/shard_map/ppermute | solution.py:292
  16.6 0.0 copy-start
  16.6 0.9 copy-done
  17.5 0.0 copy-start.1
  17.5 0.1 turn.1.turned_ref
  17.6 0.0 collective-permute-done.far_ref
  17.6 1.0 %spread.1 = bf16[8,2,64,384]{3,2,1,0:T(8,128)(2,1)} custom-call(s32[1]{0:T(128)} %bitcast.4.zh_ref, bf16[128,384]{1,0:T(8,128)(2,1)S(1)} %turn.1.turned_ref, bf16[384,128]{1,0:T(8,128)(2,1)S(1)} %collective-permute-done.far_ref), custom_call_target="tpu_custom_call" | custom-call | tf_op jit(solution)/shard_map/spread/pallas_call | solution.py:47
  18.6 4.0 %all-to-all-start = ((bf16[8,2,64,384]{3,2,1,0:T(8,128)(2,1)}), bf16[8,2,64,384]{3,2,1,0:T(8,128)(2,1)S(1)}, u32[]{:S(2)}, u32[]{:S(2)}) async-start(bf16[8,2,64,384]{3,2,1,0:T(8,128)(2,1)} %spread.1), calls=%async_computation | async-start | bytes 1572864 | tf_op jit(solution)/shard_map/all_to_all | solution.py:293
  22.6 3.6 %collective-permute-done.1.other_ref = bf16[384,1024]{1,0:T(8,128)(2,1)S(1)} collective-permute-done((bf16[384,1024]{1,0:T(8,128)(2,1)}, bf16[384,1024]{1,0:T(8,128)(2,1)S(1)}, u32[]{:S(2)}, u32[]{:S(2)}) %collective-permute-start.1) | collective-permute-done | bytes 786464 | tf_op jit(solution)/shard_map/ppermute | solution.py:292
  26.1 0.0 copy-start.2
  26.1 0.9 copy-done.2
  27.1 0.0 copy-done.1
  27.1 0.0 copy-start.3
  27.1 1.1 %copy-done.3 = bf16[384,1024]{1,0:T(8,128)(2,1)S(1)} copy-done((bf16[384,1024]{1,0:T(8,128)(2,1)S(1)}, bf16[384,1024]{1,0:T(8,128)(2,1)}, u32[]{:S(2)}) %copy-start.3) | copy-done | bytes 786456
  28.2 0.1 stack.13.cotangent_ref
  28.3 6.7 %all-to-all-done = bf16[8,2,64,384]{3,2,1,0:T(8,128)(2,1)S(1)} async-done(((bf16[8,2,64,384]{3,2,1,0:T(8,128)(2,1)}), bf16[8,2,64,384]{3,2,1,0:T(8,128)(2,1)S(1)}, u32[]{:S(2)}, u32[]{:S(2)}) %all-to-all-start) | async-done | bytes 786464 | tf_op jit(solution)/shard_map/all_to_all | solution.py:293
  35.0 0.6 contract.3
  35.6 2.4 %collective-permute-start.2 = (bf16[256,1024]{1,0:T(8,128)(2,1)S(1)}, bf16[256,1024]{1,0:T(8,128)(2,1)S(1)}, u32[]{:S(2)}, u32[]{:S(2)}) collective-permute-start(bf16[256,1024]{1,0:T(8,128)(2,1)S(1)} %contract.3), channel_id=1, source_target_pairs={{0,8},{8,0},{1,9},{9,1},{2,10},{10,2},{3,11},{11,3},{4,12},{12,4},... | collective-permute-start | bytes 1572872 | tf_op jit(solution)/shard_map/ppermute | solution.py:266
  38.1 0.6 contract.2.keep_ref
  38.6 0.9 collective-permute-done.2.arrived_ref
  39.6 0.1 add.29
  39.7 24.6 %all_to_all.15.shares_ref = bf16[16,32,512]{2,1,0:T(8,128)(2,1)S(1)} all-to-all(bf16[16,32,512]{2,1,0:T(8,128)(2,1)S(1)} %add.29), channel_id=1, replica_groups=mesh['zr'=2,'zp'=2,'q'=4,'p'=2,'core'=2,'zh'=2,'x'=4] {'zr','q','zp'}, dimensions={0} | all-to-all | bytes 1048576 | tf_op jit(solution)/shard_map/all_to_all | solution.py:270
  64.3 0.1 total_copies.1
  64.4 12.9 %all_to_all.16 = bf16[8,32,512]{2,1,0:T(8,128)(2,1)S(1)} all-to-all(bf16[8,32,512]{2,1,0:T(8,128)(2,1)S(1)} %total_copies.1), channel_id=1, replica_groups=mesh['zr'=2,'zp'=2,'q'=4,'p'=2,'core'=2,'zh'=2,'x'=4] {'p','q'}, dimensions={0} | all-to-all | bytes 524288 | tf_op jit(solution)/shard_map/all_to_all | solution.py:270
  77.2 4.9 %collective-permute-start.3 = (bf16[256,512]{1,0:T(8,128)(2,1)S(1)}, bf16[256,512]{1,0:T(8,128)(2,1)S(1)}, u32[]{:S(2)}, u32[]{:S(2)}) collective-permute-start(bf16[256,512]{1,0:T(8,128)(2,1)S(1)} %bitcast.11), channel_id=1, source_target_pairs={{0,8},{8,0},{1,9},{9,1},{2,10},{10,2},{3,11},{11,3},{4,12},{12,4},... | collective-permute-start | bytes 786440 | tf_op jit(solution)/shard_map/ppermute | solution.py:266
  82.1 0.1 pad_add_fusion.place_ref
  82.2 1.0 %collective-permute-done.3.arrived_ref = bf16[256,512]{1,0:T(8,128)(2,1)S(1)} collective-permute-done((bf16[256,512]{1,0:T(8,128)(2,1)S(1)}, bf16[256,512]{1,0:T(8,128)(2,1)S(1)}, u32[]{:S(2)}, u32[]{:S(2)}) %collective-permute-start.3) | collective-permute-done | bytes 262176 | tf_op jit(solution)/shard_map/ppermute | solution.py:266
  83.2 6.5 %apply_roots.1 = (bf16[16,512]{1,0:T(8,128)(2,1)S(1)}, bf16[16,512]{1,0:T(8,128)(2,1)S(1)}) custom-call(s32[2]{0:T(128)S(1)} %pad_add_fusion.place_ref, bf16[256,512]{1,0:T(8,128)(2,1)S(1)} %bitcast.12, bf16[256,512]{1,0:T(8,128)(2,1)S(1)} %collective-permute-done.3.arrived_ref), custom_call_target="tpu_custom_call" | custom-call | tf_op jit(solution)/shard_map/apply_roots/pallas_call | solution.py:237
  89.7 1.9 %collective-permute-start.4 = (bf16[16,512]{1,0:T(8,128)(2,1)S(1)}, bf16[16,512]{1,0:T(8,128)(2,1)S(1)}, u32[]{:S(2)}, u32[]{:S(2)}) collective-permute-start(bf16[16,512]{1,0:T(8,128)(2,1)S(1)} %get-tuple-element.8), channel_id=1, source_target_pairs={{0,128},{128,0},{1,129},{129,1},{2,130},{130,2},{3,131},{131,3},{4... | collective-permute-start | bytes 49160 | tf_op jit(solution)/shard_map/ppermute | solution.py:266
  91.6 2.6 %collective-permute-done.4.arrived_ref = bf16[16,512]{1,0:T(8,128)(2,1)S(1)} collective-permute-done((bf16[16,512]{1,0:T(8,128)(2,1)S(1)}, bf16[16,512]{1,0:T(8,128)(2,1)S(1)}, u32[]{:S(2)}, u32[]{:S(2)}) %collective-permute-start.4) | collective-permute-done | bytes 16416 | tf_op jit(solution)/shard_map/ppermute | solution.py:266
  94.2 0.6 join.1
Async XLA Ops:
  0.0 17.6 %collective-permute-start = (bf16[384,128]{1,0:T(8,128)(2,1)}, bf16[384,128]{1,0:T(8,128)(2,1)S(1)}, u32[]{:S(2)}, u32[]{:S(2)}) collective-permute-start(bf16[384,128]{1,0:T(8,128)(2,1)} %tokens_ref.1), channel_id=1, source_target_pairs={{0,4},{4,0},{1,5},{5,1},{2,6},{6,2},{3,7},{7,3},{8,12},{12,8},{9,1... | collective-permute-start | bytes 294920 | tf_op jit(solution)/shard_map/ppermute | solution.py:266
  11.5 14.7 %collective-permute-start.1 = (bf16[384,1024]{1,0:T(8,128)(2,1)}, bf16[384,1024]{1,0:T(8,128)(2,1)S(1)}, u32[]{:S(2)}, u32[]{:S(2)}) collective-permute-start(bf16[384,1024]{1,0:T(8,128)(2,1)} %own_ref.1), channel_id=1, source_target_pairs={{0,16},{8,120},{16,0},{24,40},{32,48},{40,24},{48,32},{56,72},{64,... | collective-permute-start | bytes 2359304 | tf_op jit(solution)/shard_map/ppermute | solution.py:292
  16.6 0.9 copy-start
  17.5 9.6 %copy-start.1 = (bf16[384,1024]{1,0:T(8,128)(2,1)S(1)}, bf16[384,1024]{1,0:T(8,128)(2,1)}, u32[]{:S(2)}) copy-start(bf16[384,1024]{1,0:T(8,128)(2,1)} %own_ref.1) | copy-start | bytes 2359300
  18.6 16.5 %all-to-all-start = ((bf16[8,2,64,384]{3,2,1,0:T(8,128)(2,1)}), bf16[8,2,64,384]{3,2,1,0:T(8,128)(2,1)S(1)}, u32[]{:S(2)}, u32[]{:S(2)}) async-start(bf16[8,2,64,384]{3,2,1,0:T(8,128)(2,1)} %spread.1), calls=%async_computation | async-start | bytes 1572864 | tf_op jit(solution)/shard_map/all_to_all | solution.py:293
  26.1 0.9 copy-start.2
  27.1 1.1 %copy-start.3 = (bf16[384,1024]{1,0:T(8,128)(2,1)S(1)}, bf16[384,1024]{1,0:T(8,128)(2,1)}, u32[]{:S(2)}) copy-start(bf16[384,1024]{1,0:T(8,128)(2,1)} %copy-done.2) | copy-start | bytes 2359300
  35.6 3.9 %collective-permute-start.2 = (bf16[256,1024]{1,0:T(8,128)(2,1)S(1)}, bf16[256,1024]{1,0:T(8,128)(2,1)S(1)}, u32[]{:S(2)}, u32[]{:S(2)}) collective-permute-start(bf16[256,1024]{1,0:T(8,128)(2,1)S(1)} %contract.3), channel_id=1, source_target_pairs={{0,8},{8,0},{1,9},{9,1},{2,10},{10,2},{3,11},{11,3},{4,12},{12,4},... | collective-permute-start | bytes 1572872 | tf_op jit(solution)/shard_map/ppermute | solution.py:266
  77.2 6.0 %collective-permute-start.3 = (bf16[256,512]{1,0:T(8,128)(2,1)S(1)}, bf16[256,512]{1,0:T(8,128)(2,1)S(1)}, u32[]{:S(2)}, u32[]{:S(2)}) collective-permute-start(bf16[256,512]{1,0:T(8,128)(2,1)S(1)} %bitcast.11), channel_id=1, source_target_pairs={{0,8},{8,0},{1,9},{9,1},{2,10},{10,2},{3,11},{11,3},{4,12},{12,4},... | collective-permute-start | bytes 786440 | tf_op jit(solution)/shard_map/ppermute | solution.py:266
  89.7 4.5 %collective-permute-start.4 = (bf16[16,512]{1,0:T(8,128)(2,1)S(1)}, bf16[16,512]{1,0:T(8,128)(2,1)S(1)}, u32[]{:S(2)}, u32[]{:S(2)}) collective-permute-start(bf16[16,512]{1,0:T(8,128)(2,1)S(1)} %get-tuple-element.8), channel_id=1, source_target_pairs={{0,128},{128,0},{1,129},{129,1},{2,130},{130,2},{3,131},{131,3},{4... | collective-permute-start | bytes 49160 | tf_op jit(solution)/shard_map/ppermute | solution.py:266

commit v8 on v7

--- a/solution.py
+++ b/solution.py
@@ -165,11 +165,9 @@
 
 
 def roots_kernel(
-    place_ref, own_ref, arrived_ref, keep_ref, send_ref, block_ref, flipped_ref, *scratch
+    place_ref, block_ref, out_ref, flipped_ref, *scratch
 ):
     lgram, rgram, lstep, rstep, lsquare, rsquare, lfourth, rfourth, lmat, rmat, rroot = scratch
-    block_ref[:HALF, :] = own_ref[...]
-    block_ref[HALF:, :] = arrived_ref[...]
     flipped_ref[...] = block_ref[...].T
     wide = block_ref[...].astype(jnp.float32)
     trace = jnp.sum(wide * wide, keepdims=True)
@@ -227,39 +225,38 @@
     half = dot(rows, block_ref[...]).astype(jnp.bfloat16)
     rroot[...] = dot(rroot[...], rstep[...]).astype(jnp.bfloat16)
     value = dot(half, rroot[...]).astype(jnp.bfloat16)
-    keep_ref[...] = value[:16]
-    send_ref[...] = value[16:]
-
-
-def apply_roots(places, own, arrived):
-    piece = jax.ShapeDtypeStruct((16, BLK), jnp.bfloat16)
+    out_ref[...] = value
+
+
+def apply_roots(places, block):
+    piece = jax.ShapeDtypeStruct((ROWS, BLK), jnp.bfloat16)
     narrow = pltpu.VMEM((BLK, BLK), jnp.bfloat16)
     return pl.pallas_call(
         roots_kernel,
-        in_specs=[SMEM] + [VMEM] * 2,
-        out_specs=[VMEM] * 2,
-        out_shape=[piece] * 2,
-        scratch_shapes=[narrow] * 2 + [pltpu.VMEM((BLK, BLK), jnp.float32)] * 2 + [narrow] * 9,
+        in_specs=[SMEM, VMEM],
+        out_specs=VMEM,
+        out_shape=piece,
+        scratch_shapes=[narrow] + [pltpu.VMEM((BLK, BLK), jnp.float32)] * 2 + [narrow] * 9,
         compiler_params=PARAMS,
         name="apply_roots",
-    )(places, own, arrived)
-
-
-def join_kernel(column_ref, keep_ref, arrived_ref, out_ref):
-    column = column_ref[0]
-    out_ref[:, pl.ds(pl.multiple_of(column * BLK, BLK), BLK)] = keep_ref[...]
-    out_ref[:, pl.ds(pl.multiple_of((1 - column) * BLK, BLK), BLK)] = arrived_ref[...]
-
-
-def join(column, keep, arrived):
+    )(places, block)
+
+
+def join_kernel(zp_ref, pieces_ref, out_ref):
+    rows = pl.ds(pl.multiple_of(zp_ref[0] * 16, 16), 16)
+    for column in range(2):
+        out_ref[:, column * BLK : column * BLK + BLK] = pieces_ref[column, rows, :]
+
+
+def join(zp, pieces):
     return pl.pallas_call(
         join_kernel,
-        in_specs=[SMEM] + [VMEM] * 2,
+        in_specs=[SMEM, VMEM],
         out_specs=VMEM,
         out_shape=jax.ShapeDtypeStruct((16, 2 * BLK), jnp.bfloat16),
         compiler_params=PARAMS,
         name="join",
-    )(column[None], keep, arrived)
+    )(zp[None], pieces)
 
 
 def swap(value, axis):
@@ -299,14 +296,15 @@
         tiled=True,
     ).reshape(2, 4, 2, 64, 384)
     both = stack(p, cotangent, other)
+    place = p * 256 + ((q & 1) * 4 + (q >> 1)) * ROWS + core * 16
+    places = jnp.stack([place, place + 64])
     arrived = swap(contract(1 - core, features, both, jnp.bfloat16), "core")
     keep = contract(core, features, both, jnp.float32)
+    arrived, places, zp = lax.optimization_barrier((arrived, places, zp))
     shares = exchange(add(keep, arrived), ("zr", "q", "zp"))
     own = exchange(total_copies(shares), ("p", "q")).reshape(256, BLK)
-    place = jnp.where(p == core, 0, 256) + ((q % 2) * 4 + q // 2) * ROWS + core * 16
-    places = jnp.stack([place + zp * 64, place + (1 - zp) * 64])
-    keep, sent = apply_roots(places, own, swap(own, "core"))
-    return join(zp, keep, swap(sent, "zp"))
+    update = apply_roots(places, lax.all_gather(own, "core", axis=0, tiled=True))
+    return join(zp, lax.all_gather(update[None], "zp", axis=0, tiled=True))
 
 
 def solution(mesh):

time: 96.3 us -> 94 us (0.976)
  blocking collectives: 37.5 us -> 45.7 us
  starting transfers between devices: 29.8 us -> 23 us
  waiting for transfers between devices: 14.8 us -> 11.1 us
    all_gather x0 -> x2, blocking collectives: none -> 8.19 us  [the longest x1 4.75 us: body(): lax.all_gather(own, 'core', axis=0, tiled=True)]
    ppermute x4 -> x2, starting transfers between devices: 20.6 us -> 13.9 us  [swap(): return lax.ppermute(value, axis, [(0, 1), (1, 0)])]
    ppermute x4 -> x2, waiting for transfers between devices: 4.51 us -> 0.82 us  [swap(): return lax.ppermute(value, axis, [(0, 1), (1, 0)])]
  transfers between devices with their start and end apart: 6 -> 4, of which waited for: 5 -> 3; matrix products, arithmetic and copies ran while one was open for 0% -> 0% of each run, Pallas kernels for 2% -> 2%
where the time goes in v8:
time: 94 us; the launch traced here: 92.6 us
  blocking collectives  45.7 us (49%)
  starting transfers between devices  23 us (24%)
  waiting for transfers between devices  11.1 us (12%)
  Pallas kernels  9.66 us (10%)
  local copies, waits for them, and re-layouts  2.92 us (3%)
    all_to_all x2, blocking collectives, exchange(): return lax.all_to_all(value, axes, 0, 0, tiled=True)  37.5 us
    ppermute x2, starting transfers between devices, swap(): return lax.ppermute(value, axis, [(0, 1), (1, 0)])  13.9 us
    all_to_all x1, waiting for transfers between devices, body(): lax.all_to_all(spread(lax.axis_index('zh'), turn(tokens), swap(tokens, 'z...  6.73 us
    pallas_call x1, Pallas kernels, apply_roots(): pl.pallas_call(roots_kernel, in_specs=[SMEM, VMEM], out_specs=VMEM, out_s...  6.51 us
    ppermute x1, starting transfers between devices, body(): other = lax.ppermute(cotangent, ('q', 'p', 'core'), pairs)  5.1 us
    all_gather x1, blocking collectives, body(): lax.all_gather(own, 'core', axis=0, tiled=True)  4.75 us
    all_to_all x1, starting transfers between devices, body(): lax.all_to_all(spread(lax.axis_index('zh'), turn(tokens), swap(tokens, 'z...  4.02 us
    ppermute x1, waiting for transfers between devices, body(): other = lax.ppermute(cotangent, ('q', 'p', 'core'), pairs)  3.56 us
  transfers between devices with their start and end apart: 4, of which 3 were waited for; matrix products, arithmetic and copies ran while one was open for 0% of the time, Pallas kernels for 2%

profile of v8, /device:TPU:1, one launch (start us, length us, event | category | flops | bytes accessed | tf_op | source)
XLA Modules:
  0.0 92.6 jit_solution(7298016710208955467)
XLA Ops:
  0.0 11.5 %collective-permute-start = (bf16[384,128]{1,0:T(8,128)(2,1)}, bf16[384,128]{1,0:T(8,128)(2,1)S(1)}, u32[]{:S(2)}, u32[]{:S(2)}) collective-permute-start(bf16[384,128]{1,0:T(8,128)(2,1)} %tokens_ref.1), channel_id=1, source_target_pairs={{0,4},{4,0},{1,5},{5,1},{2,6},{6,2},{3,7},{7,3},{8,12},{12,8},{9,1... | collective-permute-start | bytes 294920 | tf_op jit(solution)/shard_map/ppermute | solution.py:263
  11.5 5.1 %collective-permute-start.1 = (bf16[384,1024]{1,0:T(8,128)(2,1)}, bf16[384,1024]{1,0:T(8,128)(2,1)S(1)}, u32[]{:S(2)}, u32[]{:S(2)}) collective-permute-start(bf16[384,1024]{1,0:T(8,128)(2,1)} %own_ref.1), channel_id=1, source_target_pairs={{0,16},{8,120},{16,0},{24,40},{32,48},{40,24},{48,32},{56,72},{64,... | collective-permute-start | bytes 2359304 | tf_op jit(solution)/shard_map/ppermute | solution.py:289
  16.6 0.0 copy-start
  16.6 0.9 copy-done
  17.5 0.0 copy-start.1
  17.5 0.1 turn.1.turned_ref
  17.6 0.0 collective-permute-done.far_ref
  17.6 1.0 %spread.1 = bf16[8,2,64,384]{3,2,1,0:T(8,128)(2,1)} custom-call(s32[1]{0:T(128)} %bitcast.1.zh_ref, bf16[128,384]{1,0:T(8,128)(2,1)S(1)} %turn.1.turned_ref, bf16[384,128]{1,0:T(8,128)(2,1)S(1)} %collective-permute-done.far_ref), custom_call_target="tpu_custom_call" | custom-call | tf_op jit(solution)/shard_map/spread/pallas_call | solution.py:47
  18.6 4.0 %all-to-all-start = ((bf16[8,2,64,384]{3,2,1,0:T(8,128)(2,1)}), bf16[8,2,64,384]{3,2,1,0:T(8,128)(2,1)S(1)}, u32[]{:S(2)}, u32[]{:S(2)}) async-start(bf16[8,2,64,384]{3,2,1,0:T(8,128)(2,1)} %spread.1), calls=%async_computation | async-start | bytes 1572864 | tf_op jit(solution)/shard_map/all_to_all | solution.py:290
  22.6 3.6 %collective-permute-done.1.other_ref = bf16[384,1024]{1,0:T(8,128)(2,1)S(1)} collective-permute-done((bf16[384,1024]{1,0:T(8,128)(2,1)}, bf16[384,1024]{1,0:T(8,128)(2,1)S(1)}, u32[]{:S(2)}, u32[]{:S(2)}) %collective-permute-start.1) | collective-permute-done | bytes 786464 | tf_op jit(solution)/shard_map/ppermute | solution.py:289
  26.1 0.0 copy-start.2
  26.1 0.9 copy-done.2
  27.0 0.0 copy-done.1
  27.0 0.0 copy-start.3
  27.0 1.1 %copy-done.3 = bf16[384,1024]{1,0:T(8,128)(2,1)S(1)} copy-done((bf16[384,1024]{1,0:T(8,128)(2,1)S(1)}, bf16[384,1024]{1,0:T(8,128)(2,1)}, u32[]{:S(2)}) %copy-start.3) | copy-done | bytes 786456
  28.2 0.1 stack.13.cotangent_ref
  28.3 6.7 %all-to-all-done = bf16[8,2,64,384]{3,2,1,0:T(8,128)(2,1)S(1)} async-done(((bf16[8,2,64,384]{3,2,1,0:T(8,128)(2,1)}), bf16[8,2,64,384]{3,2,1,0:T(8,128)(2,1)S(1)}, u32[]{:S(2)}, u32[]{:S(2)}) %all-to-all-start) | async-done | bytes 786464 | tf_op jit(solution)/shard_map/all_to_all | solution.py:290
  35.0 0.6 contract.2
  35.6 2.4 %collective-permute-start.2 = (bf16[256,1024]{1,0:T(8,128)(2,1)S(1)}, bf16[256,1024]{1,0:T(8,128)(2,1)S(1)}, u32[]{:S(2)}, u32[]{:S(2)}) collective-permute-start(bf16[256,1024]{1,0:T(8,128)(2,1)S(1)} %contract.2), channel_id=1, source_target_pairs={{0,8},{8,0},{1,9},{9,1},{2,10},{10,2},{3,11},{11,3},{4,12},{12,4},... | collective-permute-start | bytes 1572872 | tf_op jit(solution)/shard_map/ppermute | solution.py:263
  38.1 0.1 pad_add_fusion.place_ref
  38.1 0.6 contract.3.keep_ref
  38.7 0.8 collective-permute-done.2.arrived_ref
  39.5 0.1 add.19
  39.6 24.7 %all_to_all.15.shares_ref = bf16[16,32,512]{2,1,0:T(8,128)(2,1)S(1)} all-to-all(bf16[16,32,512]{2,1,0:T(8,128)(2,1)S(1)} %add.19), channel_id=1, replica_groups=mesh['zr'=2,'zp'=2,'q'=4,'p'=2,'core'=2,'zh'=2,'x'=4] {'zr','q','zp'}, dimensions={0} | all-to-all | bytes 1048576 | tf_op jit(solution)/shard_map/all_to_all | solution.py:267
  64.3 0.1 total_copies.1
  64.4 12.9 %all_to_all.16 = bf16[8,32,512]{2,1,0:T(8,128)(2,1)S(1)} all-to-all(bf16[8,32,512]{2,1,0:T(8,128)(2,1)S(1)} %total_copies.1), channel_id=1, replica_groups=mesh['zr'=2,'zp'=2,'q'=4,'p'=2,'core'=2,'zh'=2,'x'=4] {'p','q'}, dimensions={0} | all-to-all | bytes 524288 | tf_op jit(solution)/shard_map/all_to_all | solution.py:267
  77.2 4.8 %all_gather.6.block_ref = bf16[512,512]{1,0:T(8,128)(2,1)S(1)} all-gather(bf16[256,512]{1,0:T(8,128)(2,1)S(1)} %bitcast.13), channel_id=1, replica_groups=mesh['zr'=2,'zp'=2,'q'=4,'p'=2,'core'=2,'zh'=2,'x'=4] {'core'}, dimensions={0}, use_global_device_ids=true | all-gather | bytes 786432 | tf_op jit(solution)/shard_map/all_gather | solution.py:306
  82.0 6.5 %apply_roots.1 = bf16[32,512]{1,0:T(8,128)(2,1)S(1)} custom-call(s32[2]{0:T(128)S(1)} %pad_add_fusion.place_ref, bf16[512,512]{1,0:T(8,128)(2,1)S(1)} %all_gather.6.block_ref), custom_call_target="tpu_custom_call" | custom-call | tf_op jit(solution)/shard_map/apply_roots/pallas_call | solution.py:234
  88.5 3.4 %all-gather = bf16[64,512]{1,0:T(8,128)(2,1)S(1)} all-gather(bf16[32,512]{1,0:T(8,128)(2,1)S(1)} %apply_roots.1), channel_id=2, replica_groups=mesh['zr'=2,'zp'=2,'q'=4,'p'=2,'core'=2,'zh'=2,'x'=4] {'zp'}, dimensions={0}, use_global_device_ids=true | all-gather | bytes 98304 | tf_op jit(solution)/shard_map/all_gather | solution.py:307
  91.9 0.6 join.1
Async XLA Ops:
  0.0 17.6 %collective-permute-start = (bf16[384,128]{1,0:T(8,128)(2,1)}, bf16[384,128]{1,0:T(8,128)(2,1)S(1)}, u32[]{:S(2)}, u32[]{:S(2)}) collective-permute-start(bf16[384,128]{1,0:T(8,128)(2,1)} %tokens_ref.1), channel_id=1, source_target_pairs={{0,4},{4,0},{1,5},{5,1},{2,6},{6,2},{3,7},{7,3},{8,12},{12,8},{9,1... | collective-permute-start | bytes 294920 | tf_op jit(solution)/shard_map/ppermute | solution.py:263
  11.5 14.7 %collective-permute-start.1 = (bf16[384,1024]{1,0:T(8,128)(2,1)}, bf16[384,1024]{1,0:T(8,128)(2,1)S(1)}, u32[]{:S(2)}, u32[]{:S(2)}) collective-permute-start(bf16[384,1024]{1,0:T(8,128)(2,1)} %own_ref.1), channel_id=1, source_target_pairs={{0,16},{8,120},{16,0},{24,40},{32,48},{40,24},{48,32},{56,72},{64,... | collective-permute-start | bytes 2359304 | tf_op jit(solution)/shard_map/ppermute | solution.py:289
  16.6 0.9 copy-start
  17.5 9.6 %copy-start.1 = (bf16[384,1024]{1,0:T(8,128)(2,1)S(1)}, bf16[384,1024]{1,0:T(8,128)(2,1)}, u32[]{:S(2)}) copy-start(bf16[384,1024]{1,0:T(8,128)(2,1)} %own_ref.1) | copy-start | bytes 2359300
  18.6 16.5 %all-to-all-start = ((bf16[8,2,64,384]{3,2,1,0:T(8,128)(2,1)}), bf16[8,2,64,384]{3,2,1,0:T(8,128)(2,1)S(1)}, u32[]{:S(2)}, u32[]{:S(2)}) async-start(bf16[8,2,64,384]{3,2,1,0:T(8,128)(2,1)} %spread.1), calls=%async_computation | async-start | bytes 1572864 | tf_op jit(solution)/shard_map/all_to_all | solution.py:290
  26.1 0.9 copy-start.2
  27.0 1.1 %copy-start.3 = (bf16[384,1024]{1,0:T(8,128)(2,1)S(1)}, bf16[384,1024]{1,0:T(8,128)(2,1)}, u32[]{:S(2)}) copy-start(bf16[384,1024]{1,0:T(8,128)(2,1)} %copy-done.2) | copy-start | bytes 2359300
  35.6 3.9 %collective-permute-start.2 = (bf16[256,1024]{1,0:T(8,128)(2,1)S(1)}, bf16[256,1024]{1,0:T(8,128)(2,1)S(1)}, u32[]{:S(2)}, u32[]{:S(2)}) collective-permute-start(bf16[256,1024]{1,0:T(8,128)(2,1)S(1)} %contract.2), channel_id=1, source_target_pairs={{0,8},{8,0},{1,9},{9,1},{2,10},{10,2},{3,11},{11,3},{4,12},{12,4},... | collective-permute-start | bytes 1572872 | tf_op jit(solution)/shard_map/ppermute | solution.py:263

commit v9 on v8

--- a/solution.py
+++ b/solution.py
@@ -10,6 +10,7 @@
 HALF = 256
 ITERS = 4
 ROWS = 32
+ORDER = (0, 2, 1, 3)
 PARAMS = pltpu.CompilerParams(vmem_limit_bytes=24 * 1024 * 1024)
 VMEM = pl.BlockSpec(memory_space=pltpu.VMEM)
 SMEM = pl.BlockSpec(memory_space=pltpu.SMEM)
@@ -110,8 +111,9 @@
     for place in range(8):
         rows = slice(place * ROWS, place * ROWS + ROWS)
         total = (keep_ref[rows] + arrived_ref[rows].astype(jnp.float32)).astype(jnp.bfloat16)
-        shares_ref[place * 2] = total[:, :BLK]
-        shares_ref[place * 2 + 1] = total[:, BLK:]
+        share = (place // 4 * 4 + ORDER.index(place % 4)) * 2
+        shares_ref[share] = total[:, :BLK]
+        shares_ref[share + 1] = total[:, BLK:]
 
 
 def add(keep, arrived):
@@ -263,8 +265,8 @@
     return lax.ppermute(value, axis, [(0, 1), (1, 0)])
 
 
-def exchange(value, axes):
-    return lax.all_to_all(value, axes, 0, 0, tiled=True)
+def exchange(value, axes, groups):
+    return lax.all_to_all(value, axes, 0, 0, axis_index_groups=groups, tiled=True)
 
 
 def partner(y, core):
@@ -287,22 +289,21 @@
     core, p, q, zp = (lax.axis_index(name) for name in ("core", "p", "q", "zp"))
     pairs = [(y * 2 + k, partner(y, k) * 2 + k) for y in range(8) for k in range(2)]
     other = lax.ppermute(cotangent, ("q", "p", "core"), pairs)
-    features = lax.all_to_all(
+    features = exchange(
         spread(lax.axis_index("zh"), turn(tokens), swap(tokens, "zh")),
         ("q", "p", "core", "zh", "x"),
-        0,
-        0,
-        axis_index_groups=pair_groups(),
-        tiled=True,
+        pair_groups(),
     ).reshape(2, 4, 2, 64, 384)
     both = stack(p, cotangent, other)
-    place = p * 256 + ((q & 1) * 4 + (q >> 1)) * ROWS + core * 16
-    places = jnp.stack([place, place + 64])
+    place = p * 256 + ((q & 1) * 4 + (q >> 1) * 2) * ROWS + core * 16
+    places = jnp.stack([place, place + ROWS])
     arrived = swap(contract(1 - core, features, both, jnp.bfloat16), "core")
     keep = contract(core, features, both, jnp.float32)
     arrived, places, zp = lax.optimization_barrier((arrived, places, zp))
-    shares = exchange(add(keep, arrived), ("zr", "q", "zp"))
-    own = exchange(total_copies(shares), ("p", "q")).reshape(256, BLK)
+    chips = [zr * 8 + zp * 4 + q for zr in range(2) for q in ORDER for zp in range(2)]
+    shares = exchange(add(keep, arrived), ("zr", "zp", "q"), [chips])
+    ring = [q * 2 + p for p in range(2) for q in ORDER]
+    own = exchange(total_copies(shares), ("q", "p"), [ring]).reshape(256, BLK)
     update = apply_roots(places, lax.all_gather(own, "core", axis=0, tiled=True))
     return join(zp, lax.all_gather(update[None], "zp", axis=0, tiled=True))
 

time: 94 us -> 92.2 us (0.981)
  blocking collectives: 45.7 us -> 44.5 us
    all_to_all x2, blocking collectives: 37.5 us -> 36 us  [exchange(): lax.all_to_all(value, axes, 0, 0, axis_index_groups=groups, tiled=True)]
where the time goes in v9:
time: 92.2 us; the launch traced here: 91.4 us
  blocking collectives  44.5 us (48%)
  starting transfers between devices  23 us (25%)
  waiting for transfers between devices  11.1 us (12%)
  Pallas kernels  9.65 us (10%)
  local copies, waits for them, and re-layouts  2.92 us (3%)
    all_to_all x2, blocking collectives, exchange(): lax.all_to_all(value, axes, 0, 0, axis_index_groups=groups, tiled=True)  36 us
    ppermute x2, starting transfers between devices, swap(): return lax.ppermute(value, axis, [(0, 1), (1, 0)])  13.9 us
    all_to_all x1, waiting for transfers between devices, exchange(): lax.all_to_all(value, axes, 0, 0, axis_index_groups=groups, tiled=True)  6.73 us
    pallas_call x1, Pallas kernels, apply_roots(): pl.pallas_call(roots_kernel, in_specs=[SMEM, VMEM], out_specs=VMEM, out_s...  6.51 us
    ppermute x1, starting transfers between devices, body(): other = lax.ppermute(cotangent, ('q', 'p', 'core'), pairs)  5.1 us
    all_gather x1, blocking collectives, body(): lax.all_gather(own, 'core', axis=0, tiled=True)  5.08 us
    all_to_all x1, starting transfers between devices, exchange(): lax.all_to_all(value, axes, 0, 0, axis_index_groups=groups, tiled=True)  4.02 us
    ppermute x1, waiting for transfers between devices, body(): other = lax.ppermute(cotangent, ('q', 'p', 'core'), pairs)  3.56 us
  transfers between devices with their start and end apart: 4, of which 3 were waited for; matrix products, arithmetic and copies ran while one was open for 0% of the time, Pallas kernels for 2%

profile of v9, /device:TPU:1, one launch (start us, length us, event | category | flops | bytes accessed | tf_op | source)
XLA Modules:
  0.0 91.4 jit_solution(7630809457455333122)
XLA Ops:
  0.0 11.5 %collective-permute-start = (bf16[384,128]{1,0:T(8,128)(2,1)}, bf16[384,128]{1,0:T(8,128)(2,1)S(1)}, u32[]{:S(2)}, u32[]{:S(2)}) collective-permute-start(bf16[384,128]{1,0:T(8,128)(2,1)} %tokens_ref.1), channel_id=1, source_target_pairs={{0,4},{4,0},{1,5},{5,1},{2,6},{6,2},{3,7},{7,3},{8,12},{12,8},{9,1... | collective-permute-start | bytes 294920 | tf_op jit(solution)/shard_map/ppermute | solution.py:265
  11.5 5.1 %collective-permute-start.1 = (bf16[384,1024]{1,0:T(8,128)(2,1)}, bf16[384,1024]{1,0:T(8,128)(2,1)S(1)}, u32[]{:S(2)}, u32[]{:S(2)}) collective-permute-start(bf16[384,1024]{1,0:T(8,128)(2,1)} %own_ref.1), channel_id=1, source_target_pairs={{0,16},{8,120},{16,0},{24,40},{32,48},{40,24},{48,32},{56,72},{64,... | collective-permute-start | bytes 2359304 | tf_op jit(solution)/shard_map/ppermute | solution.py:291
  16.6 0.0 copy-start
  16.6 0.9 copy-done
  17.5 0.0 copy-start.1
  17.5 0.1 turn.1.turned_ref
  17.6 0.0 collective-permute-done.far_ref
  17.6 1.0 %spread.1 = bf16[8,2,64,384]{3,2,1,0:T(8,128)(2,1)} custom-call(s32[1]{0:T(128)} %bitcast.1.zh_ref, bf16[128,384]{1,0:T(8,128)(2,1)S(1)} %turn.1.turned_ref, bf16[384,128]{1,0:T(8,128)(2,1)S(1)} %collective-permute-done.far_ref), custom_call_target="tpu_custom_call" | custom-call | tf_op jit(solution)/shard_map/spread/pallas_call | solution.py:48
  18.6 4.0 %all-to-all-start = ((bf16[8,2,64,384]{3,2,1,0:T(8,128)(2,1)}), bf16[8,2,64,384]{3,2,1,0:T(8,128)(2,1)S(1)}, u32[]{:S(2)}, u32[]{:S(2)}) async-start(bf16[8,2,64,384]{3,2,1,0:T(8,128)(2,1)} %spread.1), calls=%async_computation | async-start | bytes 1572864 | tf_op jit(solution)/shard_map/all_to_all | solution.py:269
  22.6 3.6 %collective-permute-done.1.other_ref = bf16[384,1024]{1,0:T(8,128)(2,1)S(1)} collective-permute-done((bf16[384,1024]{1,0:T(8,128)(2,1)}, bf16[384,1024]{1,0:T(8,128)(2,1)S(1)}, u32[]{:S(2)}, u32[]{:S(2)}) %collective-permute-start.1) | collective-permute-done | bytes 786464 | tf_op jit(solution)/shard_map/ppermute | solution.py:291
  26.1 0.0 copy-start.2
  26.1 0.9 copy-done.2
  27.0 0.0 copy-done.1
  27.0 0.0 copy-start.3
  27.0 1.1 %copy-done.3 = bf16[384,1024]{1,0:T(8,128)(2,1)S(1)} copy-done((bf16[384,1024]{1,0:T(8,128)(2,1)S(1)}, bf16[384,1024]{1,0:T(8,128)(2,1)}, u32[]{:S(2)}) %copy-start.3) | copy-done | bytes 786456
  28.2 0.1 stack.13.cotangent_ref
  28.3 6.7 %all-to-all-done = bf16[8,2,64,384]{3,2,1,0:T(8,128)(2,1)S(1)} async-done(((bf16[8,2,64,384]{3,2,1,0:T(8,128)(2,1)}), bf16[8,2,64,384]{3,2,1,0:T(8,128)(2,1)S(1)}, u32[]{:S(2)}, u32[]{:S(2)}) %all-to-all-start) | async-done | bytes 786464 | tf_op jit(solution)/shard_map/all_to_all | solution.py:269
  35.0 0.6 contract.2
  35.6 2.4 %collective-permute-start.2 = (bf16[256,1024]{1,0:T(8,128)(2,1)S(1)}, bf16[256,1024]{1,0:T(8,128)(2,1)S(1)}, u32[]{:S(2)}, u32[]{:S(2)}) collective-permute-start(bf16[256,1024]{1,0:T(8,128)(2,1)S(1)} %contract.2), channel_id=1, source_target_pairs={{0,8},{8,0},{1,9},{9,1},{2,10},{10,2},{3,11},{11,3},{4,12},{12,4},... | collective-permute-start | bytes 1572872 | tf_op jit(solution)/shard_map/ppermute | solution.py:265
  38.1 0.1 pad_add_fusion.place_ref
  38.1 0.6 contract.3.keep_ref
  38.7 0.8 collective-permute-done.2.arrived_ref
  39.5 0.1 add.19
  39.6 24.9 %all_to_all.15.shares_ref = bf16[16,32,512]{2,1,0:T(8,128)(2,1)S(1)} all-to-all(bf16[16,32,512]{2,1,0:T(8,128)(2,1)S(1)} %add.19), channel_id=1, replica_groups={{0,128,64,192,32,160,96,224,256,384,320,448,288,416,352,480},{1,129,65,..., dimensions={0} | all-to-all | bytes 1048576 | tf_op jit(solution)/shard_map/all_to_all | solution.py:269
  64.6 0.1 total_copies.1
  64.6 11.1 %all_to_all.16 = bf16[8,32,512]{2,1,0:T(8,128)(2,1)S(1)} all-to-all(bf16[8,32,512]{2,1,0:T(8,128)(2,1)S(1)} %total_copies.1), channel_id=1, replica_groups={{0,64,32,96,16,80,48,112},{1,65,33,97,17,81,49,113},{2,66,34,98,18,82,5..., dimensions={0} | all-to-all | bytes 524288 | tf_op jit(solution)/shard_map/all_to_all | solution.py:269
  75.7 5.1 %all_gather.6.block_ref = bf16[512,512]{1,0:T(8,128)(2,1)S(1)} all-gather(bf16[256,512]{1,0:T(8,128)(2,1)S(1)} %bitcast.13), channel_id=1, replica_groups=mesh['zr'=2,'zp'=2,'q'=4,'p'=2,'core'=2,'zh'=2,'x'=4] {'core'}, dimensions={0}, use_global_device_ids=true | all-gather | bytes 786432 | tf_op jit(solution)/shard_map/all_gather | solution.py:307
  80.8 6.5 %apply_roots.1 = bf16[32,512]{1,0:T(8,128)(2,1)S(1)} custom-call(s32[2]{0:T(128)S(1)} %pad_add_fusion.place_ref, bf16[512,512]{1,0:T(8,128)(2,1)S(1)} %all_gather.6.block_ref), custom_call_target="tpu_custom_call" | custom-call | tf_op jit(solution)/shard_map/apply_roots/pallas_call | solution.py:236
  87.3 3.4 %all-gather = bf16[64,512]{1,0:T(8,128)(2,1)S(1)} all-gather(bf16[32,512]{1,0:T(8,128)(2,1)S(1)} %apply_roots.1), channel_id=2, replica_groups=mesh['zr'=2,'zp'=2,'q'=4,'p'=2,'core'=2,'zh'=2,'x'=4] {'zp'}, dimensions={0}, use_global_device_ids=true | all-gather | bytes 98304 | tf_op jit(solution)/shard_map/all_gather | solution.py:308
  90.8 0.6 join.1
Async XLA Ops:
  0.0 17.6 %collective-permute-start = (bf16[384,128]{1,0:T(8,128)(2,1)}, bf16[384,128]{1,0:T(8,128)(2,1)S(1)}, u32[]{:S(2)}, u32[]{:S(2)}) collective-permute-start(bf16[384,128]{1,0:T(8,128)(2,1)} %tokens_ref.1), channel_id=1, source_target_pairs={{0,4},{4,0},{1,5},{5,1},{2,6},{6,2},{3,7},{7,3},{8,12},{12,8},{9,1... | collective-permute-start | bytes 294920 | tf_op jit(solution)/shard_map/ppermute | solution.py:265
  11.5 14.7 %collective-permute-start.1 = (bf16[384,1024]{1,0:T(8,128)(2,1)}, bf16[384,1024]{1,0:T(8,128)(2,1)S(1)}, u32[]{:S(2)}, u32[]{:S(2)}) collective-permute-start(bf16[384,1024]{1,0:T(8,128)(2,1)} %own_ref.1), channel_id=1, source_target_pairs={{0,16},{8,120},{16,0},{24,40},{32,48},{40,24},{48,32},{56,72},{64,... | collective-permute-start | bytes 2359304 | tf_op jit(solution)/shard_map/ppermute | solution.py:291
  16.6 0.9 copy-start
  17.5 9.6 %copy-start.1 = (bf16[384,1024]{1,0:T(8,128)(2,1)S(1)}, bf16[384,1024]{1,0:T(8,128)(2,1)}, u32[]{:S(2)}) copy-start(bf16[384,1024]{1,0:T(8,128)(2,1)} %own_ref.1) | copy-start | bytes 2359300
  18.6 16.5 %all-to-all-start = ((bf16[8,2,64,384]{3,2,1,0:T(8,128)(2,1)}), bf16[8,2,64,384]{3,2,1,0:T(8,128)(2,1)S(1)}, u32[]{:S(2)}, u32[]{:S(2)}) async-start(bf16[8,2,64,384]{3,2,1,0:T(8,128)(2,1)} %spread.1), calls=%async_computation | async-start | bytes 1572864 | tf_op jit(solution)/shard_map/all_to_all | solution.py:269
  26.1 0.9 copy-start.2
  27.0 1.1 %copy-start.3 = (bf16[384,1024]{1,0:T(8,128)(2,1)S(1)}, bf16[384,1024]{1,0:T(8,128)(2,1)}, u32[]{:S(2)}) copy-start(bf16[384,1024]{1,0:T(8,128)(2,1)} %copy-done.2) | copy-start | bytes 2359300
  35.6 3.9 %collective-permute-start.2 = (bf16[256,1024]{1,0:T(8,128)(2,1)S(1)}, bf16[256,1024]{1,0:T(8,128)(2,1)S(1)}, u32[]{:S(2)}, u32[]{:S(2)}) collective-permute-start(bf16[256,1024]{1,0:T(8,128)(2,1)S(1)} %contract.2), channel_id=1, source_target_pairs={{0,8},{8,0},{1,9},{9,1},{2,10},{10,2},{3,11},{11,3},{4,12},{12,4},... | collective-permute-start | bytes 1572872 | tf_op jit(solution)/shard_map/ppermute | solution.py:265

commit v10 on v9

--- a/solution.py
+++ b/solution.py
@@ -11,6 +11,7 @@
 ITERS = 4
 ROWS = 32
 ORDER = (0, 2, 1, 3)
+XS = ((0, 1, 2, 3), (2, 3, 0, 1))
 PARAMS = pltpu.CompilerParams(vmem_limit_bytes=24 * 1024 * 1024)
 VMEM = pl.BlockSpec(memory_space=pltpu.VMEM)
 SMEM = pl.BlockSpec(memory_space=pltpu.SMEM)
@@ -87,7 +88,12 @@
     features = jnp.concatenate(
         [
             jnp.concatenate(
-                [features_ref[parity, :, zh, rows, :].reshape(128, 384) for zh in range(2)], axis=0
+                [
+                    features_ref[parity, XS[parity].index(x), zh, rows, :]
+                    for zh in range(2)
+                    for x in range(4)
+                ],
+                axis=0,
             )
             for parity in range(2)
         ],
@@ -280,7 +286,7 @@
             pair = (even, partner(even, core))
             for zh in range(2):
                 groups.append(
-                    [(y * 2 + core) * 8 + zh * 4 + x for y in pair for x in range(4)]
+                    [(y * 2 + core) * 8 + zh * 4 + x for y, xs in zip(pair, XS) for x in xs]
                 )
     return groups
 

time: 92.2 us -> 92.3 us (level)
  no operation moved by 1% of the time
where the time goes in v10:
time: 92.3 us; the launch traced here: 91.6 us
  blocking collectives  44.7 us (48%)
  starting transfers between devices  23 us (25%)
  waiting for transfers between devices  11.1 us (12%)
  Pallas kernels  9.65 us (10%)
  local copies, waits for them, and re-layouts  2.92 us (3%)
    all_to_all x2, blocking collectives, exchange(): lax.all_to_all(value, axes, 0, 0, axis_index_groups=groups, tiled=True)  36.1 us
    ppermute x2, starting transfers between devices, swap(): return lax.ppermute(value, axis, [(0, 1), (1, 0)])  13.9 us
    all_to_all x1, waiting for transfers between devices, exchange(): lax.all_to_all(value, axes, 0, 0, axis_index_groups=groups, tiled=True)  6.73 us
    pallas_call x1, Pallas kernels, apply_roots(): pl.pallas_call(roots_kernel, in_specs=[SMEM, VMEM], out_specs=VMEM, out_s...  6.51 us
    all_gather x1, blocking collectives, body(): lax.all_gather(own, 'core', axis=0, tiled=True)  5.19 us
    ppermute x1, starting transfers between devices, body(): other = lax.ppermute(cotangent, ('q', 'p', 'core'), pairs)  5.1 us
    all_to_all x1, starting transfers between devices, exchange(): lax.all_to_all(value, axes, 0, 0, axis_index_groups=groups, tiled=True)  4.02 us
    ppermute x1, waiting for transfers between devices, body(): other = lax.ppermute(cotangent, ('q', 'p', 'core'), pairs)  3.56 us
  transfers between devices with their start and end apart: 4, of which 3 were waited for; matrix products, arithmetic and copies ran while one was open for 0% of the time, Pallas kernels for 2%

profile of v10, /device:TPU:1, one launch (start us, length us, event | category | flops | bytes accessed | tf_op | source)
XLA Modules:
  0.0 91.6 jit_solution(17100878883536818678)
XLA Ops:
  0.0 11.5 %collective-permute-start = (bf16[384,128]{1,0:T(8,128)(2,1)}, bf16[384,128]{1,0:T(8,128)(2,1)S(1)}, u32[]{:S(2)}, u32[]{:S(2)}) collective-permute-start(bf16[384,128]{1,0:T(8,128)(2,1)} %tokens_ref.1), channel_id=1, source_target_pairs={{0,4},{4,0},{1,5},{5,1},{2,6},{6,2},{3,7},{7,3},{8,12},{12,8},{9,1... | collective-permute-start | bytes 294920 | tf_op jit(solution)/shard_map/ppermute | solution.py:271
  11.5 5.1 %collective-permute-start.1 = (bf16[384,1024]{1,0:T(8,128)(2,1)}, bf16[384,1024]{1,0:T(8,128)(2,1)S(1)}, u32[]{:S(2)}, u32[]{:S(2)}) collective-permute-start(bf16[384,1024]{1,0:T(8,128)(2,1)} %own_ref.1), channel_id=1, source_target_pairs={{0,16},{8,120},{16,0},{24,40},{32,48},{40,24},{48,32},{56,72},{64,... | collective-permute-start | bytes 2359304 | tf_op jit(solution)/shard_map/ppermute | solution.py:297
  16.6 0.0 copy-start
  16.6 0.9 copy-done
  17.5 0.0 copy-start.1
  17.5 0.1 turn.1.turned_ref
  17.6 0.0 collective-permute-done.far_ref
  17.6 1.0 %spread.1 = bf16[8,2,64,384]{3,2,1,0:T(8,128)(2,1)} custom-call(s32[1]{0:T(128)} %bitcast.1.zh_ref, bf16[128,384]{1,0:T(8,128)(2,1)S(1)} %turn.1.turned_ref, bf16[384,128]{1,0:T(8,128)(2,1)S(1)} %collective-permute-done.far_ref), custom_call_target="tpu_custom_call" | custom-call | tf_op jit(solution)/shard_map/spread/pallas_call | solution.py:49
  18.6 4.0 %all-to-all-start = ((bf16[8,2,64,384]{3,2,1,0:T(8,128)(2,1)}), bf16[8,2,64,384]{3,2,1,0:T(8,128)(2,1)S(1)}, u32[]{:S(2)}, u32[]{:S(2)}) async-start(bf16[8,2,64,384]{3,2,1,0:T(8,128)(2,1)} %spread.1), calls=%async_computation | async-start | bytes 1572864 | tf_op jit(solution)/shard_map/all_to_all | solution.py:275
  22.6 3.6 %collective-permute-done.1.other_ref = bf16[384,1024]{1,0:T(8,128)(2,1)S(1)} collective-permute-done((bf16[384,1024]{1,0:T(8,128)(2,1)}, bf16[384,1024]{1,0:T(8,128)(2,1)S(1)}, u32[]{:S(2)}, u32[]{:S(2)}) %collective-permute-start.1) | collective-permute-done | bytes 786464 | tf_op jit(solution)/shard_map/ppermute | solution.py:297
  26.1 0.0 copy-start.2
  26.1 0.9 copy-done.2
  27.0 0.0 copy-done.1
  27.0 0.0 copy-start.3
  27.0 1.1 %copy-done.3 = bf16[384,1024]{1,0:T(8,128)(2,1)S(1)} copy-done((bf16[384,1024]{1,0:T(8,128)(2,1)S(1)}, bf16[384,1024]{1,0:T(8,128)(2,1)}, u32[]{:S(2)}) %copy-start.3) | copy-done | bytes 786456
  28.2 0.1 stack.13.cotangent_ref
  28.3 6.7 %all-to-all-done = bf16[8,2,64,384]{3,2,1,0:T(8,128)(2,1)S(1)} async-done(((bf16[8,2,64,384]{3,2,1,0:T(8,128)(2,1)}), bf16[8,2,64,384]{3,2,1,0:T(8,128)(2,1)S(1)}, u32[]{:S(2)}, u32[]{:S(2)}) %all-to-all-start) | async-done | bytes 786464 | tf_op jit(solution)/shard_map/all_to_all | solution.py:275
  35.0 0.6 contract.2
  35.6 2.4 %collective-permute-start.2 = (bf16[256,1024]{1,0:T(8,128)(2,1)S(1)}, bf16[256,1024]{1,0:T(8,128)(2,1)S(1)}, u32[]{:S(2)}, u32[]{:S(2)}) collective-permute-start(bf16[256,1024]{1,0:T(8,128)(2,1)S(1)} %contract.2), channel_id=1, source_target_pairs={{0,8},{8,0},{1,9},{9,1},{2,10},{10,2},{3,11},{11,3},{4,12},{12,4},... | collective-permute-start | bytes 1572872 | tf_op jit(solution)/shard_map/ppermute | solution.py:271
  38.1 0.1 pad_add_fusion.place_ref
  38.1 0.6 contract.3.keep_ref
  38.7 0.8 collective-permute-done.2.arrived_ref
  39.5 0.1 add.19
  39.6 25.0 %all_to_all.15.shares_ref = bf16[16,32,512]{2,1,0:T(8,128)(2,1)S(1)} all-to-all(bf16[16,32,512]{2,1,0:T(8,128)(2,1)S(1)} %add.19), channel_id=1, replica_groups={{0,128,64,192,32,160,96,224,256,384,320,448,288,416,352,480},{1,129,65,..., dimensions={0} | all-to-all | bytes 1048576 | tf_op jit(solution)/shard_map/all_to_all | solution.py:275
  64.6 0.1 total_copies.1
  64.7 11.1 %all_to_all.16 = bf16[8,32,512]{2,1,0:T(8,128)(2,1)S(1)} all-to-all(bf16[8,32,512]{2,1,0:T(8,128)(2,1)S(1)} %total_copies.1), channel_id=1, replica_groups={{0,64,32,96,16,80,48,112},{1,65,33,97,17,81,49,113},{2,66,34,98,18,82,5..., dimensions={0} | all-to-all | bytes 524288 | tf_op jit(solution)/shard_map/all_to_all | solution.py:275
  75.8 5.2 %all_gather.6.block_ref = bf16[512,512]{1,0:T(8,128)(2,1)S(1)} all-gather(bf16[256,512]{1,0:T(8,128)(2,1)S(1)} %bitcast.13), channel_id=1, replica_groups=mesh['zr'=2,'zp'=2,'q'=4,'p'=2,'core'=2,'zh'=2,'x'=4] {'core'}, dimensions={0}, use_global_device_ids=true | all-gather | bytes 786432 | tf_op jit(solution)/shard_map/all_gather | solution.py:313
  81.0 6.5 %apply_roots.1 = bf16[32,512]{1,0:T(8,128)(2,1)S(1)} custom-call(s32[2]{0:T(128)S(1)} %pad_add_fusion.place_ref, bf16[512,512]{1,0:T(8,128)(2,1)S(1)} %all_gather.6.block_ref), custom_call_target="tpu_custom_call" | custom-call | tf_op jit(solution)/shard_map/apply_roots/pallas_call | solution.py:242
  87.5 3.4 %all-gather = bf16[64,512]{1,0:T(8,128)(2,1)S(1)} all-gather(bf16[32,512]{1,0:T(8,128)(2,1)S(1)} %apply_roots.1), channel_id=2, replica_groups=mesh['zr'=2,'zp'=2,'q'=4,'p'=2,'core'=2,'zh'=2,'x'=4] {'zp'}, dimensions={0}, use_global_device_ids=true | all-gather | bytes 98304 | tf_op jit(solution)/shard_map/all_gather | solution.py:314
  90.9 0.6 join.1
Async XLA Ops:
  0.0 17.6 %collective-permute-start = (bf16[384,128]{1,0:T(8,128)(2,1)}, bf16[384,128]{1,0:T(8,128)(2,1)S(1)}, u32[]{:S(2)}, u32[]{:S(2)}) collective-permute-start(bf16[384,128]{1,0:T(8,128)(2,1)} %tokens_ref.1), channel_id=1, source_target_pairs={{0,4},{4,0},{1,5},{5,1},{2,6},{6,2},{3,7},{7,3},{8,12},{12,8},{9,1... | collective-permute-start | bytes 294920 | tf_op jit(solution)/shard_map/ppermute | solution.py:271
  11.5 14.7 %collective-permute-start.1 = (bf16[384,1024]{1,0:T(8,128)(2,1)}, bf16[384,1024]{1,0:T(8,128)(2,1)S(1)}, u32[]{:S(2)}, u32[]{:S(2)}) collective-permute-start(bf16[384,1024]{1,0:T(8,128)(2,1)} %own_ref.1), channel_id=1, source_target_pairs={{0,16},{8,120},{16,0},{24,40},{32,48},{40,24},{48,32},{56,72},{64,... | collective-permute-start | bytes 2359304 | tf_op jit(solution)/shard_map/ppermute | solution.py:297
  16.6 0.9 copy-start
  17.5 9.6 %copy-start.1 = (bf16[384,1024]{1,0:T(8,128)(2,1)S(1)}, bf16[384,1024]{1,0:T(8,128)(2,1)}, u32[]{:S(2)}) copy-start(bf16[384,1024]{1,0:T(8,128)(2,1)} %own_ref.1) | copy-start | bytes 2359300
  18.6 16.5 %all-to-all-start = ((bf16[8,2,64,384]{3,2,1,0:T(8,128)(2,1)}), bf16[8,2,64,384]{3,2,1,0:T(8,128)(2,1)S(1)}, u32[]{:S(2)}, u32[]{:S(2)}) async-start(bf16[8,2,64,384]{3,2,1,0:T(8,128)(2,1)} %spread.1), calls=%async_computation | async-start | bytes 1572864 | tf_op jit(solution)/shard_map/all_to_all | solution.py:275
  26.1 0.9 copy-start.2
  27.0 1.1 %copy-start.3 = (bf16[384,1024]{1,0:T(8,128)(2,1)S(1)}, bf16[384,1024]{1,0:T(8,128)(2,1)}, u32[]{:S(2)}) copy-start(bf16[384,1024]{1,0:T(8,128)(2,1)} %copy-done.2) | copy-start | bytes 2359300
  35.6 3.9 %collective-permute-start.2 = (bf16[256,1024]{1,0:T(8,128)(2,1)S(1)}, bf16[256,1024]{1,0:T(8,128)(2,1)S(1)}, u32[]{:S(2)}, u32[]{:S(2)}) collective-permute-start(bf16[256,1024]{1,0:T(8,128)(2,1)S(1)} %contract.2), channel_id=1, source_target_pairs={{0,8},{8,0},{1,9},{9,1},{2,10},{10,2},{3,11},{11,3},{4,12},{12,4},... | collective-permute-start | bytes 1572872 | tf_op jit(solution)/shard_map/ppermute | solution.py:271
